TPU v7x, 32 devices: a whole 2x2x4 slice. The times are simulated.
32 devices in a mesh: dp: 16 (over z, y, x), mp: 2 (over core).
Axes of the slice: x: 2, y: 2, z: 4, core: 2. Of those that a mesh axis runs over, the one named last changes fastest.
Arguments:
- block_input: bfloat16 [2, 2048, 2560], P(None, ('dp', 'mp')), may hold values from -6 to 6
- lengths: int32 [2], replicated, may hold values from 512 to 2048, as said below
- norm_gains: float32 [2, 2560], replicated, may hold values from 0.5 to 1.5
- w_branch: bfloat16 [2, 2560, 2560], P(None, 'dp', 'mp'), may hold values from -0.125 to 0.125
- channel_params: float32 [7, 2560], P(None, 'mp'), may hold values from -3 to 3
- gate_blocks: bfloat16 [2, 10, 256, 256], P(None, 'mp', 'dp'), may hold values from -0.375 to 0.375
- decay_param: float32 [2560], P('mp'), may hold values from -11 to -4
- w_out: bfloat16 [2560, 2560], P('mp', 'dp'), may hold values from -0.3125 to 0.3125
- w_mlp: bfloat16 [2, 2560, 7680], P(None, 'dp', 'mp'), may hold values from -0.125 to 0.125
- w_down: bfloat16 [7680, 2560], P('mp', 'dp'), may hold values from -0.09375 to 0.09375
- out_grad: bfloat16 [2, 2048, 2560], P(None, ('dp', 'mp')), may hold values from -6 to 6
Outputs:
- block_output: bfloat16 [2, 2048, 2560], P(None, ('dp', 'mp'))
- input_grad: float32 [2, 2048, 2560], P(None, ('dp', 'mp'))
- grad_norm_gains: float32 [2, 2560], replicated
- grad_w_branch: float32 [2, 2560, 2560], P(None, 'dp', 'mp')
- grad_channel: float32 [7, 2560], P(None, 'mp')
- grad_gate_blocks: float32 [2, 10, 256, 256], P(None, 'mp', 'dp')
- grad_decay: float32 [2560], P('mp')
- grad_w_out: float32 [2560, 2560], P('mp', 'dp')
- grad_w_mlp: float32 [2, 2560, 7680], P(None, 'dp', 'mp')
- grad_w_down: float32 [7680, 2560], P('mp', 'dp')
Inputs may be any that keep to these rules, and one draw needn't show every extreme that they name: lengths[s] is the number of valid leading tokens of slot s; some slot is full in every draw.
All inputs are finite; a program needn't handle non-finite values.
Results may differ from a plain program's by a relative error of at most 0.011.
Values may be sent and summed in bfloat16 or wider, within the bound.
A program may use at most 448 MiB of HBM per device.

v0:
```python
import jax
import jax.numpy as jnp
from jax import lax
from jax.sharding import PartitionSpec as P

MB = 2


EPS = 1e-06


def passed_along(value, axis, steps):
    count = lax.axis_size(axis)
    leading, last = (max(0, -steps), min(count, count - steps))
    return lax.ppermute(value, axis, [(source, source + steps) for source in range(leading, last)])


def entering(part, axis, combine, identity, reverse):
    count = lax.axis_size(axis)
    place = lax.axis_index(axis)
    ahead = count - 1 - place if reverse else place
    gathered = jax.tree.map(lambda a: lax.all_gather(a, axis), part)
    state = jax.tree.map(lambda a, e: jnp.zeros_like(a) + jnp.asarray(e, a.dtype), part, identity)

    def one(step, state):
        source = count - 1 - step if reverse else step
        return combine(
            state, jax.tree.map(lambda a: lax.dynamic_index_in_dim(a, source, 0, False), gathered)
        )

    return lax.fori_loop(0, ahead, one, state)


def combine_pair(earlier, later):
    return (earlier[0] * later[0], later[0] * earlier[1] + later[1])


def rms_forward(values, gain_vec):
    inv_scale = lax.rsqrt(jnp.mean(values * values, axis=-1, keepdims=True) + EPS)
    normal = values * inv_scale
    return (normal, inv_scale, normal * gain_vec)


def rms_backward(grad_normed, normal, inv_scale, gain_vec):
    grad_gain = jnp.sum(grad_normed * normal, axis=0)
    grad_n = grad_normed * gain_vec
    grad_in = inv_scale * (grad_n - normal * jnp.mean(grad_n * normal, axis=-1, keepdims=True))
    return (grad_in, grad_gain)


def fetch_weights(w_branch, gate_blocks, w_out, w_mlp, w_down):
    return (
        lax.all_gather(w_branch, "dp", axis=1, tiled=True),
        lax.all_gather(gate_blocks, "dp", axis=2, tiled=True),
        lax.all_gather(w_out, "dp", axis=1, tiled=True),
        lax.all_gather(w_mlp, "dp", axis=1, tiled=True),
        lax.all_gather(w_down, "dp", axis=1, tiled=True),
    )


def add_tuple(total, part_vals):
    if total is None:
        return part_vals
    return tuple((left + right for left, right in zip(total, part_vals)))


def body(
    block_input,
    lengths,
    norm_gains,
    w_branch,
    channel_params,
    gate_blocks,
    decay_param,
    w_out,
    w_mlp,
    w_down,
    out_grad,
):
    axis_count = lax.axis_size("dp")
    mp_count = lax.axis_size("mp")
    dp_index = lax.axis_index("dp")
    mp_index = lax.axis_index("mp")
    rows_own = block_input.shape[1]
    block_rows = rows_own * mp_count
    own_start = mp_index * rows_own
    lru_half = channel_params.shape[1]
    heads_half = gate_blocks.shape[1]
    head_size = gate_blocks.shape[3]
    seq_start = dp_index == 0
    seq_end = dp_index == axis_count - 1
    position = dp_index * block_rows + jnp.arange(block_rows, dtype=jnp.int32)
    at_start = (position == 0)[:, None]
    decay_base = jax.nn.softplus(decay_param)
    conv_taps = channel_params[0:4]
    conv_bias = channel_params[4]
    gate_bias = channel_params[5:7]
    out_list = []
    grad_list = []
    mlp_total = None
    mixer_total = None
    gain_acc = []
    chan_acc = []
    for batch in range(MB):
        fetched = fetch_weights(w_branch, gate_blocks, w_out, w_mlp, w_down)
        branch_gather, rg_gather, out_gather, mlp_gather, down_gather = fetched
        length = lengths[batch]
        valid_all = (position < length)[:, None]
        valid_own = lax.dynamic_slice_in_dim(valid_all, own_start, rows_own, 0)
        grad_own = jnp.where(valid_own, out_grad[batch], jnp.zeros_like(out_grad[batch]))
        input_low, grad_rows = (
            lax.all_gather(block_input[batch], "mp", axis=0, tiled=True),
            lax.all_gather(grad_own, "mp", axis=0, tiled=True),
        )
        input_rows = input_low.astype(jnp.float32)
        input_own = block_input[batch].astype(jnp.float32)
        normal_a, scale_a, pre_a = rms_forward(input_rows, norm_gains[0])
        normed_a = pre_a.astype(jnp.bfloat16)
        branches = jnp.einsum(
            "cd,kdl->kcl", normed_a, branch_gather, preferred_element_type=jnp.float32
        )
        gelu_gate = jax.nn.gelu(branches[0])
        conv_input = branches[1].astype(jnp.bfloat16)
        rim_rows = passed_along(conv_input[block_rows - 3 :], "dp", 1)
        rim_rows = jnp.where(seq_start, jnp.zeros_like(rim_rows), rim_rows)
        extended = jnp.concatenate([rim_rows, conv_input], axis=0).astype(jnp.float32)
        conv_out = (
            conv_bias + conv_taps[0] * extended[3:] + conv_taps[1] * extended[2 : block_rows + 2]
        )
        conv_out = (
            conv_out
            + conv_taps[2] * extended[1 : block_rows + 1]
            + conv_taps[3] * extended[:block_rows]
        )
        conv_low = conv_out.astype(jnp.bfloat16)
        conv_vals = conv_low.astype(jnp.float32)
        conv_heads = conv_low.reshape(block_rows, heads_half, head_size)
        blocks = jnp.einsum(
            "chi,ghij->gchj", conv_heads, rg_gather, preferred_element_type=jnp.float32
        )
        gate_vals = jax.nn.sigmoid(blocks.reshape(2, block_rows, lru_half) + gate_bias[:, None, :])
        log_a = -8.0 * gate_vals[1] * decay_base
        decay_rate = jnp.exp(log_a)
        square = jnp.exp(2.0 * log_a)
        root_term = jnp.sqrt(-jnp.expm1(2.0 * log_a))
        multiplier = jnp.where(at_start, 1.0, root_term)
        drive_term = conv_vals * gate_vals[0] * multiplier
        products, local_state = lax.associative_scan(combine_pair, (decay_rate, drive_term), axis=0)
        send_rate = jnp.where(seq_start, 0.0, products[-1])
        carry_in = entering(
            (send_rate, local_state[-1]),
            "dp",
            combine_pair,
            (jnp.ones_like(send_rate), jnp.zeros_like(send_rate)),
            False,
        )[1]
        carry_in = jnp.where(seq_start, 0.0, carry_in)
        state_vals = local_state + products * carry_in
        mixed_vals = (state_vals * gelu_gate).astype(jnp.bfloat16)
        residual_own = input_own + lax.psum_scatter(
            jnp.dot(mixed_vals, out_gather, preferred_element_type=jnp.float32),
            "mp",
            scatter_dimension=0,
            tiled=True,
        )
        normal_b, scale_b, pre_b = rms_forward(residual_own, norm_gains[1])
        normed_b = lax.all_gather(pre_b.astype(jnp.bfloat16), "mp", axis=0, tiled=True)
        gate_up = jnp.einsum(
            "cd,kdf->kcf", normed_b, mlp_gather, preferred_element_type=jnp.float32
        )
        act_vals = jax.nn.gelu(gate_up[0])
        hidden = (act_vals * gate_up[1]).astype(jnp.bfloat16)
        mlp_own = lax.psum_scatter(
            jnp.dot(hidden, down_gather, preferred_element_type=jnp.float32).astype(jnp.bfloat16),
            "mp",
            scatter_dimension=0,
            tiled=True,
        ).astype(jnp.float32)
        out_list.append(jnp.where(valid_own, residual_own + mlp_own, 0.0).astype(jnp.bfloat16))
        grad_hidden = lax.dot_general(
            grad_rows, down_gather, (((1,), (1,)), ((), ())), preferred_element_type=jnp.float32
        )
        grad_down = lax.dot_general(
            hidden, grad_rows, (((0,), (0,)), ((), ())), preferred_element_type=jnp.float32
        )
        act_pull = jax.vjp(jax.nn.gelu, gate_up[0])[1]
        grad_gate = act_pull(grad_hidden * gate_up[1])[0]
        grad_gate_up = jnp.stack([grad_gate, grad_hidden * act_vals]).astype(jnp.bfloat16)
        grad_mlp = jnp.einsum(
            "cd,kcf->kdf", normed_b, grad_gate_up, preferred_element_type=jnp.float32
        )
        grad_normed_b = lax.psum_scatter(
            jnp.einsum("kcf,kdf->cd", grad_gate_up, mlp_gather, preferred_element_type=jnp.float32),
            "mp",
            scatter_dimension=0,
            tiled=True,
        )
        grad_residual, gain_grad_b = rms_backward(grad_normed_b, normal_b, scale_b, norm_gains[1])
        grad_residual = grad_residual + grad_own.astype(jnp.float32)
        mlp_part = (grad_mlp, grad_down)
        mlp_total = add_tuple(mlp_total, mlp_part)
        grad_mixed_out = lax.all_gather(
            grad_residual.astype(jnp.bfloat16), "mp", axis=0, tiled=True
        )
        grad_mixed = lax.dot_general(
            grad_mixed_out, out_gather, (((1,), (1,)), ((), ())), preferred_element_type=jnp.float32
        )
        grad_out_w = lax.dot_general(
            mixed_vals, grad_mixed_out, (((0,), (0,)), ((), ())), preferred_element_type=jnp.float32
        )
        grad_state = grad_mixed * gelu_gate
        gelu_pull = jax.vjp(jax.nn.gelu, branches[0])[1]
        grad_gate_branch = gelu_pull(grad_mixed * state_vals)[0]
        rate_next = jnp.concatenate([decay_rate[1:], jnp.ones_like(decay_rate[:1])], axis=0)
        suffix, local_adj = lax.associative_scan(
            combine_pair, (rate_next, grad_state), reverse=True, axis=0
        )
        send_back = jnp.where(seq_end, 0.0, decay_rate[0] * suffix[0])
        carry_back = entering(
            (send_back, decay_rate[0] * local_adj[0]),
            "dp",
            combine_pair,
            (jnp.ones_like(send_back), jnp.zeros_like(send_back)),
            True,
        )[1]
        carry_back = jnp.where(seq_end, 0.0, carry_back)
        adjoint = local_adj + suffix * carry_back
        before = jnp.concatenate([carry_in[None, :], state_vals[:-1]], axis=0)
        grad_mult = adjoint * conv_vals * gate_vals[0]
        grad_log = adjoint * before * decay_rate + jnp.where(
            at_start, 0.0, -grad_mult * square / root_term
        )
        decay_term = jnp.sum(grad_log * (-8.0 * gate_vals[1]), axis=0) * jax.nn.sigmoid(decay_param)
        grad_pre = (
            jnp.stack([adjoint * conv_vals * multiplier, grad_log * (-8.0 * decay_base)])
            * gate_vals
            * (1.0 - gate_vals)
        )
        grad_pre_low = grad_pre.astype(jnp.bfloat16).reshape(2, block_rows, heads_half, head_size)
        grad_rg = jnp.einsum(
            "chi,gchj->ghij", conv_heads, grad_pre_low, preferred_element_type=jnp.float32
        )
        grad_conv = adjoint * gate_vals[0] * multiplier + jnp.einsum(
            "gchj,ghij->chi", grad_pre_low, rg_gather, preferred_element_type=jnp.float32
        ).reshape(block_rows, lru_half)
        tap_grads = jnp.stack(
            [
                jnp.sum(grad_conv * extended[3 - tap : 3 - tap + block_rows], axis=0)
                for tap in range(4)
            ]
        )
        chan_acc.append(
            jnp.concatenate(
                [
                    tap_grads,
                    jnp.sum(grad_conv, axis=0)[None, :],
                    jnp.sum(grad_pre, axis=1),
                    decay_term[None, :],
                ],
                axis=0,
            )
        )
        grad_ext = sum(
            (jnp.pad(conv_taps[tap] * grad_conv, ((3 - tap, tap), (0, 0))) for tap in range(4))
        )
        rim_grad = jnp.where(seq_start, 0.0, grad_ext[:3])
        rim_next = passed_along(rim_grad, "dp", -1)
        grad_input_conv = grad_ext[3:] + jnp.pad(rim_next, ((block_rows - 3, 0), (0, 0)))
        grad_branch = jnp.stack([grad_gate_branch, grad_input_conv]).astype(jnp.bfloat16)
        grad_branch_w = jnp.einsum(
            "cd,kcl->kdl", normed_a, grad_branch, preferred_element_type=jnp.float32
        )
        grad_normed_a = lax.psum_scatter(
            jnp.einsum(
                "kcl,kdl->cd", grad_branch, branch_gather, preferred_element_type=jnp.float32
            ).astype(jnp.bfloat16),
            "mp",
            scatter_dimension=0,
            tiled=True,
        ).astype(jnp.float32)
        normal_own = lax.dynamic_slice_in_dim(normal_a, own_start, rows_own, 0)
        scale_own = lax.dynamic_slice_in_dim(scale_a, own_start, rows_own, 0)
        grad_input, gain_grad_a = rms_backward(grad_normed_a, normal_own, scale_own, norm_gains[0])
        grad_list.append(grad_input + grad_residual)
        gain_acc.append(jnp.stack([gain_grad_a, gain_grad_b]))
        mixer_part = (grad_branch_w, grad_rg, grad_out_w)
        mixer_total = add_tuple(mixer_total, mixer_part)
    mlp_total = (
        lax.psum_scatter(mlp_total[0], "dp", scatter_dimension=1, tiled=True),
        lax.psum_scatter(mlp_total[1], "dp", scatter_dimension=1, tiled=True),
    )
    mixer_total = (
        lax.psum_scatter(mixer_total[0], "dp", scatter_dimension=1, tiled=True),
        lax.psum_scatter(mixer_total[1], "dp", scatter_dimension=2, tiled=True),
        lax.psum_scatter(mixer_total[2], "dp", scatter_dimension=1, tiled=True),
    )
    chan_local = sum(chan_acc)
    slot_table = jnp.zeros((8, mp_count, lru_half), jnp.float32)
    slot_table = lax.dynamic_update_slice(slot_table, chan_local[:, None, :], (0, mp_index, 0))
    grad_gains, chan_table = lax.psum((sum(gain_acc), slot_table), ("dp", "mp"))
    chan_mine = lax.dynamic_index_in_dim(chan_table, mp_index, 1, keepdims=False)
    grad_chan = chan_mine[0:7]
    grad_decay = chan_mine[7]
    grad_w_branch, grad_gate_blocks, grad_w_out = mixer_total
    grad_w_mlp, grad_w_down = mlp_total
    return (
        jnp.stack(out_list),
        jnp.stack(grad_list),
        grad_gains,
        grad_w_branch,
        grad_chan,
        grad_gate_blocks,
        grad_decay,
        grad_w_out,
        grad_w_mlp,
        grad_w_down,
    )


def solution(mesh):
    return jax.shard_map(
        body,
        mesh=mesh,
        in_specs=(
            P(None, ("dp", "mp"), None),
            P(),
            P(),
            P(None, "dp", "mp"),
            P(None, "mp"),
            P(None, "mp", "dp", None),
            P("mp"),
            P("mp", "dp"),
            P(None, "dp", "mp"),
            P("mp", "dp"),
            P(None, ("dp", "mp"), None),
        ),
        out_specs=(
            P(None, ("dp", "mp"), None),
            P(None, ("dp", "mp"), None),
            P(),
            P(None, "dp", "mp"),
            P(None, "mp"),
            P(None, "mp", "dp", None),
            P("mp"),
            P("mp", "dp"),
            P(None, "dp", "mp"),
            P("mp", "dp"),
        ),
        check_vma=False,
    )
```

profile of v0, /device:TPU:0, one launch (start us, length us, event | category | flops | bytes accessed | tf_op | source)
XLA Modules:
  0.0 5542.7 jit_solution(9945402570691899889)
XLA Ops:
  19.0 151.4 %all-gather.16.cloned.1.call-done = bf16[2,2560,1280]{2,1,0:T(8,128)(2,1)} async-done(((bf16[2,160,1280]{2,1,0:T(8,128)(2,1)}), bf16[2,2560,1280]{2,1,0:T(8,128)(2,1)}) %all-gather.16.cloned.1.call-update) | async-done | bytes 13107216 | tf_op jit(solution)/shard_map/all_gather | solution.py:53
  170.4 7.8 fusion.178
  191.8 35.2 all-gather.18.cloned.1.call-done
  358.9 38.9 all-gather.2
  438.0 36.4 all-gather.4
  482.4 37.9 all-gather.5
  523.4 6.3 fusion.180
  537.9 37.1 all-gather.3
  578.5 6.1 fusion.179
  592.2 10.9 reduce-scatter.11.cloned.1.call-done
  608.3 403.9 %all-gather.22.cloned.1.call-done = bf16[2,2560,3840]{2,1,0:T(8,128)(2,1)} async-done(((bf16[2,160,3840]{2,1,0:T(8,128)(2,1)}), bf16[2,2560,3840]{2,1,0:T(8,128)(2,1)}) %all-gather.22.cloned.1.call-update) | async-done | bytes 39321616 | tf_op jit(solution)/shard_map/all_gather | solution.py:56
  1012.2 18.2 convolution_bitcast_fusion.1
  1030.4 201.8 %all-gather.24.cloned.1.call-done = bf16[3840,2560]{0,1:T(8,128)(2,1)} async-done(((bf16[3840,160]{0,1:T(8,128)(2,1)}), bf16[3840,2560]{0,1:T(8,128)(2,1)}) %all-gather.24.cloned.1.call-update) | async-done | bytes 19660816 | tf_op jit(solution)/shard_map/all_gather | solution.py:57
  1232.1 13.4 fusion.24
  1245.6 19.6 convolution_bitcast_fusion.3
  1295.6 5.5 slice.1237
  1312.1 5.5 slice.1313
  1317.6 5.5 slice.1315
  1345.1 5.5 slice.1243
  1379.4 15.2 convolution_bitcast_fusion
  1394.6 12.2 fusion.23
  1406.8 19.6 convolution_bitcast_fusion.2
  1451.3 6.0 rev.16
  1465.0 5.9 rev.17
  1471.9 38.3 all-gather.7
  1510.1 35.9 all-gather.6
  1625.8 6.0 rev.18
  1631.7 5.9 rev.19
  1637.6 37.8 all-gather.9
  1675.5 35.9 all-gather.8
  1754.4 10.0 fusion
  1764.7 14.2 convolution_convert_fusion.1
  1786.5 9.9 fusion.1
  1796.5 13.9 convolution_convert_fusion
  1815.5 11.8 fusion.75
  1827.3 17.2 add_bitcast_fusion.1
  1844.5 38.9 copy.101
  1885.1 28.7 fusion.20
  1913.8 53.4 add_bitcast_fusion
  1967.2 114.3 %copy.109 = f32[2,2560,3840]{2,0,1:T(2,128)} copy(f32[2,2560,3840]{1,2,0:T(8,128)} %add_bitcast_fusion) | data formatting | bytes 157286400 | tf_op jit(solution)/shard_map/add | solution.py:64
  2084.5 7.0 convolution_add_fusion.1
  2092.9 15.5 fusion.182
  2108.4 29.0 convolution_add_fusion
  2150.4 41.1 psum.14
  2195.5 477.8 %all-reduce.138.cloned.1.call-done = (f32[2,2560,1280]{2,0,1:T(2,128)}, f32[2,5,256,256]{3,0,1,2:T(2,128)}) async-done(((f32[2,2560,1280]{2,0,1:T(2,128)}, f32[2,5,256,256]{3,0,1,2:T(2,128)}), (f32[2,2560,1280]{2,0,1:T(2,128)}, f32[2,5,256,256]{3,0,1,2:T(2,128)})) %all-reduce.138.cloned.1.call-update) | async-done | bytes 28835856
  2678.2 2003.4 %all-reduce.136.cloned.1.call-done = f32[2,2560,3840]{2,0,1:T(2,128)} async-done(((f32[2,2560,3840]{2,0,1:T(2,128)}), f32[2,2560,3840]{2,0,1:T(2,128)}) %all-reduce.136.cloned.1.call-update) | async-done | bytes 78643216
  4688.2 267.7 %reduce-scatter.27.cloned.1.call-done = f32[1280,160]{0,1:T(8,128)} async-done(((f32[1280,2560]{0,1:T(8,128)}), f32[1280,160]{0,1:T(8,128)}) %reduce-scatter.27.cloned.1.call-update) | async-done | bytes 819216 | tf_op jit(solution)/shard_map/reduce_scatter | solution.py:295
  4956.0 579.4 %reduce-scatter.29.cloned.1.call-done = f32[3840,160]{0,1:T(8,128)} async-done(((f32[3840,2560]{0,1:T(8,128)}), f32[3840,160]{0,1:T(8,128)}) %reduce-scatter.29.cloned.1.call-update) | async-done | bytes 2457616 | tf_op jit(solution)/shard_map/reduce_scatter | solution.py:290
  (1052 shorter events, 526.0 us)
Async XLA Ops:
  7.2 163.2 %all-gather.16.cloned.1.call-start = ((), (), s32[]{:S(2)}) async-start(), calls=%async_computation.10 | async-start | bytes 13926400 | tf_op jit(solution)/shard_map/all_gather | solution.py:53
  7.9 219.0 %all-gather.18.cloned.1.call-start = ((), (), s32[]{:S(2)}) async-start(), calls=%async_computation.11 | async-start | bytes 1392640 | tf_op jit(solution)/shard_map/all_gather | solution.py:54
  9.5 513.9 %all-gather.20.cloned.1.call-start = ((), (), s32[]{:S(2)}) async-start(), calls=%async_computation.12 | async-start | bytes 6963200 | tf_op jit(solution)/shard_map/all_gather | solution.py:55
  10.3 581.9 %reduce-scatter.15.cloned.1.call-start = ((), (), s32[]{:S(2)}) async-start(), calls=%async_computation.17 | async-start | bytes 1966080 | tf_op jit(solution)/shard_map/reduce_scatter | solution.py:160
  11.1 224.4 %copy-start.115 = (f32[2,1280]{1,0:T(2,128)}, f32[2,1280]{1,0:T(2,128)S(1)}, u32[]{:S(2)}) copy-start(f32[2,1280]{1,0:T(2,128)S(1)} %slice.1080) | copy-start | bytes 30724
  12.2 177.6 %copy-start.119 = (f32[1280]{0:T(1024)}, f32[1280]{0:T(1024)S(1)}, u32[]{:S(2)}) copy-start(f32[1280]{0:T(1024)S(1)} %get-tuple-element.319) | copy-start | bytes 15364
  12.2 177.6 %copy-start.121 = (f32[1280]{0:T(1024)}, f32[1280]{0:T(1024)S(1)}, u32[]{:S(2)}) copy-start(f32[1280]{0:T(1024)S(1)} %get-tuple-element.320) | copy-start | bytes 15364
  12.2 177.6 %copy-start.123 = (f32[1280]{0:T(1024)}, f32[1280]{0:T(1024)S(1)}, u32[]{:S(2)}) copy-start(f32[1280]{0:T(1024)S(1)} %get-tuple-element.321) | copy-start | bytes 15364
  12.2 177.6 %copy-start.125 = (f32[1280]{0:T(1024)}, f32[1280]{0:T(1024)S(1)}, u32[]{:S(2)}) copy-start(f32[1280]{0:T(1024)S(1)} %get-tuple-element.322) | copy-start | bytes 15364
  12.2 225.8 %copy-start.159 = (pred[128]{0:T(512)(128)(4,1)}, pred[128]{0:T(512)(128)(4,1)S(1)}, u32[]{:S(2)}) copy-start(pred[128]{0:T(512)(128)(4,1)S(1)} %fusion.139) | copy-start | bytes 388
  13.8 167.9 %copy-start.95 = (f32[2560]{0:T(1024)}, f32[2560]{0:T(1024)S(1)}, u32[]{:S(2)}) copy-start(f32[2560]{0:T(1024)S(1)} %get-tuple-element.324) | copy-start | bytes 30724
  13.9 1535.5 %copy-start.99 = (f32[2560]{0:T(1024)}, f32[2560]{0:T(1024)S(1)}, u32[]{:S(2)}) copy-start(f32[2560]{0:T(1024)S(1)} %get-tuple-element.323) | copy-start | bytes 30724
  16.3 165.5 %copy-start.7 = (bf16[1,128,2560]{2,1,0:T(8,128)(2,1)}, bf16[1,128,2560]{2,1,0:T(8,128)(2,1)S(1)}, u32[]{:S(2)}) copy-start(bf16[1,128,2560]{2,1,0:T(8,128)(2,1)S(1)} %all-gather) | copy-start | bytes 1966084
  16.5 165.3 %copy-start.149 = (f32[128]{0:T(128)}, f32[128]{0:T(128)S(1)}, u32[]{:S(2)}) copy-start(f32[128]{0:T(128)S(1)} %add_rsqrt_fusion.3) | copy-start | bytes 1540
  18.8 159.4 %copy-start.10 = (bf16[1,128,2560]{2,1,0:T(8,128)(2,1)}, bf16[1,128,2560]{2,1,0:T(8,128)(2,1)S(1)}, u32[]{:S(2)}) copy-start(bf16[1,128,2560]{2,1,0:T(8,128)(2,1)S(1)} %all-gather.1) | copy-start | bytes 1966084
  19.0 159.2 %copy-start.154 = (f32[128]{0:T(128)}, f32[128]{0:T(128)S(1)}, u32[]{:S(2)}) copy-start(f32[128]{0:T(128)S(1)} %add_rsqrt_fusion.1) | copy-start | bytes 1540
  178.3 10.3 collective-permute-start.1
  184.9 4.8 collective-permute-start
  190.6 47.4 copy-start.21
  238.0 1478.9 %copy-start.4 = (f32[2,128,1280]{2,1,0:T(8,128)}, f32[2,128,1280]{2,1,0:T(8,128)S(1)}, u32[]{:S(2)}) copy-start(f32[2,128,1280]{2,1,0:T(8,128)S(1)} %get-tuple-element.558) | copy-start | bytes 3932164
  356.1 48.8 copy-start.109
  356.1 48.8 copy-start.110
  358.0 56.4 %copy-start.68 = (f32[128,1280]{1,0:T(8,128)}, f32[128,1280]{1,0:T(8,128)S(1)}, u32[]{:S(2)}) copy-start(f32[128,1280]{1,0:T(8,128)S(1)} %pad.409) | copy-start | bytes 1966084
  437.1 83.2 %copy-start.69 = (f32[128,1280]{1,0:T(8,128)}, f32[128,1280]{1,0:T(8,128)S(1)}, u32[]{:S(2)}) copy-start(f32[128,1280]{1,0:T(8,128)S(1)} %pad.437) | copy-start | bytes 1966084
  529.7 73.4 %reduce-scatter.11.cloned.1.call-start = ((), (), s32[]{:S(2)}) async-start(), calls=%async_computation.13 | async-start | bytes 1966080 | tf_op jit(solution)/shard_map/reduce_scatter | solution.py:160
  584.7 427.4 %all-gather.22.cloned.1.call-start = ((), (), s32[]{:S(2)}) async-start(), calls=%async_computation.14 | async-start | bytes 41779200 | tf_op jit(solution)/shard_map/all_gather | solution.py:56
  585.3 646.8 %all-gather.24.cloned.1.call-start = ((), (), s32[]{:S(2)}) async-start(), calls=%async_computation.15 | async-start | bytes 20889600 | tf_op jit(solution)/shard_map/all_gather | solution.py:57
  586.1 737.1 %reduce-scatter.19.cloned.1.call-start = ((), (), s32[]{:S(2)}) async-start(), calls=%async_computation.19 | async-start | bytes 1966080 | tf_op jit(solution)/shard_map/reduce_scatter | solution.py:192
  605.7 719.3 %copy-start.13 = (f32[64,2560]{1,0:T(8,128)}, f32[64,2560]{1,0:T(8,128)S(1)}, u32[]{:S(2)}) copy-start(f32[64,2560]{1,0:T(8,128)S(1)} %get-tuple-element.380) | copy-start | bytes 1966084
  605.8 719.3 %copy-start.152 = (f32[64]{0:T(128)}, f32[64]{0:T(128)S(1)}, u32[]{:S(2)}) copy-start(f32[64]{0:T(128)S(1)} %add_rsqrt_fusion.2) | copy-start | bytes 772
  1265.2 282.1 %reduce-scatter.23.cloned.1.call-start = ((), (), s32[]{:S(2)}) async-start(), calls=%async_computation.21 | async-start | bytes 1966080 | tf_op jit(solution)/shard_map/reduce_scatter | solution.py:192
  1323.2 226.2 %copy-start.157 = (f32[64]{0:T(128)}, f32[64]{0:T(128)S(1)}, u32[]{:S(2)}) copy-start(f32[64]{0:T(128)S(1)} %add_rsqrt_fusion) | copy-start | bytes 772
  1426.5 716.1 %all-reduce.134.cloned.1.call-start = ((), (), s32[]{:S(2)}) async-start(), calls=%async_computation.23 | async-start | bytes 163840 | tf_op jit(solution)/shard_map/psum | solution.py:300
  1462.8 84.5 %copy-start.15 = (f32[64,2560]{1,0:T(8,128)S(1)}, f32[64,2560]{1,0:T(8,128)}, u32[]{:S(2)}) copy-start(f32[64,2560]{1,0:T(8,128)} %get-tuple-element.428) | copy-start | bytes 1966084
  1625.8 87.3 %copy-start.20 = (bf16[128,1280]{1,0:T(8,128)(2,1)S(1)}, bf16[128,1280]{1,0:T(8,128)(2,1)}, u32[]{:S(2)}) copy-start(bf16[128,1280]{1,0:T(8,128)(2,1)} %copy-done.19) | copy-start | bytes 983044
  1625.8 87.3 %copy-start.22 = (bf16[128,1280]{1,0:T(8,128)(2,1)S(1)}, bf16[128,1280]{1,0:T(8,128)(2,1)}, u32[]{:S(2)}) copy-start(bf16[128,1280]{1,0:T(8,128)(2,1)} %copy-done.21) | copy-start | bytes 983044
  1625.8 87.3 %copy-start.131 = (f32[1,1280]{1,0:T(1,128)S(1)}, f32[1,1280]{1,0:T(1,128)}, u32[]{:S(2)}) copy-start(f32[1,1280]{1,0:T(1,128)} %broadcast_in_dim.107) | copy-start | bytes 15364
  1625.8 87.3 %copy-start.160 = (pred[128]{0:T(512)(128)(4,1)S(1)}, pred[128]{0:T(512)(128)(4,1)}, u32[]{:S(2)}) copy-start(pred[128]{0:T(512)(128)(4,1)} %copy-done.159) | copy-start | bytes 388
  1746.9 5.7 collective-permute-start.2
  1751.0 394.5 %reduce-scatter.21.cloned.1.call-start = ((), (), s32[]{:S(2)}) async-start(), calls=%async_computation.20 | async-start | bytes 983040 | tf_op jit(solution)/shard_map/reduce_scatter | solution.py:273
  1764.5 382.5 %reduce-scatter.13.cloned.1.call-start = ((), (), s32[]{:S(2)}) async-start(), calls=%async_computation.16 | async-start | bytes 983040 | tf_op jit(solution)/shard_map/reduce_scatter | solution.py:173
  1778.9 368.1 %reduce-scatter.25.cloned.1.call-start = ((), (), s32[]{:S(2)}) async-start(), calls=%async_computation.22 | async-start | bytes 983040 | tf_op jit(solution)/shard_map/reduce_scatter | solution.py:273
  1779.0 6.7 collective-permute-start.3
  1796.4 395.1 %reduce-scatter.17.cloned.1.call-start = ((), (), s32[]{:S(2)}) async-start(), calls=%async_computation.18 | async-start | bytes 983040 | tf_op jit(solution)/shard_map/reduce_scatter | solution.py:173
  1810.4 862.8 %all-reduce.138.cloned.1.call-start = ((), (), s32[]{:S(2)}) async-start(), calls=%async_computation.27 | async-start | bytes 57671680
  1883.4 2798.1 %all-reduce.136.cloned.1.call-start = ((), (), s32[]{:S(2)}) async-start(), calls=%async_computation.26 | async-start | bytes 157286400
  2081.5 2874.5 %reduce-scatter.27.cloned.1.call-start = ((), (), s32[]{:S(2)}) async-start(), calls=%async_computation.24 | async-start | bytes 13926400 | tf_op jit(solution)/shard_map/reduce_scatter | solution.py:295
  2091.6 3443.8 %reduce-scatter.29.cloned.1.call-start = ((), (), s32[]{:S(2)}) async-start(), calls=%async_computation.25 | async-start | bytes 41779200 | tf_op jit(solution)/shard_map/reduce_scatter | solution.py:290
  (149 other events, 1450.0 us)
Sparse Core Ops, SparseCore 0:
  10.7 159.5 all-gather.15
  173.7 53.2 all-gather.17
  229.7 95.7 all-gather.19
  529.8 5.7 reduce-scatter.14
  584.8 18.1 reduce-scatter.10
  605.6 406.5 all-gather.21
  1015.0 217.1 all-gather.23
  1265.3 6.9 reduce-scatter.18
  1426.6 7.0 reduce-scatter.22
  1751.1 119.2 all-reduce.133
  1872.6 10.0 reduce-scatter.20
  1884.9 9.2 reduce-scatter.12
  1897.0 9.2 reduce-scatter.24
  1908.5 9.2 reduce-scatter.16
  1924.7 748.5 all-reduce.137
  2680.7 2000.7 all-reduce.135
  4684.3 271.6 reduce-scatter.26
  4962.5 572.8 reduce-scatter.28
where the time goes:
time: 5570 us; the launch traced here: 5540 us
  waiting for transfers between devices  4140 us (74%)
  local copies, waits for them, and re-layouts  502 us (9%)
  blocking collectives  360 us (6%)
  matrix products  351 us (6%)
  other arithmetic  155 us (3%)
    unnamed x20, waiting for transfers between devices  2480 us
    reduce_scatter x1, waiting for transfers between devices, body(): lax.psum_scatter(mlp_total[1], 'dp', scatter_dimension=1, tiled=True)  579 us
    all_gather x1, waiting for transfers between devices, fetch_weights(): lax.all_gather(w_mlp, 'dp', axis=1, tiled=True)  404 us
    all_gather x8, blocking collectives, entering(): gathered = jax.tree.map(lambda a: lax.all_gather(a, axis), part)  298 us
    reduce_scatter x1, waiting for transfers between devices, body(): lax.psum_scatter(mixer_total[2], 'dp', scatter_dimension=1, tiled=True)  268 us
    all_gather x1, waiting for transfers between devices, fetch_weights(): lax.all_gather(w_down, 'dp', axis=1, tiled=True)  202 us
    add x3, local copies, waits for them, and re-layouts, add_tuple(): return tuple((left + right for left, right in zip(total, part_vals)))  156 us
    all_gather x1, waiting for transfers between devices, fetch_weights(): lax.all_gather(w_branch, 'dp', axis=1, tiled=True)  151 us
  transfers between devices with their start and end apart: 22, of which 12 were waited for; matrix products, arithmetic and copies ran while one was open for 13% of the time, Pallas kernels for 0%

commit v1 on v0

v1 whole, which is shorter than its diff:
```python
import functools

import jax
import jax.numpy as jnp
from jax import lax
from jax.experimental import pallas as pl
from jax.experimental.pallas import tpu as pltpu
from jax.sharding import PartitionSpec as P

MESH = pl.DeviceIdType.MESH
VMEM_LIMIT = 56 * 1024 * 1024


EPS = 1e-06
TP = 4
BF = jnp.bfloat16
F32 = jnp.float32


def combine_pair(earlier, later):
    return (earlier[0] * later[0], later[0] * earlier[1] + later[1])


def plan():
    ndp = lax.axis_size("dp")
    ng = ndp // TP
    dp = lax.axis_index("dp")
    return ndp, ng, dp // ng, dp % ng


def z_groups():
    ndp = lax.axis_size("dp")
    ng = ndp // TP
    return [[t * ng + g for t in range(TP)] for g in range(ng)]


def g_groups():
    ndp = lax.axis_size("dp")
    ng = ndp // TP
    return [[t * ng + g for g in range(ng)] for t in range(TP)]


class Comm:
    def __init__(self, send, recv):
        self.send, self.recv, self.n = send, recv, 0
        self.ndp = lax.axis_size("dp")
        self.ng = self.ndp // TP
        dp = lax.axis_index("dp")
        self.t, self.g, self.m = dp // self.ng, dp % self.ng, lax.axis_index("mp")
        self.bits = [1 << k for k in range(self.ng.bit_length() - 1)]

    def at(self, t=None, g=None, m=None):
        t = self.t if t is None else t
        g = self.g if g is None else g
        return (t * self.ng + g, self.m if m is None else m)

    def flip(self, g, b):
        return g + b - 2 * b * ((g // b) % 2)

    def barrier(self):
        sem = pltpu.get_barrier_semaphore()
        partners = [self.at(t=(self.t + o) % TP) for o in range(1, TP)]
        partners += [self.at(g=self.flip(self.g, b)) for b in self.bits] + [self.at(m=1 - self.m)]
        for p in partners:
            pl.semaphore_signal(sem, inc=1, device_id=p, device_id_type=MESH)
        pl.semaphore_wait(sem, len(partners))

    def slot(self):
        self.n += 1
        return self.n - 1

    def to(self, src, dst, dev, slot):
        return pltpu.make_async_remote_copy(
            src_ref=src, dst_ref=dst, send_sem=self.send.at[slot], recv_sem=self.recv.at[slot],
            device_id=dev, device_id_type=MESH,
        )

    def local(self, src, dst, slot):
        return pltpu.make_async_copy(src, dst, self.send.at[slot])


def run(*flows):
    flows = list(flows)
    while flows:
        for f in list(flows):
            try:
                next(f)
            except StopIteration:
                flows.remove(f)


def ag_flow(c, own, full):
    t, m = c.t, c.m
    sib = c.at(m=1 - m)
    up = [c.slot() for _ in range(TP - 1)]
    down = [c.slot() for _ in range(TP - 1)]
    d2u = [c.slot() for _ in range(TP - 1)]
    d2d = [c.slot() for _ in range(TP - 1)]
    d2o, loc = c.slot(), c.slot()

    def up_copy(k):
        b = t - k
        return c.to(own if k == 0 else full.at[:, b, m], full.at[:, b, m], c.at(t=t + 1), up[k])

    def down_copy(k):
        b = t + k
        return c.to(own if k == 0 else full.at[:, b, m], full.at[:, b, m], c.at(t=t - 1), down[k])

    def side(b, slot, src=None):
        return c.to(full.at[:, b, m] if src is None else src, full.at[:, b, m], sib, slot)

    def got(b, slot, mm):
        return c.to(full.at[:, b, mm], full.at[:, b, mm], sib, slot)

    pl.when(t < TP - 1)(lambda: up_copy(0).start())
    pl.when(t > 0)(lambda: down_copy(0).start())
    side(t, d2o, own).start()
    c.local(own, full.at[:, t, m], loc).start()
    yield
    for k in range(TP - 1):
        def from_below():
            got(t - 1 - k, up[k], m).wait_recv()
            side(t - 1 - k, d2u[k]).start()
            if k < TP - 2:
                pl.when(t < TP - 1)(lambda: up_copy(k + 1).start())

        def from_above():
            got(t + 1 + k, down[k], m).wait_recv()
            side(t + 1 + k, d2d[k]).start()
            if k < TP - 2:
                pl.when(t > 0)(lambda: down_copy(k + 1).start())

        pl.when(t - 1 - k >= 0)(from_below)
        pl.when(t + 1 + k < TP)(from_above)
        yield
    c.local(own, full.at[:, t, m], loc).wait()
    side(t, d2o, own).wait_send()
    got(t, d2o, 1 - m).wait_recv()
    for k in range(TP - 1):
        pl.when((t < TP - 1) & (t - k >= 0))(lambda: up_copy(k).wait_send())
        pl.when((t > 0) & (t + k < TP))(lambda: down_copy(k).wait_send())

        def below():
            side(t - 1 - k, d2u[k]).wait_send()
            got(t - 1 - k, d2u[k], 1 - m).wait_recv()

        def above():
            side(t + 1 + k, d2d[k]).wait_send()
            got(t + 1 + k, d2d[k], 1 - m).wait_recv()

        pl.when(t - 1 - k >= 0)(below)
        pl.when(t + 1 + k < TP)(above)


def rs_scratch(rows, width):
    return [
        pltpu.VMEM((2, TP, rows, width), BF),
        pltpu.VMEM((2, TP - 1, 2, rows, width), BF),
        pltpu.VMEM((2, TP - 1, 2, rows, width), BF),
    ]


def rs_flow(c, part, out, sib, inbox, outbox):
    t, m = c.t, c.m
    n = part.shape[3]
    other = c.at(m=1 - m)
    lower = t < TP // 2
    u = jnp.where(lower, t, TP - 1 - t)
    da = jnp.where(lower, 0, 1)
    step = 1 - 2 * da
    near = [c.slot() for _ in range(TP)]
    base = c.n
    for _ in range(2 * (TP - 1)):
        c.slot()

    def real(d):
        return jnp.where(lower, d, TP - 1 - d)

    def cross(d):
        return c.to(part.at[:, real(d), 1 - m], sib.at[:, real(d)], other, near[d])

    def msg(flow, j):
        way = da if flow == 0 else 1 - da
        dev = c.at(t=t + step if flow == 0 else t - step)
        return c.to(outbox.at[way, j], inbox.at[way, j], dev, base + way * (TP - 1) + j)

    def add(d, into, terms):
        b = real(d)

        def rows16(i, _):
            sl = pl.ds(pl.multiple_of(i * 16, 16), 16)
            for s in range(2):
                v = part[s, b, m, sl, :].astype(F32) + sib[s, b, sl, :].astype(F32)
                for way, j in terms:
                    v = v + inbox[way, j, s, sl, :].astype(F32)
                into(s, sl, v)
            return 0

        lax.fori_loop(0, n // 16, rows16, 0)

    def put(way, j):
        def into(s, sl, v):
            outbox[way, j, s, sl, :] = v.astype(BF)
        return into

    def final(s, sl, v):
        out[s, sl, :] = v

    for d in (3, 2, 0, 1):
        cross(d).start()
    yield
    for d, j in ((3, 0), (2, 1)):
        cross(d).wait_recv()
        for lvl in range(2):
            def go():
                if lvl == 1:
                    msg(0, j).wait_recv()
                add(d, put(da, j), [(da, j)] if lvl else [])
                msg(0, j).start()
            pl.when(u == lvl)(go)
        yield
    cross(0).wait_recv()
    cross(1).wait_recv()

    def first():
        add(1, put(da, 2), [])
        msg(0, 2).start()

    pl.when(u == 0)(first)

    def back():
        msg(1, 0).wait_recv()
        add(0, put(1 - da, 0), [(1 - da, 0)])
        msg(1, 0).start()

    pl.when(u == 1)(back)
    yield

    def end0():
        msg(1, 0).wait_recv()
        add(0, final, [(1 - da, 0)])

    def end1():
        msg(0, 2).wait_recv()
        msg(1, 1).wait_recv()
        add(1, final, [(da, 2), (1 - da, 1)])

    pl.when(u == 0)(end0)
    pl.when(u == 1)(end1)
    for d in range(TP):
        cross(d).wait_send()
    for j in range(2):
        msg(0, j).wait_send()
    pl.when(u == 0)(lambda: msg(0, 2).wait_send())
    pl.when(u == 1)(lambda: msg(1, 0).wait_send())


def spread_z(c, src, dst, need=None):
    slots = [c.slot() for _ in range(TP)]

    def copy(o):
        to = (c.t + o) % TP
        return c.to(src(to), dst(c.t), c.at(t=to), slots[o])

    def mine():
        return c.local(src(c.t), dst(c.t), slots[0])

    def back(o):
        frm = (c.t + TP - o) % TP
        return c.to(src(frm), dst(frm), c.at(t=frm), slots[o])

    def when(t, f):
        if need is None:
            f()
        else:
            pl.when(t == need)(f)

    for o in range(1, TP):
        when((c.t + o) % TP, lambda: copy(o).start())
    when(c.t, lambda: mine().start())
    yield
    when(c.t, lambda: mine().wait())
    for o in range(1, TP):
        when(c.t, lambda: back(o).wait_recv())
    yield
    for o in range(1, TP):
        when((c.t + o) % TP, lambda: copy(o).wait_send())


def plane_gather(c, block, order):
    have = [0]
    done = []
    for b in order:
        dev = c.at(g=c.flip(c.g, b))
        sent = []
        for x in have:
            gg = c.g
            for bit in c.bits:
                if x & bit:
                    gg = c.flip(gg, bit)
            copy = c.to(block(gg), block(gg), dev, c.slot())
            copy.start()
            sent.append(copy)
        yield
        for copy in sent:
            copy.wait_recv()
        done += sent
        have = have + [x ^ b for x in have]
    for copy in done:
        copy.wait_send()


def plane_reduce(c, own, sums, inbox, order):
    def place(x):
        gg = c.g
        for bit in c.bits:
            if x & bit:
                gg = c.flip(gg, bit)
        return gg

    left = list(range(c.ng))
    spot = {}
    done = []
    base = 0
    for k, b in enumerate(order):
        dev = c.at(g=c.flip(c.g, b))
        away = [x for x in left if x & b]
        left = [x for x in left if not x & b]
        sent = []
        for i, x in enumerate(away):
            src = own(place(x)) if k == 0 else sums.at[spot[x]]
            copy = c.to(src, inbox.at[base + i], dev, c.slot())
            copy.start()
            sent.append(copy)
        held = []
        if k == 0:
            spot = {x: i for i, x in enumerate(left)}
            for x in left:
                held.append(c.local(own(place(x)), sums.at[spot[x]], c.slot()))
                held[-1].start()
        yield
        for i, x in enumerate(left):
            sent[i].wait_recv()
            if k == 0:
                held[i].wait()
            add_blocks(sums.at[spot[x]], inbox.at[base + i])
        base += len(away)
        done += sent
    for copy in done:
        copy.wait_send()


def add_blocks(a, b):
    def one(i, _):
        a[i] = (a[i].astype(F32) + b[i].astype(F32)).astype(BF)
        return 0

    lax.fori_loop(0, a.shape[0], one, 0)


def call(kernel, out_shape, in_specs, out_specs, scratch, cid, slots=160):
    return pl.pallas_call(
        kernel,
        out_shape=out_shape,
        in_specs=in_specs,
        out_specs=out_specs,
        scratch_shapes=list(scratch) + [pltpu.SemaphoreType.DMA((slots,)), pltpu.SemaphoreType.DMA((slots,))],
        compiler_params=pltpu.CompilerParams(collective_id=cid, has_side_effects=True, vmem_limit_bytes=VMEM_LIMIT),
    )


HBM = pl.BlockSpec(memory_space=pl.ANY)
VM = pl.BlockSpec(memory_space=pltpu.VMEM)


def start_kernel(x, go, gain, wbr, wot, gates, mlp, full_a, full_g, wb, wo, gb, wm, own, zero, send, recv):
    c = Comm(send, recv)
    c.barrier()
    r = wbr.shape[1]

    def head(ref, lead):
        def src(t):
            lane = pl.multiple_of(t * 256, 256)
            return ref.at[(*lead, slice(None), pl.ds(lane, 256))]
        return src

    pieces = []
    for k in range(2):
        pieces.append((head(wbr, (k,)), wb, (k,), wbr.at[k, :, pl.ds(1024, 256)]))
    pieces.append((head(wot, ()), wo, (), wot.at[:, pl.ds(1024, 256)]))
    z = []
    for src, dst, lead, extra in pieces:
        z.append(spread_z(c, src, lambda t, dst=dst, lead=lead: dst.at[(*lead, t, c.g, slice(None), pl.ds(0, 256))]))
        z.append(spread_z(c, lambda t, extra=extra: extra, lambda t, dst=dst, lead=lead: dst.at[(*lead, t, c.g, slice(None), pl.ds(256, 256))], 1))
    z.append(spread_z(c, lambda t: gates.at[:, t], lambda t: gb.at[:, 0, t, c.g]))
    z.append(spread_z(c, lambda t: gates.at[:, 4], lambda t: gb.at[:, 1, t, c.g], 1))
    for f in z:
        next(f)
    x32 = [x[s].astype(F32) for s in range(2)]
    for s in range(2):
        v = x32[s] * lax.rsqrt(jnp.mean(x32[s] * x32[s], axis=-1, keepdims=True) + EPS) * gain[...]
        own[s] = v.astype(BF)
    ag = ag_flow(c, own, full_a)
    next(ag)
    zero[...] = jnp.zeros_like(zero)
    fills = []
    for k in range(2):
        fills.append((zero, wb.at[k, :, c.g, :, pl.ds(256, 256)], c.slot()))
    fills.append((zero, wo.at[:, c.g, :, pl.ds(256, 256)], c.slot()))
    for k in range(2):
        fills.append((zero.at[:, pl.ds(0, gates.shape[2])], gb.at[k, 1, :, c.g], c.slot()))

    def fill():
        for f in fills:
            c.local(*f).start()
        for f in fills:
            c.local(*f).wait()

    pl.when(c.t != 1)(fill)
    zm = [spread_z(c, lambda t, k=k: mlp.at[t, k], lambda t, k=k: wm.at[k, t, c.g]) for k in range(3)]
    for f in z:
        next(f)
    fwd, rev = c.bits, c.bits[::-1]
    g1 = [plane_gather(c, lambda g: wb.at[0, :, g], fwd), plane_gather(c, lambda g: wb.at[1, :, g], rev),
          plane_gather(c, lambda g: wo.at[pl.ds(0, 2), g], fwd), plane_gather(c, lambda g: wo.at[pl.ds(2, 2), g], rev),
          plane_gather(c, lambda g: gb.at[0, :, :, g], fwd), plane_gather(c, lambda g: gb.at[1, :, :, g], rev)]
    for f in g1:
        next(f)
    next(ag)
    ag2 = ag_flow(c, go, full_g)
    for f in zm:
        next(f)
    for f in g1:
        next(f)
    run(ag)
    next(ag2)
    for f in zm:
        next(f)
    g2 = [plane_gather(c, lambda g: wm.at[0, :, g], fwd), plane_gather(c, lambda g: wm.at[1, :, g], rev),
          plane_gather(c, lambda g: wm.at[2, pl.ds(0, 2), g], fwd), plane_gather(c, lambda g: wm.at[2, pl.ds(2, 2), g], rev)]
    run(*z, *zm, *g1, *g2, ag2)


def start_call(x, go, gain, wbr, wot, gates, mlp):
    ng = lax.axis_size("dp") // TP
    _, n, d = x.shape
    r, gr, fs = wbr.shape[1], gates.shape[2], mlp.shape[3]
    S = jax.ShapeDtypeStruct
    return call(
        start_kernel,
        (S((2, TP, 2, n, d), BF), S((2, TP, 2, n, d), BF), S((2, TP, ng, r, 512), BF), S((TP, ng, r, 512), BF),
         S((2, 2, TP, ng, gr, 256), BF), S((3, TP, ng, r, fs), BF)),
        [VM, VM, VM, HBM, HBM, HBM, HBM],
        (HBM,) * 6,
        [pltpu.VMEM((2, n, d), BF), pltpu.VMEM((TP, r, 256), BF)],
        1,
    )(x, go, gain[None], wbr, wot, gates, mlp)


def mid_kernel(part, x, gain, res, full, tot, own, sib, inbox, outbox, send, recv):
    c = Comm(send, recv)
    c.barrier()
    run(rs_flow(c, part, tot, sib, inbox, outbox))
    for s in range(2):
        v = x[s].astype(F32) + tot[s]
        res[s] = v
        own[s] = (v * lax.rsqrt(jnp.mean(v * v, axis=-1, keepdims=True) + EPS) * gain[...]).astype(BF)
    run(ag_flow(c, own, full))


def mid_call(part, x, gain):
    _, n, d = x.shape
    S = jax.ShapeDtypeStruct
    return call(
        mid_kernel,
        (S((2, n, d), F32), S((2, TP, 2, n, d), BF)),
        [VM, VM, VM],
        (VM, HBM),
        [pltpu.VMEM((2, n, d), F32), pltpu.VMEM((2, n, d), BF)] + rs_scratch(n, d),
        2,
    )(part.reshape(2, TP, 2, n, d), x, gain[None])


def back_kernel(part, part2, res, go, gain, gres, gsum, mlp_own, full, tot, own, sib, inbox, outbox, sib2, inbox2, outbox2, send, recv):
    c = Comm(send, recv)
    c.barrier()
    run(rs_flow(c, part, tot, sib, inbox, outbox))
    total = jnp.zeros_like(gsum)
    for s in range(2):
        v = res[s]
        scale = lax.rsqrt(jnp.mean(v * v, axis=-1, keepdims=True) + EPS)
        normal = v * scale
        gn = tot[s]
        total = total + jnp.sum(gn * normal, axis=0, keepdims=True)
        q = gn * gain[...]
        gr = scale * (q - normal * jnp.mean(q * normal, axis=-1, keepdims=True)) + go[s].astype(F32)
        gres[s] = gr
        own[s] = gr.astype(BF)
    gsum[...] = total
    run(ag_flow(c, own, full), rs_flow(c, part2, mlp_own, sib2, inbox2, outbox2))


def back_call(part, part2, res, go, gain):
    _, n, d = go.shape
    S = jax.ShapeDtypeStruct
    shape = (2, TP, 2, n, d)
    return call(
        back_kernel,
        (S((2, n, d), F32), S((1, d), F32), S((2, n, d), F32), S(shape, BF)),
        [VM] * 5,
        (VM, VM, VM, HBM),
        [pltpu.VMEM((2, n, d), F32), pltpu.VMEM((2, n, d), BF)] + rs_scratch(n, d) + rs_scratch(n, d),
        3,
    )(part.reshape(shape), part2.reshape(shape), res, go, gain[None])


def end_kernel(part, x, gres, gain, gwb, gwo, ggb, gwm, gin, gsum, owb, owo, ogb, owm,
               tot, sib, inbox, outbox, su_m, in_m, su_x, in_x, su_g, in_g, send, recv):
    c = Comm(send, recv)
    c.barrier()
    fwd, rev = c.bits, c.bits[::-1]
    red, spread = [], []
    for k in range(3):
        own = lambda g, k=k: gwm.at[k, :, g]
        red.append(plane_reduce(c, own, su_m.at[k], in_m.at[k], rev if k % 2 else fwd))
        spread.append(spread_z(c, lambda t, k=k: su_m.at[k, 0, t], lambda t, k=k: owm.at[k, t]))
    for k in range(3):
        own = (lambda g, k=k: gwb.at[k, :, g]) if k < 2 else (lambda g: gwo.at[:, g])
        out = (lambda t, k=k: owb.at[k, t]) if k < 2 else (lambda t: owo.at[t])
        red.append(plane_reduce(c, own, su_x.at[k], in_x.at[k], fwd if k % 2 else rev))
        spread.append(spread_z(c, lambda t, k=k: su_x.at[k, 0, t], out))
    for k in range(2):
        for h in range(2):
            i = 2 * k + h
            red.append(plane_reduce(c, lambda g, k=k, h=h: ggb.at[k, h, :, g], su_g.at[i], in_g.at[i], fwd if k else rev))
            spread.append(spread_z(c, lambda t, i=i: su_g.at[i, 0, t], lambda t, k=k, h=h: ogb.at[k, h, t]))
    rs = rs_flow(c, part, tot, sib, inbox, outbox)
    next(rs)
    for f in red:
        next(f)
    run(rs)
    total = jnp.zeros_like(gsum)
    for s in range(2):
        v = x[s].astype(F32)
        scale = lax.rsqrt(jnp.mean(v * v, axis=-1, keepdims=True) + EPS)
        normal = v * scale
        gn = tot[s]
        total = total + jnp.sum(gn * normal, axis=0, keepdims=True)
        q = gn * gain[...]
        gin[s] = scale * (q - normal * jnp.mean(q * normal, axis=-1, keepdims=True)) + gres[s]
    gsum[...] = total
    for _ in range(len(c.bits) - 1):
        for f in red:
            next(f)
    for f, s in zip(red, spread):
        run(f)
        next(s)
    run(*spread)


def end_call(part, x, gres, gain, gwb, gwo, ggb, gwm):
    _, n, d = x.shape
    ng = lax.axis_size("dp") // TP
    r, gr, fs = gwb.shape[3], ggb.shape[4], gwm.shape[4]
    S = jax.ShapeDtypeStruct
    half = ng // 2

    def sets(k, rows, width):
        return [pltpu.VMEM((k, half, TP, rows, width), BF), pltpu.VMEM((k, ng - 1, TP, rows, width), BF)]

    return call(
        end_kernel,
        (S((2, n, d), F32), S((1, d), F32), S((2, TP, r, 512), BF), S((TP, r, 512), BF), S((2, 2, TP, gr, 256), BF), S((3, TP, r, fs), BF)),
        [VM] * 4 + [HBM] * 4,
        (VM, VM) + (HBM,) * 4,
        [pltpu.VMEM((2, n, d), F32)] + rs_scratch(n, d) + sets(3, r, fs) + sets(3, r, 512) + sets(4, gr, 256),
        4, 400,
    )(part.reshape(2, TP, 2, n, d), x, gres, gain[None], gwb, gwo, ggb, gwm)


def heads_of(a, axis):
    _, _, t, _ = plan()
    p = lax.dynamic_slice_in_dim(a, t * 256, 256, axis)
    q = lax.dynamic_slice_in_dim(a, 1024, 256, axis)
    q = jnp.where(t == 1, q, jnp.zeros_like(q))
    return jnp.concatenate([p, q], axis)


def heads_back(a, axis):
    ga = lax.all_gather(a, "dp", axis=0, axis_index_groups=z_groups())
    parts = [lax.slice_in_dim(ga[i], 0, 256, axis=axis) for i in range(TP)] + [lax.slice_in_dim(ga[1], 256, 512, axis=axis)]
    return jnp.concatenate(parts, axis)


def gather_g(x):
    return lax.all_gather(x, "dp", axis=0, axis_index_groups=g_groups())


def shift_blocks(x, step):
    ndp, ng, t, g = plan()
    ga = gather_g(x)
    seq = ga.reshape(ng, 2, TP, *x.shape[1:]).transpose(1, 2, 0, 3, 4).reshape(2, ndp, *x.shape[1:])
    z = jnp.zeros_like(seq[:, :1])
    if step == 1:
        seq = jnp.concatenate([z, seq[:, :-1]], 1)
    else:
        seq = jnp.concatenate([seq[:, 1:], z], 1)
    seq = seq.reshape(2, TP, ng, *x.shape[1:])
    return lax.dynamic_index_in_dim(seq, g, 2, False).reshape(x.shape)


def carries(prod, last, reverse):
    ndp, ng, t, g = plan()
    C = prod.shape[-1]
    def seqd(x):
        return gather_g(x).reshape(ng, 2, TP, C).transpose(1, 2, 0, 3).reshape(2, ndp, C)
    p, l = seqd(prod), seqd(last)
    c = jnp.zeros((2, C), F32)
    outs = [None] * ndp
    order = range(ndp - 1, -1, -1) if reverse else range(ndp)
    for i in order:
        outs[i] = c
        c = l[:, i] + p[:, i] * c
    o = jnp.stack(outs, 1).reshape(2, TP, ng, C)
    return lax.dynamic_index_in_dim(o, g, 2, False).reshape(8, C)


def mixer_forward(branch0, conv_input, gb, chan, decay_base, at_start):
    C = conv_input.shape[-1]
    ci = conv_input.reshape(8, -1, C)
    n = ci.shape[1]
    rim = shift_blocks(ci[:, n - 3:], 1)
    ext = jnp.concatenate([rim, ci], 1).astype(F32)
    conv = chan[4] + chan[0] * ext[:, 3:] + chan[1] * ext[:, 2:n + 2]
    conv = conv + chan[2] * ext[:, 1:n + 1] + chan[3] * ext[:, :n]
    conv_low = conv.astype(BF)
    cv = conv_low.astype(F32)
    pre = jnp.einsum("bnhi,ghij->gbnhj", conv_low.reshape(8, n, 2, 256), gb, preferred_element_type=F32).reshape(2, 8, n, C)
    gv = jax.nn.sigmoid(pre + chan[5:7][:, None, None, :])
    log_a = -8.0 * gv[1] * decay_base
    decay = jnp.exp(log_a)
    root = jnp.sqrt(-jnp.expm1(2.0 * log_a))
    mult = jnp.where(at_start, 1.0, root)
    drive = cv * gv[0] * mult
    prod, loc = lax.associative_scan(combine_pair, (decay, drive), axis=1)
    carry = carries(prod[:, -1], loc[:, -1], False)
    state = loc + prod * carry[:, None]
    mixed = (state * jax.nn.gelu(branch0.reshape(8, n, C))).astype(BF)
    return mixed.reshape(8 * n, C), (ext, conv_low, gv, state, carry, prod[:, -1])


def mixer_backward(grad_mixed, branch0, saved, gb, chan, decay_base, at_start):
    ext, conv_low, gv, state, carry, pl_ = saved
    n, C = conv_low.shape[1:]
    cv = conv_low.astype(F32)
    branch0 = branch0.reshape(8, n, C)
    gm = grad_mixed.reshape(8, n, C)
    gelu, pull = jax.vjp(jax.nn.gelu, branch0)
    grad_gate_branch = pull(gm * state)[0]
    gs = gm * gelu
    log_a = -8.0 * gv[1] * decay_base
    decay = jnp.exp(log_a)
    root = jnp.sqrt(-jnp.expm1(2.0 * log_a))
    mult = jnp.where(at_start, 1.0, root)
    rate_next = jnp.concatenate([decay[:, 1:], jnp.ones_like(decay[:, :1])], 1)
    suffix, loc = lax.associative_scan(combine_pair, (rate_next, gs), reverse=True, axis=1)
    back = carries(decay[:, 0] * suffix[:, 0], decay[:, 0] * loc[:, 0], True)
    adj = loc + suffix * back[:, None]
    before = jnp.concatenate([carry[:, None], state[:, :-1]], 1)
    gmult = adj * cv * gv[0]
    glog = adj * before * decay + jnp.where(at_start, 0.0, -gmult * jnp.exp(2.0 * log_a) / root)
    gdec = jnp.sum(glog * (-8.0 * gv[1]), axis=(0, 1))
    gpre = jnp.stack([adj * cv * mult, glog * (-8.0 * decay_base)]) * gv * (1.0 - gv)
    gpl = gpre.astype(BF).reshape(2, 8, n, 2, 256)
    ggb = jnp.einsum("bnhi,gbnhj->ghij", conv_low.reshape(8, n, 2, 256), gpl, preferred_element_type=F32)
    gconv = adj * gv[0] * mult + jnp.einsum("gbnhj,ghij->bnhi", gpl, gb, preferred_element_type=F32).reshape(8, n, C)
    taps = [jnp.sum(gconv * ext[:, 3 - k:3 - k + n], axis=(0, 1)) for k in range(4)]
    rows = jnp.stack(taps + [jnp.sum(gconv, axis=(0, 1)), jnp.sum(gpre[0], axis=(0, 1)), jnp.sum(gpre[1], axis=(0, 1)), gdec])
    nxt = shift_blocks(gconv[:, :3], -1)
    gext = jnp.concatenate([gconv, nxt], 1)
    gci = sum(chan[k] * gext[:, k:k + n] for k in range(4))
    gbr = jnp.stack([grad_gate_branch, gci]).astype(BF)
    return gbr.reshape(2, 8 * n, C), ggb, rows


def dot(a, b, ca, cb):
    return lax.dot_general(a, b, (((ca,), (cb,)), ((), ())), preferred_element_type=F32)


def pack(parts):
    return jnp.stack(parts)


def body(block_input, lengths, norm_gains, w_branch, channel_params, gate_blocks, decay_param, w_out, w_mlp, w_down, out_grad):
    ndp, ng, t, g = plan()
    dp, mp = lax.axis_index("dp"), lax.axis_index("mp")
    rows, width = block_input.shape[1:]
    r = w_branch.shape[1]
    fs = w_mlp.shape[2] // TP
    chan = heads_of(channel_params, 1)
    dpar = heads_of(decay_param[None], 1)[0]
    decay_base = jax.nn.softplus(dpar)
    pos = dp * 2 * rows + mp * rows + jnp.arange(rows, dtype=jnp.int32)
    valid = (pos[None] < lengths[:, None])[..., None]
    blk = jnp.arange(8) % TP * ng + g
    at_start = ((blk[:, None] * 2 * rows + jnp.arange(2 * rows)[None]) == 0)[..., None]
    x = block_input
    grad_own = jnp.where(valid, out_grad, jnp.zeros_like(out_grad))
    mlp = jnp.concatenate([w_mlp, w_down.T[None]], 0).reshape(3, r, TP, fs).transpose(2, 0, 1, 3)
    na, go, wb, wo, gb, wm = start_call(x, grad_own, norm_gains[0], w_branch, w_out.T, gate_blocks, mlp)
    na, go = na.reshape(-1, width), go.reshape(-1, width)
    wb, wo, wm = wb.reshape(2, width, 512), wo.reshape(width, 512), wm.reshape(3, width, fs)
    gb = gb.reshape(2, 2, 256, 256)
    wd = wm[2]
    branch0 = dot(na, wb[0], 1, 0)
    conv_input = dot(na, wb[1], 1, 0).astype(BF)
    mixed, saved = mixer_forward(branch0, conv_input, gb, chan, decay_base, at_start)
    residual, nb = mid_call(dot(mixed, wo, 1, 1).astype(BF), x, norm_gains[1])
    nb = nb.reshape(-1, width)
    first, second = dot(nb, wm[0], 1, 0), dot(nb, wm[1], 1, 0)
    act, act_pull = jax.vjp(jax.nn.gelu, first)
    hidden = (act * second).astype(BF)
    mlp_part = dot(hidden, wd, 1, 1).astype(BF)
    gh = dot(go, wd, 1, 0)
    gwd = dot(go, hidden, 0, 0).astype(BF)
    ggu = [act_pull(gh * second)[0].astype(BF), (gh * act).astype(BF)]
    gwm = [dot(nb, ggu[k], 0, 0).astype(BF) for k in range(2)]
    gnb = (dot(ggu[0], wm[0], 1, 1) + dot(ggu[1], wm[1], 1, 1)).astype(BF)
    gres, gain_b, mlp_own, gmo = back_call(gnb, mlp_part, residual, grad_own, norm_gains[1])
    out = jnp.where(valid, residual + mlp_own, 0.0).astype(BF)
    gmo = gmo.reshape(-1, width)
    gwo = dot(gmo, mixed, 0, 0).astype(BF)
    gbr, ggb, chan_rows = mixer_backward(dot(gmo, wo, 1, 0), branch0, saved, gb, chan, decay_base, at_start)
    gwb = [dot(na, gbr[k], 0, 0).astype(BF) for k in range(2)]
    gna = (dot(gbr[0], wb[0], 1, 1) + dot(gbr[1], wb[1], 1, 1)).astype(BF)
    gr = gate_blocks.shape[2]
    gin, gain_a, owb, owo, ogb, owm = end_call(
        gna, x, gres, norm_gains[0],
        jnp.stack(gwb).reshape(2, TP, ng, r, 512), gwo.reshape(TP, ng, r, 512),
        ggb.astype(BF).reshape(2, 2, TP, ng, gr, 256), jnp.stack(gwm + [gwd]).reshape(3, TP, ng, r, fs),
    )
    owb, owo = owb.astype(F32), owo.astype(F32)
    g_wb = jnp.concatenate([owb[:, i, :, :256] for i in range(TP)] + [owb[:, 1, :, 256:]], -1)
    g_wo = jnp.concatenate([owo[i, :, :256] for i in range(TP)] + [owo[1, :, 256:]], -1).T
    g_gb = jnp.concatenate([ogb[:, 0], ogb[:, 1, 1:2]], 1).astype(F32)
    g_wm = owm[:2].transpose(0, 2, 1, 3).reshape(2, r, TP * fs).astype(F32)
    g_wd = owm[2].transpose(0, 2, 1).reshape(TP * fs, r).astype(F32)
    gains = lax.psum(jnp.concatenate([gain_a, gain_b]), ("dp", "mp"))
    chan_rows = lax.psum(chan_rows, "dp", axis_index_groups=g_groups())
    crow = heads_back(chan_rows, 1)
    return out, gin, gains, g_wb, crow[:7], g_gb, crow[7] * jax.nn.sigmoid(decay_param), g_wo, g_wm, g_wd


def solution(mesh):
    return jax.shard_map(
        body,
        mesh=mesh,
        in_specs=(P(None, ("dp", "mp"), None), P(), P(), P(None, "dp", "mp"), P(None, "mp"), P(None, "mp", "dp", None), P("mp"), P("mp", "dp"), P(None, "dp", "mp"), P("mp", "dp"), P(None, ("dp", "mp"), None)),
        out_specs=(P(None, ("dp", "mp"), None), P(None, ("dp", "mp"), None), P(), P(None, "dp", "mp"), P(None, "mp"), P(None, "mp", "dp", None), P("mp"), P("mp", "dp"), P(None, "dp", "mp"), P("mp", "dp")),
        check_vma=False,
    )
```

time: 5570 us -> 1670 us (0.30)
  waiting for transfers between devices: 4140 us -> 0 us
  Pallas kernels: 0 us -> 812 us
  blocking collectives: 360 us -> 117 us
  matrix products: 351 us -> 149 us
  local copies, waits for them, and re-layouts: 502 us -> 402 us
    unnamed x20 -> x0, waiting for transfers between devices: 2480 us -> none
    reduce_scatter x10 -> x0, waiting for transfers between devices: 858 us -> none  [the longest x1 579 us: body(): lax.psum_scatter(mlp_total[1], 'dp', scatter_dimension=1, tiled=True)]
    pallas_call x0 -> x4, Pallas kernels: none -> 812 us  [the longest x1 300 us: start_call(): call(start_kernel, (S((2, TP, 2, n, d), BF), S((2, TP, 2, n, d), BF), S((...]
    all_gather x5 -> x0, waiting for transfers between devices: 792 us -> none  [the longest x1 404 us: fetch_weights(): lax.all_gather(w_mlp, 'dp', axis=1, tiled=True)]
    all_gather x16 -> x7, blocking collectives: 318 us -> 61.6 us  [the longest x6 48.3 us: gather_g(): return lax.all_gather(x, 'dp', axis=0, axis_index_groups=g_groups())]
    dot_general x30 -> x21, matrix products: 351 us -> 149 us  [the longest x18 144 us: dot(): lax.dot_general(a, b, (((ca,), (cb,)), ((), ())), preferred_element_type=...]
    add x3 -> x0, local copies, waits for them, and re-layouts: 156 us -> none  [add_tuple(): return tuple((left + right for left, right in zip(total, part_vals)))]
    pad x96 -> x48, local copies, waits for them, and re-layouts: 67.8 us -> 141 us  [the longest x24 75.3 us: mixer_backward(): lax.associative_scan(combine_pair, (rate_next, gs), reverse=True, axis=1)]
  transfers between devices with their start and end apart: 22 -> 0, of which waited for: 12 -> 0; matrix products, arithmetic and copies ran while one was open for 13% -> 0% of each run, Pallas kernels for 0% -> 0%
where the time goes in v1:
time: 1670 us; the launch traced here: 1650 us
  Pallas kernels  812 us (49%)
  local copies, waits for them, and re-layouts  402 us (24%)
  other arithmetic  171 us (10%)
  matrix products  149 us (9%)
  blocking collectives  117 us (7%)
    pallas_call x1, Pallas kernels, start_call(): call(start_kernel, (S((2, TP, 2, n, d), BF), S((2, TP, 2, n, d), BF), S((...  300 us
    pallas_call x1, Pallas kernels, end_call(): call(end_kernel, (S((2, n, d), F32), S((1, d), F32), S((2, TP, r, 512), B...  287 us
    dot_general x18, matrix products, dot(): lax.dot_general(a, b, (((ca,), (cb,)), ((), ())), preferred_element_type=...  144 us
    pallas_call x1, Pallas kernels, back_call(): call(back_kernel, (S((2, n, d), F32), S((1, d), F32), S((2, n, d), F32),...  120 us
    pallas_call x1, Pallas kernels, mid_call(): call(mid_kernel, (S((2, n, d), F32), S((2, TP, 2, n, d), BF)), [VM, VM, V...  105 us
    pad x24, local copies, waits for them, and re-layouts, mixer_backward(): lax.associative_scan(combine_pair, (rate_next, gs), reverse=True, axis=1)  75.3 us
    pad x24, local copies, waits for them, and re-layouts, mixer_forward(): prod, loc = lax.associative_scan(combine_pair, (decay, drive), axis=1)  65.5 us
    slice x49, local copies, waits for them, and re-layouts, mixer_backward(): lax.associative_scan(combine_pair, (rate_next, gs), reverse=True, axis=1)  60.5 us

profile of v1, /device:TPU:0, one launch (start us, length us, event | category | flops | bytes accessed | tf_op | source)
XLA Modules:
  0.0 1653.5 jit_solution(18065180467147704073)
XLA Ops:
  8.7 6.3 concatenate.123
  18.7 299.8 %shard_map.186 = (bf16[2,4,2,64,2560]{4,3,2,1,0:T(8,128)(2,1)}, bf16[2,4,2,64,2560]{4,3,2,1,0:T(8,128)(2,1)}, bf16[2,4,4,160,512]{4,3,2,1,0:T(8,128)(2,1)}, bf16...) custom-call(bf16[2,64,2560]{2,1,0:T(8,128)(2,1)} %x.125, ...), custom_call_target="tpu_custom_call" | custom-call | tf_op jit(solution)/shard_map/pallas_call | solution.py:449
  326.0 8.0 all-gather
  359.3 5.6 slice.829
  459.7 5.8 pad.201
  467.9 6.8 pad.203
  474.7 5.6 slice.875
  490.6 5.9 pad.186
  501.8 6.8 pad.202
  509.6 7.6 all-gather.2
  519.8 6.9 pad.189
  534.6 7.9 all-gather.1
  552.9 11.3 multiply_convert_fusion.2
  568.9 105.2 %shard_map.187 = (f32[2,64,2560]{2,1,0:T(8,128)}, bf16[2,4,2,64,2560]{4,3,2,1,0:T(8,128)(2,1)}) custom-call(bf16[2,4,2,64,2560]{4,3,2,1,0:T(8,128)(2,1)} %bitcast.291, bf16[2,64,2560]{2,1,0:T(8,128)(2,1)} %x.125, f32[1,2560]{1,0:T(1,128)} %get-tuple-element.161.gain), custom_call_target="tpu_custom_call" | custom-call | tf_op jit(solution)/shard_map/pallas_call | solution.py:474
  674.1 7.3 fusion.120
  681.4 10.5 fusion.133
  692.0 7.2 fusion.132
  699.2 14.3 multiply_convert_fusion
  713.4 11.1 fusion.134
  724.6 10.1 add_convert_fusion.1
  734.6 9.6 convolution_convert_fusion.1
  744.2 119.6 %shard_map.188 = (f32[2,64,2560]{2,1,0:T(8,128)}, f32[1,2560]{1,0:T(1,128)}, f32[2,64,2560]{2,1,0:T(8,128)}, bf16[2,4,2,64,2560]{4,3,2,1,0:T(8,128)(2,1)}) custom-call(bf16[2,4,2,64,2560]{4,3,2,1,0:T(8,128)(2,1)} %bitcast.289, bf16[2,4,2,64,2560]{4,3,2,1,0:T(8,128)(2,1)} %bitcast.290, f32[2,64,2560]{2,1,0:T(8,128)} %get-tuple-element.32.res, ...), custom_call_target="tpu_custom_call" | custom-call | tf_op jit(solution)/shard_map/pallas_call | solution.py:507
  866.3 9.5 fusion.42
  875.8 5.8 fusion.135
  1031.0 5.8 pad.214
  1042.4 6.8 pad.216
  1051.6 6.9 pad.217
  1062.5 16.6 %rev.8 = f32[8,128,512]{2,1,0:T(8,128)} reverse(f32[8,128,512]{2,1,0:T(8,128)} %add.878), dimensions={1} | reverse | bytes 4194304 | tf_op jit(solution)/shard_map/rev | solution.py:666
  1093.0 16.8 %rev.9 = f32[8,128,512]{2,1,0:T(8,128)} reverse(f32[8,128,512]{2,1,0:T(8,128)} %add.885), dimensions={1} | reverse | bytes 4194304 | tf_op jit(solution)/shard_map/rev | solution.py:666
  1111.0 8.4 all-gather.4
  1119.7 7.3 all-gather.3
  1127.6 6.3 multiply_reduce_fusion
  1165.7 9.0 all-gather.5
  1176.7 7.7 add_convert_fusion
  1184.4 5.8 convolution_convert_fusion.6
  1202.3 6.9 convolution_convert_fusion.2
  1209.2 8.0 copy.142
  1217.2 9.4 convolution_convert_fusion.3
  1226.5 8.0 copy.141
  1234.5 9.5 convolution_convert_fusion.4
  1244.0 7.8 copy.140
  1251.9 13.3 pad_maximum_fusion.gwm
  1265.2 287.2 %shard_map.189 = (f32[2,64,2560]{2,1,0:T(8,128)}, f32[1,2560]{1,0:T(1,128)}, bf16[2,4,160,512]{3,2,1,0:T(8,128)(2,1)}, bf16[4,160,512]{2,1,0:T(8,128)(2,1)}, bf1...) custom-call(bf16[2,4,2,64,2560]{4,3,2,1,0:T(8,128)(2,1)} %bitcast.292, bf16[2,64,2560]{2,1,0:T(8,128)(2,1)} %x.125, ...), custom_call_target="tpu_custom_call" | custom-call | tf_op jit(solution)/shard_map/pallas_call | solution.py:571
  1553.1 38.8 %psum.14 = f32[2,2560]{1,0:T(2,128)} all-reduce(f32[2,2560]{1,0:T(2,128)S(1)} %pad_maximum_fusion.27), channel_id=1, replica_groups=mesh['dp'=16,'mp'=2] {'dp','mp'}, use_global_device_ids=true, to_apply=%region_0.1 | all-reduce | flops 5120 | bytes 40960 | tf_op jit(solution)/shard_map/psum | solution.py:748
  1597.8 16.9 %psum.15 = f32[1,8,512]{2,1,0:T(8,128)S(1)} all-reduce(f32[1,8,512]{2,1,0:T(8,128)S(1)} %bitcast.423), channel_id=1, replica_groups={{0,2,4,6},{8,10,12,14},{16,18,20,22},{24,26,28,30},{1,3,5,7},{9,11,13,1..., use_global_device_ids=true, to_apply=%region_9.10 | all-reduce | flops 4096 | bytes 32768 | tf_op jit(solution)/shard_map/psum | solution.py:749
  1614.7 13.3 all_gather.41
  1630.9 5.7 copy.148
  1636.7 7.4 reshape.363
  (565 shorter events, 426.3 us)
Async XLA Ops:
  334.7 20.4 %copy-start = (f32[8,131,512]{2,1,0:T(8,128)}, f32[8,131,512]{2,1,0:T(8,128)S(1)}, u32[]{:S(2)}) copy-start(f32[8,131,512]{2,1,0:T(8,128)S(1)} %maximum_convert_fusion) | copy-start | bytes 6438916
  335.6 19.6 %copy-start.58 = (f32[1,512]{1,0:T(1,128)}, f32[1,512]{1,0:T(1,128)S(1)}, u32[]{:S(2)}) copy-start(f32[1,512]{1,0:T(1,128)S(1)} %get-tuple-element.164) | copy-start | bytes 6148
  335.6 19.6 %copy-start.60 = (f32[1,512]{1,0:T(1,128)}, f32[1,512]{1,0:T(1,128)S(1)}, u32[]{:S(2)}) copy-start(f32[1,512]{1,0:T(1,128)S(1)} %get-tuple-element.165) | copy-start | bytes 6148
  335.6 19.6 %copy-start.62 = (f32[1,512]{1,0:T(1,128)}, f32[1,512]{1,0:T(1,128)S(1)}, u32[]{:S(2)}) copy-start(f32[1,512]{1,0:T(1,128)S(1)} %get-tuple-element.166) | copy-start | bytes 6148
  335.6 19.6 %copy-start.64 = (f32[1,512]{1,0:T(1,128)}, f32[1,512]{1,0:T(1,128)S(1)}, u32[]{:S(2)}) copy-start(f32[1,512]{1,0:T(1,128)S(1)} %get-tuple-element.167) | copy-start | bytes 6148
  335.6 19.6 %copy-start.72 = (f32[1,512]{1,0:T(1,128)}, f32[1,512]{1,0:T(1,128)S(1)}, u32[]{:S(2)}) copy-start(f32[1,512]{1,0:T(1,128)S(1)} %get-tuple-element.163) | copy-start | bytes 6148
  379.6 9.6 copy-start.18
  422.9 26.3 %copy-start.24 = (f32[8,32,512]{2,1,0:T(8,128)}, f32[8,32,512]{2,1,0:T(8,128)S(1)}, u32[]{:S(2)}) copy-start(f32[8,32,512]{2,1,0:T(8,128)S(1)} %pad.185) | copy-start | bytes 1572868
  439.3 12.6 copy-start.26
  457.2 10.7 copy-start.14
  474.7 8.5 copy-start.25
  474.7 8.5 copy-start.27
  517.4 25.4 %copy-start.54 = (f32[4,2,4,512]{3,1,0,2:T(2,128)}, f32[4,2,4,512]{3,1,0,2:T(2,128)S(1)}, u32[]{:S(2)}) copy-start(f32[4,2,4,512]{3,1,0,2:T(2,128)S(1)} %copy.121) | copy-start | bytes 196612
  529.1 13.7 copy-start.78
  552.9 11.3 copy-start.86
  674.1 17.8 %slice-start = ((s8[5242880]{0:T(1024)(128)(4,1)}), s8[4194304]{0:T(1024)(128)(4,1)S(1)}, s32[]{:S(2)}) async-start(s8[5242880]{0:T(1024)(128)(4,1)} %bitcast.443), calls=%async_computation | async-start | bytes 8388608
  681.4 10.5 copy-start.22
  681.4 10.5 slice-start.1
  713.4 11.1 copy-start.91
  744.2 119.6 %copy-start.20 = (f32[2,64,2560]{2,1,0:T(8,128)S(1)}, f32[2,64,2560]{2,1,0:T(8,128)}, u32[]{:S(2)}) copy-start(f32[2,64,2560]{2,1,0:T(8,128)} %get-tuple-element.32.res) | copy-start | bytes 3932164
  744.2 119.6 %copy-start.84 = (pred[2,64]{1,0:T(4,128)(4,1)S(1)}, pred[2,64]{1,0:T(4,128)(4,1)}, u32[]{:S(2)}) copy-start(pred[2,64]{1,0:T(4,128)(4,1)} %copy-done.83) | copy-start | bytes 388
  866.3 9.5 copy-start.40
  896.2 103.6 %copy-start.19 = (f32[8,64,512]{2,1,0:T(8,128)}, f32[8,64,512]{2,1,0:T(8,128)S(1)}, u32[]{:S(2)}) copy-start(f32[8,64,512]{2,1,0:T(8,128)S(1)} %get-tuple-element.98) | copy-start | bytes 3145732
  903.9 77.9 %copy-start.36 = (f32[8,32,512]{2,1,0:T(8,128)}, f32[8,32,512]{2,1,0:T(8,128)S(1)}, u32[]{:S(2)}) copy-start(f32[8,32,512]{2,1,0:T(8,128)S(1)} %get-tuple-element.106) | copy-start | bytes 1572868
  909.9 35.9 %copy-start.47 = (f32[8,16,512]{2,1,0:T(8,128)}, f32[8,16,512]{2,1,0:T(8,128)S(1)}, u32[]{:S(2)}) copy-start(f32[8,16,512]{2,1,0:T(8,128)S(1)} %get-tuple-element.114) | copy-start | bytes 786436
  916.3 37.5 %copy-start.51 = (f32[8,8,512]{2,1,0:T(8,128)}, f32[8,8,512]{2,1,0:T(8,128)S(1)}, u32[]{:S(2)}) copy-start(f32[8,8,512]{2,1,0:T(8,128)S(1)} %get-tuple-element.122) | copy-start | bytes 393220
  1001.3 10.3 copy-start.29
  1006.2 8.1 copy-start.30
  1014.6 9.0 copy-start.31
  1014.6 9.0 copy-start.33
  1092.9 34.6 %copy-start.1 = (f32[8,131,512]{2,1,0:T(8,128)S(1)}, f32[8,131,512]{2,1,0:T(8,128)}, u32[]{:S(2)}) copy-start(f32[8,131,512]{2,1,0:T(8,128)} %copy-done) | copy-start | bytes 6438916
  1092.9 34.6 %copy-start.59 = (f32[1,512]{1,0:T(1,128)S(1)}, f32[1,512]{1,0:T(1,128)}, u32[]{:S(2)}) copy-start(f32[1,512]{1,0:T(1,128)} %copy-done.58) | copy-start | bytes 6148
  1092.9 34.6 %copy-start.61 = (f32[1,512]{1,0:T(1,128)S(1)}, f32[1,512]{1,0:T(1,128)}, u32[]{:S(2)}) copy-start(f32[1,512]{1,0:T(1,128)} %copy-done.60) | copy-start | bytes 6148
  1092.9 34.6 %copy-start.63 = (f32[1,512]{1,0:T(1,128)S(1)}, f32[1,512]{1,0:T(1,128)}, u32[]{:S(2)}) copy-start(f32[1,512]{1,0:T(1,128)} %copy-done.62) | copy-start | bytes 6148
  1092.9 34.6 %copy-start.65 = (f32[1,512]{1,0:T(1,128)S(1)}, f32[1,512]{1,0:T(1,128)}, u32[]{:S(2)}) copy-start(f32[1,512]{1,0:T(1,128)} %copy-done.64) | copy-start | bytes 6148
  1092.9 34.6 %copy-start.68 = (f32[2,4,1,512]{3,2,1,0:T(1,128)S(1)}, f32[2,4,1,512]{3,2,1,0:T(1,128)}, u32[]{:S(2)}) copy-start(f32[2,4,1,512]{3,2,1,0:T(1,128)} %copy.173) | copy-start | bytes 49156
  1093.0 34.6 %copy-start.71 = (f32[512]{0:T(512)S(1)}, f32[512]{0:T(512)}, u32[]{:S(2)}) copy-start(f32[512]{0:T(512)} %copy-done.70) | copy-start | bytes 6148
  1093.0 34.6 %copy-start.73 = (f32[1,512]{1,0:T(1,128)S(1)}, f32[1,512]{1,0:T(1,128)}, u32[]{:S(2)}) copy-start(f32[1,512]{1,0:T(1,128)} %copy-done.72) | copy-start | bytes 6148
  1093.0 34.6 %copy-start.80 = (pred[8,128]{1,0:T(8,128)(4,1)S(1)}, pred[8,128]{1,0:T(8,128)(4,1)}, u32[]{:S(2)}) copy-start(pred[8,128]{1,0:T(8,128)(4,1)} %copy-done.79) | copy-start | bytes 3076
  1165.7 9.4 copy-start.16
  1176.7 13.6 slice-start.4
  1184.4 11.9 slice-start.6
  1193.5 8.8 slice-start.2
  1265.2 287.2 %copy-start.81 = (f32[1,2560]{1,0:T(1,128)S(1)}, f32[1,2560]{1,0:T(1,128)}, u32[]{:S(2)}) copy-start(f32[1,2560]{1,0:T(1,128)} %get-tuple-element.41) | copy-start | bytes 30724
  1265.2 329.9 %copy-start.11 = (f32[8,128,512]{2,1,0:T(8,128)S(1)}, f32[8,128,512]{2,1,0:T(8,128)}, u32[]{:S(2)}) copy-start(f32[8,128,512]{2,1,0:T(8,128)} %get-tuple-element.169) | copy-start | bytes 6291460
  1597.4 30.7 %copy-start.74 = (bf16[2,2,4,16,256]{4,3,2,1,0:T(8,128)(2,1)S(1)}, bf16[2,2,4,16,256]{4,3,2,1,0:T(8,128)(2,1)}, u32[]{:S(2)}) copy-start(bf16[2,2,4,16,256]{4,3,2,1,0:T(8,128)(2,1)} %get-tuple-element.43) | copy-start | bytes 393220
  1597.5 31.4 %copy-start.76 = (f32[1280]{0:T(1024)S(1)}, f32[1280]{0:T(1024)}, u32[]{:S(2)}) copy-start(f32[1280]{0:T(1024)} %param.17) | copy-start | bytes 15364
  1597.5 32.0 %copy-start.52 = (bf16[4,160,512]{2,1,0:T(8,128)(2,1)S(1)}, bf16[4,160,512]{2,1,0:T(8,128)(2,1)}, u32[]{:S(2)}) copy-start(bf16[4,160,512]{2,1,0:T(8,128)(2,1)} %get-tuple-element.44) | copy-start | bytes 1966084
  (55 other events, 191.0 us)

commit v2 on v1

--- a/solution.py
+++ b/solution.py
@@ -8,17 +8,13 @@
 from jax.sharding import PartitionSpec as P
 
 MESH = pl.DeviceIdType.MESH
-VMEM_LIMIT = 56 * 1024 * 1024
+VMEM_LIMIT = 60 * 1024 * 1024
 
 
 EPS = 1e-06
 TP = 4
 BF = jnp.bfloat16
 F32 = jnp.float32
-
-
-def combine_pair(earlier, later):
-    return (earlier[0] * later[0], later[0] * earlier[1] + later[1])
 
 
 def plan():
@@ -26,18 +22,6 @@
     ng = ndp // TP
     dp = lax.axis_index("dp")
     return ndp, ng, dp // ng, dp % ng
-
-
-def z_groups():
-    ndp = lax.axis_size("dp")
-    ng = ndp // TP
-    return [[t * ng + g for t in range(TP)] for g in range(ng)]
-
-
-def g_groups():
-    ndp = lax.axis_size("dp")
-    ng = ndp // TP
-    return [[t * ng + g for g in range(ng)] for t in range(TP)]
 
 
 class Comm:
@@ -514,8 +498,29 @@
     )(part.reshape(shape), part2.reshape(shape), res, go, gain[None])
 
 
-def end_kernel(part, x, gres, gain, gwb, gwo, ggb, gwm, gin, gsum, owb, owo, ogb, owm,
-               tot, sib, inbox, outbox, su_m, in_m, su_x, in_x, su_g, in_g, send, recv):
+def small_flow(c, small, inbox, zbox, sbox, gains, table):
+    for k, b in enumerate(c.bits):
+        copy = c.to(small.at[k], inbox.at[k], c.at(g=c.flip(c.g, b)), c.slot())
+        copy.start()
+        yield
+        copy.wait()
+        small[k + 1] = small[k] + inbox[k]
+    last = len(c.bits)
+    z = spread_z(c, lambda t: small.at[last], lambda t: zbox.at[t])
+    next(z)
+    yield
+    run(z)
+    sbox[0] = zbox[0, 0:8] + zbox[1, 0:8] + zbox[2, 0:8] + zbox[3, 0:8]
+    table[...] = zbox[:, 8:16, 0:512]
+    copy = c.to(sbox.at[0], sbox.at[1], c.at(m=1 - c.m), c.slot())
+    copy.start()
+    yield
+    copy.wait()
+    gains[...] = sbox[0] + sbox[1]
+
+
+def end_kernel(part, x, gres, gain, gwb, gwo, ggb, gwm, gain_b, chan_rows, gin, gains, table, owb, owo, ogb, owm,
+               small, small_in, zbox, sbox, tot, sib, inbox, outbox, su_m, in_m, su_x, in_x, su_g, in_g, send, recv):
     c = Comm(send, recv)
     c.barrier()
     fwd, rev = c.bits, c.bits[::-1]
@@ -539,7 +544,7 @@
     for f in red:
         next(f)
     run(rs)
-    total = jnp.zeros_like(gsum)
+    total = jnp.zeros_like(gain)
     for s in range(2):
         v = x[s].astype(F32)
         scale = lax.rsqrt(jnp.mean(v * v, axis=-1, keepdims=True) + EPS)
@@ -548,17 +553,23 @@
         total = total + jnp.sum(gn * normal, axis=0, keepdims=True)
         q = gn * gain[...]
         gin[s] = scale * (q - normal * jnp.mean(q * normal, axis=-1, keepdims=True)) + gres[s]
-    gsum[...] = total
+    small[0] = jnp.zeros_like(small[0])
+    small[0, 0:1, :] = total
+    small[0, 1:2, :] = gain_b[...]
+    small[0, 8:16, 0:512] = chan_rows[...]
+    sm = small_flow(c, small, small_in, zbox, sbox, gains, table)
+    next(sm)
     for _ in range(len(c.bits) - 1):
         for f in red:
             next(f)
+        next(sm)
     for f, s in zip(red, spread):
         run(f)
         next(s)
-    run(*spread)
-
-
-def end_call(part, x, gres, gain, gwb, gwo, ggb, gwm):
+    run(sm, *spread)
+
+
+def end_call(part, x, gres, gain, gwb, gwo, ggb, gwm, gain_b, chan_rows):
     _, n, d = x.shape
     ng = lax.axis_size("dp") // TP
     r, gr, fs = gwb.shape[3], ggb.shape[4], gwm.shape[4]
@@ -570,12 +581,13 @@
 
     return call(
         end_kernel,
-        (S((2, n, d), F32), S((1, d), F32), S((2, TP, r, 512), BF), S((TP, r, 512), BF), S((2, 2, TP, gr, 256), BF), S((3, TP, r, fs), BF)),
-        [VM] * 4 + [HBM] * 4,
-        (VM, VM) + (HBM,) * 4,
-        [pltpu.VMEM((2, n, d), F32)] + rs_scratch(n, d) + sets(3, r, fs) + sets(3, r, 512) + sets(4, gr, 256),
+        (S((2, n, d), F32), S((8, d), F32), S((TP, 8, 512), F32), S((2, TP, r, 512), BF), S((TP, r, 512), BF), S((2, 2, TP, gr, 256), BF), S((3, TP, r, fs), BF)),
+        [VM] * 4 + [HBM] * 4 + [VM] * 2,
+        (VM,) * 3 + (HBM,) * 4,
+        [pltpu.VMEM((ng.bit_length(), 16, d), F32), pltpu.VMEM((ng.bit_length() - 1, 16, d), F32), pltpu.VMEM((TP, 16, d), F32), pltpu.VMEM((2, 8, d), F32)]
+        + [pltpu.VMEM((2, n, d), F32)] + rs_scratch(n, d) + sets(3, r, fs) + sets(3, r, 512) + sets(4, gr, 256),
         4, 400,
-    )(part.reshape(2, TP, 2, n, d), x, gres, gain[None], gwb, gwo, ggb, gwm)
+    )(part.reshape(2, TP, 2, n, d), x, gres, gain[None], gwb, gwo, ggb, gwm, gain_b, chan_rows)
 
 
 def heads_of(a, axis):
@@ -586,101 +598,255 @@
     return jnp.concatenate([p, q], axis)
 
 
-def heads_back(a, axis):
-    ga = lax.all_gather(a, "dp", axis=0, axis_index_groups=z_groups())
-    parts = [lax.slice_in_dim(ga[i], 0, 256, axis=axis) for i in range(TP)] + [lax.slice_in_dim(ga[1], 256, 512, axis=axis)]
-    return jnp.concatenate(parts, axis)
-
-
-def gather_g(x):
-    return lax.all_gather(x, "dp", axis=0, axis_index_groups=g_groups())
-
-
-def shift_blocks(x, step):
-    ndp, ng, t, g = plan()
-    ga = gather_g(x)
-    seq = ga.reshape(ng, 2, TP, *x.shape[1:]).transpose(1, 2, 0, 3, 4).reshape(2, ndp, *x.shape[1:])
-    z = jnp.zeros_like(seq[:, :1])
-    if step == 1:
-        seq = jnp.concatenate([z, seq[:, :-1]], 1)
-    else:
-        seq = jnp.concatenate([seq[:, 1:], z], 1)
-    seq = seq.reshape(2, TP, ng, *x.shape[1:])
-    return lax.dynamic_index_in_dim(seq, g, 2, False).reshape(x.shape)
-
-
-def carries(prod, last, reverse):
-    ndp, ng, t, g = plan()
-    C = prod.shape[-1]
-    def seqd(x):
-        return gather_g(x).reshape(ng, 2, TP, C).transpose(1, 2, 0, 3).reshape(2, ndp, C)
-    p, l = seqd(prod), seqd(last)
-    c = jnp.zeros((2, C), F32)
-    outs = [None] * ndp
-    order = range(ndp - 1, -1, -1) if reverse else range(ndp)
-    for i in order:
-        outs[i] = c
-        c = l[:, i] + p[:, i] * c
-    o = jnp.stack(outs, 1).reshape(2, TP, ng, C)
-    return lax.dynamic_index_in_dim(o, g, 2, False).reshape(8, C)
-
-
-def mixer_forward(branch0, conv_input, gb, chan, decay_base, at_start):
-    C = conv_input.shape[-1]
-    ci = conv_input.reshape(8, -1, C)
-    n = ci.shape[1]
-    rim = shift_blocks(ci[:, n - 3:], 1)
-    ext = jnp.concatenate([rim, ci], 1).astype(F32)
-    conv = chan[4] + chan[0] * ext[:, 3:] + chan[1] * ext[:, 2:n + 2]
-    conv = conv + chan[2] * ext[:, 1:n + 1] + chan[3] * ext[:, :n]
-    conv_low = conv.astype(BF)
-    cv = conv_low.astype(F32)
-    pre = jnp.einsum("bnhi,ghij->gbnhj", conv_low.reshape(8, n, 2, 256), gb, preferred_element_type=F32).reshape(2, 8, n, C)
-    gv = jax.nn.sigmoid(pre + chan[5:7][:, None, None, :])
-    log_a = -8.0 * gv[1] * decay_base
-    decay = jnp.exp(log_a)
-    root = jnp.sqrt(-jnp.expm1(2.0 * log_a))
-    mult = jnp.where(at_start, 1.0, root)
-    drive = cv * gv[0] * mult
-    prod, loc = lax.associative_scan(combine_pair, (decay, drive), axis=1)
-    carry = carries(prod[:, -1], loc[:, -1], False)
-    state = loc + prod * carry[:, None]
-    mixed = (state * jax.nn.gelu(branch0.reshape(8, n, C))).astype(BF)
-    return mixed.reshape(8 * n, C), (ext, conv_low, gv, state, carry, prod[:, -1])
-
-
-def mixer_backward(grad_mixed, branch0, saved, gb, chan, decay_base, at_start):
-    ext, conv_low, gv, state, carry, pl_ = saved
-    n, C = conv_low.shape[1:]
-    cv = conv_low.astype(F32)
-    branch0 = branch0.reshape(8, n, C)
-    gm = grad_mixed.reshape(8, n, C)
-    gelu, pull = jax.vjp(jax.nn.gelu, branch0)
-    grad_gate_branch = pull(gm * state)[0]
-    gs = gm * gelu
-    log_a = -8.0 * gv[1] * decay_base
-    decay = jnp.exp(log_a)
-    root = jnp.sqrt(-jnp.expm1(2.0 * log_a))
-    mult = jnp.where(at_start, 1.0, root)
-    rate_next = jnp.concatenate([decay[:, 1:], jnp.ones_like(decay[:, :1])], 1)
-    suffix, loc = lax.associative_scan(combine_pair, (rate_next, gs), reverse=True, axis=1)
-    back = carries(decay[:, 0] * suffix[:, 0], decay[:, 0] * loc[:, 0], True)
-    adj = loc + suffix * back[:, None]
-    before = jnp.concatenate([carry[:, None], state[:, :-1]], 1)
-    gmult = adj * cv * gv[0]
-    glog = adj * before * decay + jnp.where(at_start, 0.0, -gmult * jnp.exp(2.0 * log_a) / root)
-    gdec = jnp.sum(glog * (-8.0 * gv[1]), axis=(0, 1))
-    gpre = jnp.stack([adj * cv * mult, glog * (-8.0 * decay_base)]) * gv * (1.0 - gv)
-    gpl = gpre.astype(BF).reshape(2, 8, n, 2, 256)
-    ggb = jnp.einsum("bnhi,gbnhj->ghij", conv_low.reshape(8, n, 2, 256), gpl, preferred_element_type=F32)
-    gconv = adj * gv[0] * mult + jnp.einsum("gbnhj,ghij->bnhi", gpl, gb, preferred_element_type=F32).reshape(8, n, C)
-    taps = [jnp.sum(gconv * ext[:, 3 - k:3 - k + n], axis=(0, 1)) for k in range(4)]
-    rows = jnp.stack(taps + [jnp.sum(gconv, axis=(0, 1)), jnp.sum(gpre[0], axis=(0, 1)), jnp.sum(gpre[1], axis=(0, 1)), gdec])
-    nxt = shift_blocks(gconv[:, :3], -1)
-    gext = jnp.concatenate([gconv, nxt], 1)
-    gci = sum(chan[k] * gext[:, k:k + n] for k in range(4))
-    gbr = jnp.stack([grad_gate_branch, gci]).astype(BF)
-    return gbr.reshape(2, 8 * n, C), ggb, rows
+def gelu_pair(v):
+    k = 0.7978845608028654
+    v2 = v * v
+    th = jnp.tanh(k * v * (1.0 + 0.044715 * v2))
+    half = 0.5 * (1.0 + th)
+    return v * half, half + 0.5 * v * (1.0 - th * th) * k * (1.0 + 3.0 * 0.044715 * v2)
+
+
+def decay_terms(ga, db):
+    log_a = -8.0 * ga * db
+    y = 2.0 * log_a
+    series = 1.0 + y * (1 / 8)
+    for k in range(7, 1, -1):
+        series = 1.0 + y * (1 / k) * series
+    m1 = jnp.where(y > -0.35, y * series, jnp.exp(y) - 1.0)
+    return jnp.exp(log_a), jnp.sqrt(-m1)
+
+
+def lanes_in(ref, rows, v):
+    for q in range(ref.shape[0]):
+        ref[q, rows, :] = v[:, q * 128:(q + 1) * 128]
+
+
+def lanes_out(ref, rows):
+    return jnp.concatenate([ref[q, rows, :] for q in range(ref.shape[0])], axis=1)
+
+
+def each(ref, at):
+    return [ref[q, at, :] for q in range(ref.shape[0])]
+
+
+def split(v):
+    return [v[:, q * 128:(q + 1) * 128] for q in range(v.shape[1] // 128)]
+
+
+def plane_partners(c):
+    return [c.at(g=(c.g + o) % c.ng) for o in range(1, c.ng)]
+
+
+def greet(partners):
+    sem = pltpu.get_barrier_semaphore()
+    for p in partners:
+        pl.semaphore_signal(sem, inc=1, device_id=p, device_id_type=MESH)
+    pl.semaphore_wait(sem, len(partners))
+
+
+def share(c, table):
+    copies = []
+    for o in range(1, c.ng):
+        slot = c.slot()
+        copies.append((o, slot))
+        c.to(table.at[c.g], table.at[c.g], c.at(g=(c.g + o) % c.ng), slot).start()
+    for o, slot in copies:
+        frm = (c.g + c.ng - o) % c.ng
+        c.to(table.at[frm], table.at[frm], c.at(g=frm), slot).wait_recv()
+    for o, slot in copies:
+        c.to(table.at[c.g], table.at[c.g], c.at(g=(c.g + o) % c.ng), slot).wait_send()
+
+
+def entering(c, prod, last, width, reverse):
+    rows = [None] * (2 * TP)
+    spots = [(t, g) for t in range(TP) for g in range(c.ng)]
+    for s in range(2):
+        cur = jnp.zeros((1, width), F32)
+        for t, g in (spots[::-1] if reverse else spots):
+            b = s * TP + t
+            old = rows[b]
+            rows[b] = cur if old is None else jnp.where(c.g == g, cur, old)
+            cur = last(g)[b:b + 1] + prod(g)[b:b + 1] * cur
+    return jnp.concatenate(rows, axis=0)
+
+
+def mix_fwd_kernel(br0, ci, gb, chan, db, mixed, conv, gates, state, rim, carry, table, a_ref, d_ref, ext, rim_in, send, recv):
+    c = Comm(send, recv)
+    greet(plane_partners(c))
+    n, width = ci.shape[1], ci.shape[2]
+    rslot = c.slot()
+    out = c.to(ci.at[:, pl.ds(n - 16, 16)], rim_in, c.at(g=(c.g + 1) % c.ng), rslot)
+    out.start()
+    out.wait()
+    row = lax.broadcasted_iota(jnp.int32, (n, 1), 0)
+    for b in range(2 * TP):
+        t = b % TP
+        same = rim_in[b].astype(F32)[8:]
+        prev = jnp.zeros_like(same) if t == 0 else rim_in[b - 1].astype(F32)[8:]
+        head = jnp.where(c.g == 0, prev, same)
+        rim[b] = head
+        ext[b % 2, pl.ds(0, 8), :] = head
+        ext[b % 2, pl.ds(8, n), :] = ci[b].astype(F32)
+        cv = chan[4:5] + chan[0:1] * ext[b % 2, pl.ds(8, n), :] + chan[1:2] * ext[b % 2, pl.ds(7, n), :]
+        cv = cv + chan[2:3] * ext[b % 2, pl.ds(6, n), :] + chan[3:4] * ext[b % 2, pl.ds(5, n), :]
+        low = cv.astype(BF)
+        rows = pl.ds(b * n, n)
+        conv[rows, :] = low
+        cv = low.astype(F32)
+        gv = []
+        for k in range(2):
+            pre = jnp.concatenate([jnp.dot(low[:, h * 256:(h + 1) * 256], gb[k, h], preferred_element_type=F32) for h in range(2)], axis=1)
+            v = jax.nn.sigmoid(pre + chan[5 + k:6 + k])
+            gates[k, rows, :] = v
+            gv.append(v)
+        decay, mult = decay_terms(gv[1], db[...])
+        if t == 0:
+            mult = jnp.where((row == 0) & (c.g == 0), 1.0, mult)
+        lanes_in(a_ref, rows, decay)
+        lanes_in(d_ref, rows, cv * gv[0] * mult)
+
+    def step1(r, ph):
+        at = pl.ds(r, 2 * TP, stride=n)
+        return [(p * av, h * av + dv) for (p, h), av, dv in zip(ph, each(a_ref, at), each(d_ref, at))]
+
+    one = jnp.ones((2 * TP, 128), F32)
+    ph = lax.fori_loop(0, n, step1, [(one, 0.0 * one)] * (width // 128), unroll=8)
+    p = jnp.concatenate([v[0] for v in ph], axis=1)
+    h = jnp.concatenate([v[1] for v in ph], axis=1)
+    table[c.g, 0] = p
+    table[c.g, 1] = h
+    share(c, table)
+    cin = entering(c, lambda g: table[g, 0], lambda g: table[g, 1], width, False)
+    carry[...] = cin
+
+    def step2(r, hs):
+        at = pl.ds(r, 2 * TP, stride=n)
+        hs = [h * av + dv for h, av, dv in zip(hs, each(a_ref, at), each(d_ref, at))]
+        for q, h in enumerate(hs):
+            d_ref[q, at, :] = h
+        return hs
+
+    lax.fori_loop(0, n, step2, split(cin), unroll=8)
+    for b in range(2 * TP):
+        rows = pl.ds(b * n, n)
+        v = lanes_out(d_ref, rows)
+        state[rows, :] = v
+        mixed[rows, :] = (v * gelu_pair(br0[rows, :])[0]).astype(BF)
+
+
+def mix_fwd_call(br0, ci, gb, chan, db):
+    ng = lax.axis_size("dp") // TP
+    rows, width = br0.shape
+    n = rows // (2 * TP)
+    S = jax.ShapeDtypeStruct
+    return call(
+        mix_fwd_kernel,
+        (S((rows, width), BF), S((rows, width), BF), S((2, rows, width), F32), S((rows, width), F32),
+         S((2 * TP, 8, width), F32), S((2 * TP, width), F32), S((ng, 2, 2 * TP, width), F32)),
+        [VM] * 5,
+        (VM,) * 7,
+        [pltpu.VMEM((width // 128, rows, 128), F32), pltpu.VMEM((width // 128, rows, 128), F32), pltpu.VMEM((2, n + 8, width), F32), pltpu.VMEM((2 * TP, 16, width), BF)],
+        5, 32,
+    )(br0, ci.reshape(2 * TP, n, width), gb, chan, db[None])
+
+
+def mix_bwd_kernel(gm, br0, ci, gb, chan, db, conv, gates, state, rim, carry, table, gbr, ggb, sums,
+                   a_ref, adj, gc, gpl, ext, heads, etab, rim_in, send, recv):
+    c = Comm(send, recv)
+    greet(plane_partners(c))
+    n, width = ci.shape[1], ci.shape[2]
+    for b in range(2 * TP):
+        rows = pl.ds(b * n, n)
+        act, slope = gelu_pair(br0[rows, :])
+        g = gm[rows, :]
+        lanes_in(adj, rows, g * act)
+        gbr[0, rows, :] = (g * state[rows, :] * slope).astype(BF)
+        lanes_in(a_ref, rows, jnp.exp(-8.0 * gates[1, rows, :] * db[...]))
+
+    def step1(i, es):
+        at = pl.ds(n - 1 - i, 2 * TP, stride=n)
+        return [(v + e) * av for v, e, av in zip(each(adj, at), es, each(a_ref, at))]
+
+    e = lax.fori_loop(0, n, step1, [jnp.zeros((2 * TP, 128), F32)] * (width // 128), unroll=8)
+    e = jnp.concatenate(e, axis=1)
+    etab[c.g] = e
+    share(c, etab)
+    ein = entering(c, lambda g: table[g, 0], lambda g: etab[g], width, True)
+
+    def step2(i, es):
+        at = pl.ds(n - 1 - i, 2 * TP, stride=n)
+        vs = [v + e for v, e in zip(each(adj, at), es)]
+        for q, v in enumerate(vs):
+            adj[q, at, :] = v
+        return [v * av for v, av in zip(vs, each(a_ref, at))]
+
+    lax.fori_loop(0, n, step2, split(ein), unroll=8)
+    row = lax.broadcasted_iota(jnp.int32, (n, 1), 0)
+    total = [jnp.zeros((1, width), F32) for _ in range(8)]
+    for b in range(2 * TP):
+        rows = pl.ds(b * n, n)
+        first = (row == 0) & (c.g == 0) if b % TP == 0 else None
+        ad = lanes_out(adj, rows)
+        gx, ga = gates[0, rows, :], gates[1, rows, :]
+        decay, root = decay_terms(ga, db[...])
+        mult = root if first is None else jnp.where(first, 1.0, root)
+        cv = conv[rows, :].astype(F32)
+        before = jnp.where(row == 0, carry[b:b + 1, :], pltpu.roll(state[rows, :], 1, 0))
+        gmult = -(ad * cv * gx) * (decay * decay) / root
+        if first is not None:
+            gmult = jnp.where(first, 0.0, gmult)
+        glog = ad * before * decay + gmult
+        total[7] = total[7] + jnp.sum(glog * (-8.0 * ga), axis=0, keepdims=True)
+        pre = [ad * cv * mult * gx * (1.0 - gx), glog * (-8.0 * db[...]) * ga * (1.0 - ga)]
+        conved = ad * gx * mult
+        for k in range(2):
+            total[5 + k] = total[5 + k] + jnp.sum(pre[k], axis=0, keepdims=True)
+            low = pre[k].astype(BF)
+            gpl[k, rows, :] = low
+            conved = conved + jnp.concatenate([
+                lax.dot_general(low[:, h * 256:(h + 1) * 256], gb[k, h], (((1,), (1,)), ((), ())), preferred_element_type=F32)
+                for h in range(2)], axis=1)
+        gc[b, pl.ds(0, n), :] = conved
+        heads[b] = conved[:8]
+        ext[b % 2, pl.ds(0, 8), :] = rim[b]
+        ext[b % 2, pl.ds(8, n), :] = ci[b].astype(F32)
+        for k in range(4):
+            total[k] = total[k] + jnp.sum(conved * ext[b % 2, pl.ds(8 - k, n), :], axis=0, keepdims=True)
+        total[4] = total[4] + jnp.sum(conved, axis=0, keepdims=True)
+    rslot = c.slot()
+    out = c.to(heads, rim_in, c.at(g=(c.g + c.ng - 1) % c.ng), rslot)
+    out.start()
+    sums[...] = jnp.concatenate(total, axis=0)
+    for k in range(2):
+        for h in range(2):
+            ggb[k, h] = lax.dot_general(conv[:, h * 256:(h + 1) * 256], gpl[k, :, h * 256:(h + 1) * 256], (((0,), (0,)), ((), ())), preferred_element_type=F32)
+    out.wait()
+    for b in range(2 * TP):
+        rows = pl.ds(b * n, n)
+        same = rim_in[b]
+        nxt = jnp.zeros_like(same) if b % TP == TP - 1 else rim_in[b + 1]
+        gc[b, pl.ds(n, 8), :] = jnp.where(c.g == c.ng - 1, nxt, same)
+        v = chan[0:1] * gc[b, pl.ds(0, n), :]
+        for k in range(1, 4):
+            v = v + chan[k:k + 1] * gc[b, pl.ds(k, n), :]
+        gbr[1, rows, :] = v.astype(BF)
+
+
+def mix_bwd_call(gm, br0, ci, gb, chan, db, saved):
+    ng = lax.axis_size("dp") // TP
+    rows, width = br0.shape
+    n = rows // (2 * TP)
+    S = jax.ShapeDtypeStruct
+    V = pltpu.VMEM
+    return call(
+        mix_bwd_kernel,
+        (S((2, rows, width), BF), S((2, 2, 256, 256), F32), S((8, width), F32)),
+        [VM] * 12,
+        (VM,) * 3,
+        [V((width // 128, rows, 128), F32), V((width // 128, rows, 128), F32), V((2 * TP, n + 8, width), F32), V((2, rows, width), BF),
+         V((2, n + 8, width), F32), V((2 * TP, 8, width), F32), V((ng, 2 * TP, width), F32), V((2 * TP, 8, width), F32)],
+        6, 32,
+    )(gm, br0, ci.reshape(2 * TP, n, width), gb, chan, db[None], *saved)
 
 
 def dot(a, b, ca, cb):
@@ -702,8 +868,6 @@
     decay_base = jax.nn.softplus(dpar)
     pos = dp * 2 * rows + mp * rows + jnp.arange(rows, dtype=jnp.int32)
     valid = (pos[None] < lengths[:, None])[..., None]
-    blk = jnp.arange(8) % TP * ng + g
-    at_start = ((blk[:, None] * 2 * rows + jnp.arange(2 * rows)[None]) == 0)[..., None]
     x = block_input
     grad_own = jnp.where(valid, out_grad, jnp.zeros_like(out_grad))
     mlp = jnp.concatenate([w_mlp, w_down.T[None]], 0).reshape(3, r, TP, fs).transpose(2, 0, 1, 3)
@@ -714,7 +878,7 @@
     wd = wm[2]
     branch0 = dot(na, wb[0], 1, 0)
     conv_input = dot(na, wb[1], 1, 0).astype(BF)
-    mixed, saved = mixer_forward(branch0, conv_input, gb, chan, decay_base, at_start)
+    mixed, *saved = mix_fwd_call(branch0, conv_input, gb, chan, decay_base)
     residual, nb = mid_call(dot(mixed, wo, 1, 1).astype(BF), x, norm_gains[1])
     nb = nb.reshape(-1, width)
     first, second = dot(nb, wm[0], 1, 0), dot(nb, wm[1], 1, 0)
@@ -730,14 +894,14 @@
     out = jnp.where(valid, residual + mlp_own, 0.0).astype(BF)
     gmo = gmo.reshape(-1, width)
     gwo = dot(gmo, mixed, 0, 0).astype(BF)
-    gbr, ggb, chan_rows = mixer_backward(dot(gmo, wo, 1, 0), branch0, saved, gb, chan, decay_base, at_start)
+    gbr, ggb, chan_rows = mix_bwd_call(dot(gmo, wo, 1, 0), branch0, conv_input, gb, chan, decay_base, saved)
     gwb = [dot(na, gbr[k], 0, 0).astype(BF) for k in range(2)]
     gna = (dot(gbr[0], wb[0], 1, 1) + dot(gbr[1], wb[1], 1, 1)).astype(BF)
     gr = gate_blocks.shape[2]
-    gin, gain_a, owb, owo, ogb, owm = end_call(
+    gin, gains, table, owb, owo, ogb, owm = end_call(
         gna, x, gres, norm_gains[0],
         jnp.stack(gwb).reshape(2, TP, ng, r, 512), gwo.reshape(TP, ng, r, 512),
-        ggb.astype(BF).reshape(2, 2, TP, ng, gr, 256), jnp.stack(gwm + [gwd]).reshape(3, TP, ng, r, fs),
+        ggb.astype(BF).reshape(2, 2, TP, ng, gr, 256), jnp.stack(gwm + [gwd]).reshape(3, TP, ng, r, fs), gain_b, chan_rows,
     )
     owb, owo = owb.astype(F32), owo.astype(F32)
     g_wb = jnp.concatenate([owb[:, i, :, :256] for i in range(TP)] + [owb[:, 1, :, 256:]], -1)
@@ -745,10 +909,8 @@
     g_gb = jnp.concatenate([ogb[:, 0], ogb[:, 1, 1:2]], 1).astype(F32)
     g_wm = owm[:2].transpose(0, 2, 1, 3).reshape(2, r, TP * fs).astype(F32)
     g_wd = owm[2].transpose(0, 2, 1).reshape(TP * fs, r).astype(F32)
-    gains = lax.psum(jnp.concatenate([gain_a, gain_b]), ("dp", "mp"))
-    chan_rows = lax.psum(chan_rows, "dp", axis_index_groups=g_groups())
-    crow = heads_back(chan_rows, 1)
-    return out, gin, gains, g_wb, crow[:7], g_gb, crow[7] * jax.nn.sigmoid(decay_param), g_wo, g_wm, g_wd
+    crow = jnp.concatenate([table[i, :, :256] for i in range(TP)] + [table[1, :, 256:]], -1)
+    return out, gin, gains[:2], g_wb, crow[:7], g_gb, crow[7] * jax.nn.sigmoid(decay_param), g_wo, g_wm, g_wd
 
 
 def solution(mesh):

time: 1670 us -> 1150 us (0.69)
  local copies, waits for them, and re-layouts: 402 us -> 73.6 us
  other arithmetic: 171 us -> 31.6 us
  blocking collectives: 117 us -> 0 us
  Pallas kernels: 812 us -> 893 us
    pad x48 -> x0, local copies, waits for them, and re-layouts: 141 us -> none  [the longest x24 75.3 us: mixer_backward(): lax.associative_scan(combine_pair, (rate_next, gs), reverse=True, axis=1)]
    slice x100 -> x1, local copies, waits for them, and re-layouts: 118 us -> 1.57 us  [body(): gains[:2]]
    pallas_call x1 -> x3, Pallas kernels: 287 us -> 367 us  [the longest x1 303 us: end_call(): call(end_kernel, (S((2, n, d), F32), S((8, d), F32), S((TP, 8, 512), F32)...]
    all_gather x7 -> x0, blocking collectives: 61.6 us -> none  [the longest x6 48.3 us: gather_g(): return lax.all_gather(x, 'dp', axis=0, axis_index_groups=g_groups())]
    add x38 -> x0, other arithmetic: 56.1 us -> none  [the longest x14 21.5 us: mixer_backward(): lax.associative_scan(combine_pair, (rate_next, gs), reverse=True, axis=1)]
    psum x2 -> x0, blocking collectives: 55.8 us -> none  [the longest x1 38.8 us: body(): gains = lax.psum(jnp.concatenate([gain_a, gain_b]), ('dp', 'mp'))]
    rev x2 -> x0, local copies, waits for them, and re-layouts: 33.4 us -> none  [mixer_backward(): lax.associative_scan(combine_pair, (rate_next, gs), reverse=True, axis=1)]
    mul x18 -> x0, other arithmetic: 33.3 us -> none  [the longest x12 22.8 us: combine_pair(): return (earlier[0] * later[0], later[0] * earlier[1] + later[1])]
where the time goes in v2:
time: 1150 us; the launch traced here: 1140 us
  Pallas kernels  893 us (78%)
  matrix products  138 us (12%)
  local copies, waits for them, and re-layouts  73.6 us (6%)
  other arithmetic  31.6 us (3%)
    pallas_call x1, Pallas kernels, end_call(): call(end_kernel, (S((2, n, d), F32), S((8, d), F32), S((TP, 8, 512), F32)...  303 us
    pallas_call x1, Pallas kernels, start_call(): call(start_kernel, (S((2, TP, 2, n, d), BF), S((2, TP, 2, n, d), BF), S((...  300 us
    dot_general x18, matrix products, dot(): lax.dot_general(a, b, (((ca,), (cb,)), ((), ())), preferred_element_type=...  138 us
    pallas_call x1, Pallas kernels, back_call(): call(back_kernel, (S((2, n, d), F32), S((1, d), F32), S((2, n, d), F32),...  119 us
    pallas_call x1, Pallas kernels, mid_call(): call(mid_kernel, (S((2, n, d), F32), S((2, TP, 2, n, d), BF)), [VM, VM, V...  107 us
    pallas_call x1, Pallas kernels, mix_bwd_call(): call(mix_bwd_kernel, (S((2, rows, width), BF), S((2, 2, 256, 256), F32),...  35.6 us
    pallas_call x1, Pallas kernels, mix_fwd_call(): call(mix_fwd_kernel, (S((rows, width), BF), S((rows, width), BF), S((2, r...  28.6 us

profile of v2, /device:TPU:0, one launch (start us, length us, event | category | flops | bytes accessed | tf_op | source)
XLA Modules:
  0.0 1138.0 jit_solution(11753015131518819595)
XLA Ops:
  1.4 2.0 broadcast_select_fusion.go
  3.4 1.4 fusion.28
  4.8 3.7 concatenate.55
  8.6 1.4 copy.30
  10.0 6.3 concatenate.54
  17.7 2.3 maximum_bitcast_fusion.mlp
  20.0 299.8 %shard_map.186 = (bf16[2,4,2,64,2560]{4,3,2,1,0:T(8,128)(2,1)}, bf16[2,4,2,64,2560]{4,3,2,1,0:T(8,128)(2,1)}, bf16[2,4,4,160,512]{4,3,2,1,0:T(8,128)(2,1)}, bf16...) custom-call(bf16[2,64,2560]{2,1,0:T(8,128)(2,1)} %x.5, ...), custom_call_target="tpu_custom_call" | custom-call | tf_op jit(solution)/shard_map/pallas_call | solution.py:433
  319.8 3.1 fusion.27
  322.9 0.9 copy-done.14
  323.8 4.2 fusion.29.br0
  328.0 3.8 convolution_convert_fusion.8
  333.9 28.6 %shard_map.187 = (bf16[1024,512]{1,0:T(8,128)(2,1)}, bf16[1024,512]{1,0:T(8,128)(2,1)}, f32[2,1024,512]{2,1,0:T(8,128)}, f32[1024,512]{1,0:T(8,128)}, f32[8,8,51...) custom-call(f32[1024,512]{1,0:T(8,128)} %fusion.29.br0, bf16[8,128,512]{2,1,0:T(8,128)(2,1)} %bitcast.158, ...), custom_call_target="tpu_custom_call" | custom-call | tf_op jit(solution)/shard_map/pallas_call | solution.py:742
  362.5 7.4 convolution_convert_fusion
  369.8 107.3 %shard_map.188 = (f32[2,64,2560]{2,1,0:T(8,128)}, bf16[2,4,2,64,2560]{4,3,2,1,0:T(8,128)(2,1)}) custom-call(bf16[2,4,2,64,2560]{4,3,2,1,0:T(8,128)(2,1)} %bitcast.151, bf16[2,64,2560]{2,1,0:T(8,128)(2,1)} %x.5, f32[1,2560]{1,0:T(1,128)} %get-tuple-element.78.gain), custom_call_target="tpu_custom_call" | custom-call | tf_op jit(solution)/shard_map/pallas_call | solution.py:458
  477.1 7.5 fusion.26
  484.6 10.4 fusion.31
  495.1 7.2 fusion.30
  502.2 14.3 %multiply_convert_fusion = (bf16[1024,960]{0,1:T(8,128)(2,1)}, bf16[1024,960]{0,1:T(8,128)(2,1)}, bf16[1024,960]{0,1:T(8,128)(2,1)}) fusion(f32[1024,960]{0,1:T(8,128)} %fusion.31, f32[1024,960]{0,1:T(8,128)} %fusion.30, bf16[1024,2560]{1,0:T(8,128)(2,1)} %bitcast.188, bf16[2560,960]{1,0:T(8,128)(2,1)S(1)} %bitcast.154), kind=kOutput, calls=%fused_computation.23 | convolution fusion | flops 5058723840 | bytes 23920640 | tf_op jit(solution)/shard_map/dot_general | solution.py:853
  516.5 11.2 fusion.32
  527.7 10.1 add_convert_fusion.1
  537.8 9.5 convolution_convert_fusion.1
  547.3 118.6 %shard_map.189 = (f32[2,64,2560]{2,1,0:T(8,128)}, f32[1,2560]{1,0:T(1,128)}, f32[2,64,2560]{2,1,0:T(8,128)}, bf16[2,4,2,64,2560]{4,3,2,1,0:T(8,128)(2,1)}) custom-call(bf16[2,4,2,64,2560]{4,3,2,1,0:T(8,128)(2,1)} %bitcast.149, bf16[2,4,2,64,2560]{4,3,2,1,0:T(8,128)(2,1)} %bitcast.150, f32[2,64,2560]{2,1,0:T(8,128)} %get-tuple-element.44.res, ...), custom_call_target="tpu_custom_call" | custom-call | tf_op jit(solution)/shard_map/pallas_call | solution.py:491
  665.9 2.3 select_convert_fusion
  668.2 7.5 fusion.33.gm
  675.7 35.6 %shard_map.190 = (bf16[2,1024,512]{2,1,0:T(8,128)(2,1)}, f32[2,2,256,256]{3,2,1,0:T(8,128)}, f32[8,512]{1,0:T(8,128)}) custom-call(f32[1024,512]{1,0:T(8,128)} %fusion.33.gm, f32[1024,512]{1,0:T(8,128)} %fusion.29.br0, bf16[8,128,512]{2,1,0:T(8,128)(2,1)} %bitcast.159, bf16[2,2,256,256]{3,2,1,0:T(8,128)(2,1)} %bitcast.169, f32[7,512]{1,0:T(8,128)} %pad_maximum_fusion.2.chan, ...), custom_call_target="tpu_custom_call" | custom-call | tf_op jit(solution)/shard_map/pallas_call | solution.py:841
  711.4 9.1 fusion.10
  720.5 7.6 add_convert_fusion
  728.1 3.2 convolution_convert_fusion.6
  731.3 3.2 convolution_convert_fusion.7
  734.5 2.8 pad_maximum_fusion.1.gwb
  737.3 4.2 convolution_convert_fusion.5
  742.4 6.9 convolution_convert_fusion.2
  749.3 8.0 copy.33
  757.3 9.4 convolution_convert_fusion.3
  766.7 8.0 copy.32
  774.7 9.4 convolution_convert_fusion.4
  784.0 7.8 copy.31
  791.9 13.3 %pad_maximum_fusion.gwm = bf16[3,4,4,160,960]{4,3,2,1,0:T(8,128)(2,1)} fusion(bf16[1,4,4,160,960]{4,3,2,1,0:T(8,128)(2,1)} %bitcast.145, bf16[1,4,4,160,960]{4,3,2,1,0:T(8,128)(2,1)} %bitcast.146, bf16[1,4,4,160,960]{4,3,2,1,0:T(8,128)(2,1)} %bitcast.147), kind=kLoop, calls=%fused_computation | loop fusion | flops 14745600 | bytes 29491200 | tf_op jit(solution)/shard_map/stack | solution.py:904
  805.2 303.2 %shard_map.191 = (f32[2,64,2560]{2,1,0:T(8,128)}, f32[8,2560]{1,0:T(8,128)}, f32[4,8,512]{2,1,0:T(8,128)}, bf16[2,4,160,512]{3,2,1,0:T(8,128)(2,1)}, bf16[4,160,...) custom-call(bf16[2,4,2,64,2560]{4,3,2,1,0:T(8,128)(2,1)} %bitcast.148, ...), custom_call_target="tpu_custom_call" | custom-call | tf_op jit(solution)/shard_map/pallas_call | solution.py:582
  1108.4 1.6 slice.115
  1110.0 1.7 convert_element_type.94
  1111.9 1.1 copy-done.7
  1115.5 5.7 copy.39
  1121.2 7.4 reshape.250
  1128.6 1.6 convert_bitcast_fusion.1
  1130.2 1.7 copy.40
  1131.9 3.4 reshape.251
  1135.4 2.5 copy.58
  (92 shorter events, 7.6 us)
Async XLA Ops:
  16.4 1.3 copy-start.1
  319.8 4.1 copy-start.14
  322.9 5.1 copy-start.4
  328.0 5.2 copy-start.9
  477.1 18.0 %slice-start = ((s8[5242880]{0:T(1024)(128)(4,1)}), s8[4194304]{0:T(1024)(128)(4,1)S(1)}, s32[]{:S(2)}) async-start(s8[5242880]{0:T(1024)(128)(4,1)} %bitcast.175), calls=%async_computation | async-start | bytes 8388608
  484.6 10.5 copy-start.2
  484.6 10.4 slice-start.1
  516.5 11.2 copy-start.17
  547.3 118.6 %copy-start = (f32[2,64,2560]{2,1,0:T(8,128)S(1)}, f32[2,64,2560]{2,1,0:T(8,128)}, u32[]{:S(2)}) copy-start(f32[2,64,2560]{2,1,0:T(8,128)} %get-tuple-element.44.res) | copy-start | bytes 3932164
  711.4 9.2 copy-start.15
  711.4 16.7 %slice-start.4 = ((s8[5242880]{0:T(1024)(128)(4,1)}), s8[4194304]{0:T(1024)(128)(4,1)S(1)}, s32[]{:S(2)}) async-start(s8[5242880]{0:T(1024)(128)(4,1)} %bitcast.183), calls=%async_computation.4 | async-start | bytes 8388608
  720.5 7.6 slice-start.5
  728.1 9.2 slice-start.6
  731.3 6.0 slice-start.7
  734.5 2.8 copy-start.16
  734.5 7.9 slice-start.2
  737.3 4.3 copy-start.5
  737.3 5.1 slice-start.3
  737.3 5.1 copy-start.20
  749.3 8.0 copy-start.18
  766.7 8.0 copy-start.19
  1108.4 3.5 copy-start.12
  1108.4 4.6 copy-start.8
  1108.4 5.3 copy-start.10
  1108.4 5.9 copy-start.6
  1111.6 3.0 copy-start.3
  1111.8 1.2 copy-start.7
  1111.9 3.4 copy-start.13
  1114.6 0.9 copy-start.11

commit v3 on v2

--- a/solution.py
+++ b/solution.py
@@ -140,7 +140,7 @@
     return [
         pltpu.VMEM((2, TP, rows, width), BF),
         pltpu.VMEM((2, TP - 1, 2, rows, width), BF),
-        pltpu.VMEM((2, TP - 1, 2, rows, width), BF),
+        pltpu.VMEM((TP - 1, 2, rows, width), BF),
     ]
 
 
@@ -166,7 +166,7 @@
     def msg(flow, j):
         way = da if flow == 0 else 1 - da
         dev = c.at(t=t + step if flow == 0 else t - step)
-        return c.to(outbox.at[way, j], inbox.at[way, j], dev, base + way * (TP - 1) + j)
+        return c.to(outbox.at[j if flow == 0 else 2], inbox.at[way, j], dev, base + way * (TP - 1) + j)
 
     def add(d, into, terms):
         b = real(d)
@@ -182,9 +182,9 @@
 
         lax.fori_loop(0, n // 16, rows16, 0)
 
-    def put(way, j):
+    def put(j):
         def into(s, sl, v):
-            outbox[way, j, s, sl, :] = v.astype(BF)
+            outbox[j, s, sl, :] = v.astype(BF)
         return into
 
     def final(s, sl, v):
@@ -199,7 +199,7 @@
             def go():
                 if lvl == 1:
                     msg(0, j).wait_recv()
-                add(d, put(da, j), [(da, j)] if lvl else [])
+                add(d, put(j), [(da, j)] if lvl else [])
                 msg(0, j).start()
             pl.when(u == lvl)(go)
         yield
@@ -207,14 +207,14 @@
     cross(1).wait_recv()
 
     def first():
-        add(1, put(da, 2), [])
+        add(1, put(2), [])
         msg(0, 2).start()
 
     pl.when(u == 0)(first)
 
     def back():
         msg(1, 0).wait_recv()
-        add(0, put(1 - da, 0), [(1 - da, 0)])
+        add(0, put(2), [(1 - da, 0)])
         msg(1, 0).start()
 
     pl.when(u == 1)(back)
@@ -239,41 +239,63 @@
     pl.when(u == 1)(lambda: msg(1, 0).wait_send())
 
 
-def spread_z(c, src, dst, need=None):
+def inner(t):
+    return (t == 1) | (t == 2)
+
+
+def outer(t):
+    return (t == 0) | (t == TP - 1)
+
+
+def fifth(t):
+    return t == 1
+
+
+def cut(width, t):
+    tiles = width // 128
+    big = -(-tiles // TP)
+    small = (tiles - 2 * big) // 2
+    return pl.multiple_of((small * t + (big - small) * (t > 1) * (t - 1)) * 128, 128), big * 128, small * 128
+
+
+def spread_z(c, src, dst, kinds=((None, 0),), owner="to"):
     slots = [c.slot() for _ in range(TP)]
 
-    def copy(o):
+    def each_kind(sender, taker, f):
+        own = taker if owner == "to" else sender
+        for which, k in kinds:
+            if which is None:
+                f(k)
+            else:
+                pl.when(which(own))(functools.partial(f, k))
+
+    def copy(o, k):
         to = (c.t + o) % TP
-        return c.to(src(to), dst(c.t), c.at(t=to), slots[o])
-
-    def mine():
-        return c.local(src(c.t), dst(c.t), slots[0])
-
-    def back(o):
+        return c.to(src(to, k), dst(c.t, k), c.at(t=to), slots[o])
+
+    def back(o, k):
         frm = (c.t + TP - o) % TP
-        return c.to(src(frm), dst(frm), c.at(t=frm), slots[o])
-
-    def when(t, f):
-        if need is None:
-            f()
-        else:
-            pl.when(t == need)(f)
+        return c.to(dst(frm, k), dst(frm, k), c.at(t=frm), slots[o])
 
     for o in range(1, TP):
-        when((c.t + o) % TP, lambda: copy(o).start())
-    when(c.t, lambda: mine().start())
+        each_kind(c.t, (c.t + o) % TP, lambda k: copy(o, k).start())
+    each_kind(c.t, c.t, lambda k: c.local(src(c.t, k), dst(c.t, k), slots[0]).start())
     yield
-    when(c.t, lambda: mine().wait())
+    each_kind(c.t, c.t, lambda k: c.local(src(c.t, k), dst(c.t, k), slots[0]).wait())
     for o in range(1, TP):
-        when(c.t, lambda: back(o).wait_recv())
+        each_kind((c.t + TP - o) % TP, c.t, lambda k: back(o, k).wait_recv())
     yield
     for o in range(1, TP):
-        when((c.t + o) % TP, lambda: copy(o).wait_send())
-
-
-def plane_gather(c, block, order):
+        each_kind(c.t, (c.t + o) % TP, lambda k: copy(o, k).wait_send())
+
+
+def plane_gather(c, block, order, own=None):
     have = [0]
     done = []
+    held = None
+    if own is not None:
+        held = c.local(own, block(c.g), c.slot())
+        held.start()
     for b in order:
         dev = c.at(g=c.flip(c.g, b))
         sent = []
@@ -282,7 +304,8 @@
             for bit in c.bits:
                 if x & bit:
                     gg = c.flip(gg, bit)
-            copy = c.to(block(gg), block(gg), dev, c.slot())
+            src = own if own is not None and x == 0 else block(gg)
+            copy = c.to(src, block(gg), dev, c.slot())
             copy.start()
             sent.append(copy)
         yield
@@ -292,6 +315,8 @@
         have = have + [x ^ b for x in have]
     for copy in done:
         copy.wait_send()
+    if held is not None:
+        held.wait()
 
 
 def plane_reduce(c, own, sums, inbox, order):
@@ -357,40 +382,75 @@
 VM = pl.BlockSpec(memory_space=pltpu.VMEM)
 
 
-def start_kernel(x, go, gain, wbr, wot, gates, mlp, full_a, full_g, wb, wo, gb, wm, own, zero, send, recv):
+def heads_to(ref, dst, extra):
+    def src(t, k):
+        return ref.at[:, pl.ds(1024, 256)] if extra else ref.at[:, pl.ds(pl.multiple_of(t * 256, 256), 256)]
+
+    def into(t, k):
+        return dst(t).at[:, pl.ds(256 if extra else 0, 256)]
+
+    return src, into, (((fifth, 0),) if extra else ((None, 0),))
+
+
+def units_to(ref, dst):
+    width = ref.shape[1]
+    _, big, small = cut(width, 0)
+
+    def src(t, k):
+        return ref.at[:, pl.ds(cut(width, t)[0], k)]
+
+    def into(t, k):
+        return dst(t).at[:, pl.ds(0, k)]
+
+    return src, into, ((inner, big), (outer, small))
+
+
+def units_back(ref, dst):
+    width = dst.shape[1]
+    _, big, small = cut(width, 0)
+
+    def src(t, k):
+        return ref(t).at[:, pl.ds(0, k)]
+
+    def into(t, k):
+        return dst.at[:, pl.ds(cut(width, t)[0], k)]
+
+    return src, into, ((inner, big), (outer, small)), "from"
+
+
+def heads_out(ref, dst, extra):
+    def src(t, k):
+        return ref(t).at[:, pl.ds(256 if extra else 0, 256)]
+
+    def into(t, k):
+        return dst.at[:, pl.ds(1024, 256)] if extra else dst.at[:, pl.ds(pl.multiple_of(t * 256, 256), 256)]
+
+    return src, into, (((fifth, 0),) if extra else ((None, 0),)), "from"
+
+
+def start_kernel(x, gain, wbr, wot, gates, full_a, wb0, wb1, wop, gb, own, zero, send, recv):
     c = Comm(send, recv)
     c.barrier()
-    r = wbr.shape[1]
-
-    def head(ref, lead):
-        def src(t):
-            lane = pl.multiple_of(t * 256, 256)
-            return ref.at[(*lead, slice(None), pl.ds(lane, 256))]
-        return src
-
-    pieces = []
-    for k in range(2):
-        pieces.append((head(wbr, (k,)), wb, (k,), wbr.at[k, :, pl.ds(1024, 256)]))
-    pieces.append((head(wot, ()), wo, (), wot.at[:, pl.ds(1024, 256)]))
+    wb = (wb0, wb1)
     z = []
-    for src, dst, lead, extra in pieces:
-        z.append(spread_z(c, src, lambda t, dst=dst, lead=lead: dst.at[(*lead, t, c.g, slice(None), pl.ds(0, 256))]))
-        z.append(spread_z(c, lambda t, extra=extra: extra, lambda t, dst=dst, lead=lead: dst.at[(*lead, t, c.g, slice(None), pl.ds(256, 256))], 1))
-    z.append(spread_z(c, lambda t: gates.at[:, t], lambda t: gb.at[:, 0, t, c.g]))
-    z.append(spread_z(c, lambda t: gates.at[:, 4], lambda t: gb.at[:, 1, t, c.g], 1))
+    for extra in (False, True):
+        for k in range(2):
+            z.append(spread_z(c, *heads_to(wbr.at[k], lambda t, k=k: wb[k].at[t, c.g], extra)))
+    z.append(spread_z(c, lambda t, k: gates.at[:, t], lambda t, k: gb.at[:, 0, t, c.g]))
+    z.append(spread_z(c, lambda t, k: gates.at[:, 4], lambda t, k: gb.at[:, 1, t, c.g], ((fifth, 0),)))
     for f in z:
         next(f)
-    x32 = [x[s].astype(F32) for s in range(2)]
     for s in range(2):
-        v = x32[s] * lax.rsqrt(jnp.mean(x32[s] * x32[s], axis=-1, keepdims=True) + EPS) * gain[...]
-        own[s] = v.astype(BF)
+        v = x[s].astype(F32)
+        own[s] = (v * lax.rsqrt(jnp.mean(v * v, axis=-1, keepdims=True) + EPS) * gain[...]).astype(BF)
     ag = ag_flow(c, own, full_a)
     next(ag)
+    z2 = [spread_z(c, *heads_to(wot, lambda t: wop.at[t], extra)) for extra in (False, True)]
+    for f in z2:
+        next(f)
     zero[...] = jnp.zeros_like(zero)
-    fills = []
-    for k in range(2):
-        fills.append((zero, wb.at[k, :, c.g, :, pl.ds(256, 256)], c.slot()))
-    fills.append((zero, wo.at[:, c.g, :, pl.ds(256, 256)], c.slot()))
+    fills = [(zero, wb[k].at[:, c.g, :, pl.ds(256, 256)], c.slot()) for k in range(2)]
+    fills.append((zero, wop.at[:, :, pl.ds(256, 256)], c.slot()))
     for k in range(2):
         fills.append((zero.at[:, pl.ds(0, gates.shape[2])], gb.at[k, 1, :, c.g], c.slot()))
 
@@ -401,74 +461,107 @@
             c.local(*f).wait()
 
     pl.when(c.t != 1)(fill)
-    zm = [spread_z(c, lambda t, k=k: mlp.at[t, k], lambda t, k=k: wm.at[k, t, c.g]) for k in range(3)]
     for f in z:
         next(f)
     fwd, rev = c.bits, c.bits[::-1]
-    g1 = [plane_gather(c, lambda g: wb.at[0, :, g], fwd), plane_gather(c, lambda g: wb.at[1, :, g], rev),
-          plane_gather(c, lambda g: wo.at[pl.ds(0, 2), g], fwd), plane_gather(c, lambda g: wo.at[pl.ds(2, 2), g], rev),
+    g1 = [plane_gather(c, lambda g: wb0.at[:, g], fwd), plane_gather(c, lambda g: wb1.at[:, g], rev),
           plane_gather(c, lambda g: gb.at[0, :, :, g], fwd), plane_gather(c, lambda g: gb.at[1, :, :, g], rev)]
     for f in g1:
         next(f)
     next(ag)
-    ag2 = ag_flow(c, go, full_g)
-    for f in zm:
-        next(f)
-    for f in g1:
-        next(f)
-    run(ag)
-    next(ag2)
-    for f in zm:
-        next(f)
-    g2 = [plane_gather(c, lambda g: wm.at[0, :, g], fwd), plane_gather(c, lambda g: wm.at[1, :, g], rev),
-          plane_gather(c, lambda g: wm.at[2, pl.ds(0, 2), g], fwd), plane_gather(c, lambda g: wm.at[2, pl.ds(2, 2), g], rev)]
-    run(*z, *zm, *g1, *g2, ag2)
-
-
-def start_call(x, go, gain, wbr, wot, gates, mlp):
+    run(*g1, ag, *z, *z2)
+
+
+def start_call(x, gain, wbr, wot, gates):
     ng = lax.axis_size("dp") // TP
     _, n, d = x.shape
-    r, gr, fs = wbr.shape[1], gates.shape[2], mlp.shape[3]
+    r, gr = wbr.shape[1], gates.shape[2]
     S = jax.ShapeDtypeStruct
     return call(
         start_kernel,
-        (S((2, TP, 2, n, d), BF), S((2, TP, 2, n, d), BF), S((2, TP, ng, r, 512), BF), S((TP, ng, r, 512), BF),
-         S((2, 2, TP, ng, gr, 256), BF), S((3, TP, ng, r, fs), BF)),
-        [VM, VM, VM, HBM, HBM, HBM, HBM],
-        (HBM,) * 6,
+        (S((2, TP, 2, n, d), BF), S((TP, ng, r, 512), BF), S((TP, ng, r, 512), BF), S((TP, r, 512), BF), S((2, 2, TP, ng, gr, 256), BF)),
+        [VM, VM, HBM, HBM, HBM],
+        (HBM,) * 5,
         [pltpu.VMEM((2, n, d), BF), pltpu.VMEM((TP, r, 256), BF)],
         1,
-    )(x, go, gain[None], wbr, wot, gates, mlp)
-
-
-def mid_kernel(part, x, gain, res, full, tot, own, sib, inbox, outbox, send, recv):
+    )(x, gain[None], wbr, wot, gates)
+
+
+def mid_kernel(part, x, go, gain, p0, m1, m2, zero, res, full, full_g, w0, w1, w2, tot, own, sib, inbox, outbox, send, recv):
     c = Comm(send, recv)
     c.barrier()
-    run(rs_flow(c, part, tot, sib, inbox, outbox))
+    fwd, rev = c.bits, c.bits[::-1]
+    rs = rs_flow(c, part, tot, sib, inbox, outbox)
+    next(rs)
+    pad = zero.shape[2]
+    fills = [(zero, w.at[:, c.g, :, pl.ds(w.shape[3] - pad, pad)], c.slot()) for w in (w1, w2)]
+
+    def fill():
+        for f in fills:
+            c.local(*f).start()
+        for f in fills:
+            c.local(*f).wait()
+
+    g0 = plane_gather(c, lambda g: w0.at[:, g], fwd, p0)
+    next(g0)
+    z1 = spread_z(c, *units_to(m1, lambda t: w1.at[t, c.g]))
+    next(z1)
+    pl.when(outer(c.t))(fill)
+    z2 = spread_z(c, *units_to(m2, lambda t: w2.at[t, c.g]))
+    next(rs)
+    next(z2)
+    next(rs)
+    next(z1)
+    g1 = plane_gather(c, lambda g: w1.at[:, g], rev)
+    next(g1)
+    next(rs)
+    next(g0)
+    next(z2)
+    half = [plane_gather(c, lambda g: w2.at[pl.ds(0, 2), g], fwd), plane_gather(c, lambda g: w2.at[pl.ds(2, 2), g], rev)]
+    for f in half:
+        next(f)
+    run(rs)
     for s in range(2):
         v = x[s].astype(F32) + tot[s]
         res[s] = v
         own[s] = (v * lax.rsqrt(jnp.mean(v * v, axis=-1, keepdims=True) + EPS) * gain[...]).astype(BF)
-    run(ag_flow(c, own, full))
-
-
-def mid_call(part, x, gain):
+    ag = ag_flow(c, own, full)
+    next(ag)
+    ag2 = ag_flow(c, go, full_g)
+    next(ag2)
+    run(g1, ag, *half, ag2, g0, z1, z2)
+
+
+def mid_call(part, x, go, gain, p0, m1, m2):
     _, n, d = x.shape
+    ng = lax.axis_size("dp") // TP
+    _, r, fs = p0.shape
+    _, big, small = cut(m1.shape[1], 0)
+    zero = jnp.zeros((TP, r, big - small), BF)
     S = jax.ShapeDtypeStruct
+    w = S((TP, ng, r, fs), BF)
     return call(
         mid_kernel,
-        (S((2, n, d), F32), S((2, TP, 2, n, d), BF)),
-        [VM, VM, VM],
-        (VM, HBM),
+        (S((2, n, d), F32), S((2, TP, 2, n, d), BF), S((2, TP, 2, n, d), BF), w, w, w),
+        [VM, VM, VM, VM, HBM, HBM, HBM, VM],
+        (VM,) + (HBM,) * 5,
         [pltpu.VMEM((2, n, d), F32), pltpu.VMEM((2, n, d), BF)] + rs_scratch(n, d),
         2,
-    )(part.reshape(2, TP, 2, n, d), x, gain[None])
-
-
-def back_kernel(part, part2, res, go, gain, gres, gsum, mlp_own, full, tot, own, sib, inbox, outbox, sib2, inbox2, outbox2, send, recv):
+    )(part.reshape(2, TP, 2, n, d), x, go, gain[None], p0, m1, m2, zero)
+
+
+def back_kernel(part, part2, res, go, gain, h0, h1, h2, gres, gsum, mlp_own, full, o0, r1, r2,
+                tot, own, sib, inbox, outbox, sib2, inbox2, outbox2, su, ib, send, recv):
     c = Comm(send, recv)
     c.barrier()
-    run(rs_flow(c, part, tot, sib, inbox, outbox))
+    fwd, rev = c.bits, c.bits[::-1]
+    rs = rs_flow(c, part, tot, sib, inbox, outbox)
+    next(rs)
+    red = [plane_reduce(c, lambda g, h=h: h.at[:, g], su.at[k], ib.at[k], (fwd, rev, fwd)[k]) for k, h in enumerate((h0, h1, h2))]
+    for f in red[:2]:
+        next(f)
+    rs2 = rs_flow(c, part2, mlp_own, sib2, inbox2, outbox2)
+    run(rs)
     total = jnp.zeros_like(gsum)
     for s in range(2):
         v = res[s]
@@ -481,21 +574,58 @@
         gres[s] = gr
         own[s] = gr.astype(BF)
     gsum[...] = total
-    run(ag_flow(c, own, full), rs_flow(c, part2, mlp_own, sib2, inbox2, outbox2))
-
-
-def back_call(part, part2, res, go, gain):
+    ag = ag_flow(c, own, full)
+    next(ag)
+    next(rs2)
+    next(red[2])
+    next(red[0])
+    next(rs2)
+    next(ag)
+    next(red[1])
+    next(rs2)
+    next(ag)
+    for f in red[2:] + red[:1]:
+        for _ in range(len(c.bits) - 1 if f is red[2] else len(c.bits) - 2):
+            next(f)
+    for f in red[1:2]:
+        for _ in range(len(c.bits) - 2):
+            next(f)
+    next(rs2)
+    finish(red[0])
+    s0 = spread_z(c, *units_back(lambda t: su.at[0, 0, t], o0))
+    next(s0)
+    finish(ag)
+    finish(rs2)
+    finish(red[1])
+    l1 = c.local(su.at[1, 0], r1, c.slot())
+    l1.start()
+    finish(red[2])
+    l2 = c.local(su.at[2, 0], r2, c.slot())
+    l2.start()
+    run(s0)
+    l1.wait()
+    l2.wait()
+
+
+def finish(f):
+    for _ in f:
+        pass
+
+
+def back_call(part, part2, res, go, gain, h0, h1, h2, units):
     _, n, d = go.shape
+    _, ng, r, fs = h0.shape
     S = jax.ShapeDtypeStruct
     shape = (2, TP, 2, n, d)
     return call(
         back_kernel,
-        (S((2, n, d), F32), S((1, d), F32), S((2, n, d), F32), S(shape, BF)),
-        [VM] * 5,
-        (VM, VM, VM, HBM),
-        [pltpu.VMEM((2, n, d), F32), pltpu.VMEM((2, n, d), BF)] + rs_scratch(n, d) + rs_scratch(n, d),
-        3,
-    )(part.reshape(shape), part2.reshape(shape), res, go, gain[None])
+        (S((2, n, d), F32), S((1, d), F32), S((2, n, d), F32), S(shape, BF), S((r, units), BF), S((TP, r, fs), BF), S((TP, r, fs), BF)),
+        [VM] * 5 + [HBM] * 3,
+        (VM, VM, VM, HBM, HBM, HBM, HBM),
+        [pltpu.VMEM((2, n, d), F32), pltpu.VMEM((2, n, d), BF)] + rs_scratch(n, d) + rs_scratch(n, d)
+        + [pltpu.VMEM((3, ng // 2, TP, r, fs), BF), pltpu.VMEM((3, ng - 1, TP, r, fs), BF)],
+        3, 256,
+    )(part.reshape(shape), part2.reshape(shape), res, go, gain[None], h0, h1, h2)
 
 
 def small_flow(c, small, inbox, zbox, sbox, gains, table):
@@ -506,7 +636,7 @@
         copy.wait()
         small[k + 1] = small[k] + inbox[k]
     last = len(c.bits)
-    z = spread_z(c, lambda t: small.at[last], lambda t: zbox.at[t])
+    z = spread_z(c, lambda t, k: small.at[last], lambda t, k: zbox.at[t])
     next(z)
     yield
     run(z)
@@ -519,31 +649,34 @@
     gains[...] = sbox[0] + sbox[1]
 
 
-def end_kernel(part, x, gres, gain, gwb, gwo, ggb, gwm, gain_b, chan_rows, gin, gains, table, owb, owo, ogb, owm,
-               small, small_in, zbox, sbox, tot, sib, inbox, outbox, su_m, in_m, su_x, in_x, su_g, in_g, send, recv):
+def end_kernel(part, x, gres, gain, gwb0, gwb1, ggb, rwo, r2, gain_b, chan_rows, gin, gains, table, owb, owo, ogb, o2,
+               small, small_in, zbox, sbox, tot, sib, inbox, outbox, su_x, in_x, su_g, in_g, send, recv):
     c = Comm(send, recv)
     c.barrier()
     fwd, rev = c.bits, c.bits[::-1]
     red, spread = [], []
-    for k in range(3):
-        own = lambda g, k=k: gwm.at[k, :, g]
-        red.append(plane_reduce(c, own, su_m.at[k], in_m.at[k], rev if k % 2 else fwd))
-        spread.append(spread_z(c, lambda t, k=k: su_m.at[k, 0, t], lambda t, k=k: owm.at[k, t]))
-    for k in range(3):
-        own = (lambda g, k=k: gwb.at[k, :, g]) if k < 2 else (lambda g: gwo.at[:, g])
-        out = (lambda t, k=k: owb.at[k, t]) if k < 2 else (lambda t: owo.at[t])
-        red.append(plane_reduce(c, own, su_x.at[k], in_x.at[k], fwd if k % 2 else rev))
-        spread.append(spread_z(c, lambda t, k=k: su_x.at[k, 0, t], out))
+    for k, gw in enumerate((gwb0, gwb1)):
+        red.append(plane_reduce(c, lambda g, gw=gw: gw.at[:, g], su_x.at[k], in_x.at[k], rev if k else fwd))
+        for extra in (False, True):
+            spread.append((k, spread_z(c, *heads_out(lambda t, k=k: su_x.at[k, 0, t], owb.at[k], extra))))
     for k in range(2):
         for h in range(2):
             i = 2 * k + h
             red.append(plane_reduce(c, lambda g, k=k, h=h: ggb.at[k, h, :, g], su_g.at[i], in_g.at[i], fwd if k else rev))
-            spread.append(spread_z(c, lambda t, i=i: su_g.at[i, 0, t], lambda t, k=k, h=h: ogb.at[k, h, t]))
+            spread.append((2 + i, spread_z(
+                c, lambda t, q, i=i: su_g.at[i, 0, t], lambda t, q, k=k, h=h: ogb.at[k, 4 if h else t],
+                ((fifth, 0),) if h else ((None, 0),), "from")))
     rs = rs_flow(c, part, tot, sib, inbox, outbox)
     next(rs)
     for f in red:
         next(f)
-    run(rs)
+    z0 = [spread_z(c, *units_back(lambda t: r2.at[t], o2))]
+    for extra in (False, True):
+        z0.append(spread_z(c, *heads_out(lambda t: rwo.at[t], owo, extra)))
+    next(rs)
+    for f in z0:
+        next(f)
+    finish(rs)
     total = jnp.zeros_like(gain)
     for s in range(2):
         v = x[s].astype(F32)
@@ -563,31 +696,33 @@
         for f in red:
             next(f)
         next(sm)
-    for f, s in zip(red, spread):
-        run(f)
-        next(s)
-    run(sm, *spread)
-
-
-def end_call(part, x, gres, gain, gwb, gwo, ggb, gwm, gain_b, chan_rows):
+    for i, f in enumerate(red):
+        finish(f)
+        for k, z in spread:
+            if k == i:
+                next(z)
+    next(sm)
+    run(sm, *z0, *[z for _, z in spread])
+
+
+def end_call(part, x, gres, gain, gwb0, gwb1, ggb, rwo, r2, gain_b, chan_rows, units):
     _, n, d = x.shape
     ng = lax.axis_size("dp") // TP
-    r, gr, fs = gwb.shape[3], ggb.shape[4], gwm.shape[4]
+    r, gr, steps = gwb0.shape[2], ggb.shape[4], (lax.axis_size("dp") // TP).bit_length()
     S = jax.ShapeDtypeStruct
-    half = ng // 2
 
     def sets(k, rows, width):
-        return [pltpu.VMEM((k, half, TP, rows, width), BF), pltpu.VMEM((k, ng - 1, TP, rows, width), BF)]
+        return [pltpu.VMEM((k, ng // 2, TP, rows, width), BF), pltpu.VMEM((k, ng - 1, TP, rows, width), BF)]
 
     return call(
         end_kernel,
-        (S((2, n, d), F32), S((8, d), F32), S((TP, 8, 512), F32), S((2, TP, r, 512), BF), S((TP, r, 512), BF), S((2, 2, TP, gr, 256), BF), S((3, TP, r, fs), BF)),
-        [VM] * 4 + [HBM] * 4 + [VM] * 2,
+        (S((2, n, d), F32), S((8, d), F32), S((TP, 8, 512), F32), S((2, r, 1280), BF), S((r, 1280), BF), S((2, 5, gr, 256), BF), S((r, units), BF)),
+        [VM] * 4 + [HBM] * 5 + [VM] * 2,
         (VM,) * 3 + (HBM,) * 4,
-        [pltpu.VMEM((ng.bit_length(), 16, d), F32), pltpu.VMEM((ng.bit_length() - 1, 16, d), F32), pltpu.VMEM((TP, 16, d), F32), pltpu.VMEM((2, 8, d), F32)]
-        + [pltpu.VMEM((2, n, d), F32)] + rs_scratch(n, d) + sets(3, r, fs) + sets(3, r, 512) + sets(4, gr, 256),
-        4, 400,
-    )(part.reshape(2, TP, 2, n, d), x, gres, gain[None], gwb, gwo, ggb, gwm, gain_b, chan_rows)
+        [pltpu.VMEM((steps, 16, d), F32), pltpu.VMEM((steps - 1, 16, d), F32), pltpu.VMEM((TP, 16, d), F32), pltpu.VMEM((2, 8, d), F32),
+         pltpu.VMEM((2, n, d), F32)] + rs_scratch(n, d) + sets(2, r, 512) + sets(4, gr, 256),
+        4, 256,
+    )(part.reshape(2, TP, 2, n, d), x, gres, gain[None], gwb0, gwb1, ggb, rwo, r2, gain_b, chan_rows)
 
 
 def heads_of(a, axis):
@@ -642,6 +777,10 @@
     for p in partners:
         pl.semaphore_signal(sem, inc=1, device_id=p, device_id_type=MESH)
     pl.semaphore_wait(sem, len(partners))
+
+
+def line_partners(c):
+    return [c.at(t=(c.t + o) % TP) for o in range(1, TP)]
 
 
 def share(c, table):
@@ -670,13 +809,22 @@
     return jnp.concatenate(rows, axis=0)
 
 
-def mix_fwd_kernel(br0, ci, gb, chan, db, mixed, conv, gates, state, rim, carry, table, a_ref, d_ref, ext, rim_in, send, recv):
+def mix_fwd_kernel(br0, ci, gb, chan, db, wop, m0, zero, mixed, conv, gates, state, rim, carry, table, wo, p0, a_ref, d_ref, ext, rim_in, send, recv):
     c = Comm(send, recv)
-    greet(plane_partners(c))
+    greet(plane_partners(c) + line_partners(c))
     n, width = ci.shape[1], ci.shape[2]
     rslot = c.slot()
     out = c.to(ci.at[:, pl.ds(n - 16, 16)], rim_in, c.at(g=(c.g + 1) % c.ng), rslot)
     out.start()
+    z0 = spread_z(c, *units_to(m0, lambda t: p0.at[t]))
+    next(z0)
+    fwd, rev = c.bits, c.bits[::-1]
+    g0 = [plane_gather(c, lambda g: wo.at[pl.ds(0, 2), g], fwd, wop.at[pl.ds(0, 2)]), plane_gather(c, lambda g: wo.at[pl.ds(2, 2), g], rev, wop.at[pl.ds(2, 2)])]
+    for f in g0:
+        next(f)
+    pad = zero.shape[2]
+    fill = c.local(zero, p0.at[:, :, pl.ds(p0.shape[2] - pad, pad)], c.slot())
+    pl.when(outer(c.t))(lambda: fill.start())
     out.wait()
     row = lax.broadcasted_iota(jnp.int32, (n, 1), 0)
     for b in range(2 * TP):
@@ -715,6 +863,8 @@
     h = jnp.concatenate([v[1] for v in ph], axis=1)
     table[c.g, 0] = p
     table[c.g, 1] = h
+    for f in g0:
+        next(f)
     share(c, table)
     cin = entering(c, lambda g: table[g, 0], lambda g: table[g, 1], width, False)
     carry[...] = cin
@@ -732,29 +882,39 @@
         v = lanes_out(d_ref, rows)
         state[rows, :] = v
         mixed[rows, :] = (v * gelu_pair(br0[rows, :])[0]).astype(BF)
-
-
-def mix_fwd_call(br0, ci, gb, chan, db):
+    run(*g0, z0)
+    pl.when(outer(c.t))(lambda: fill.wait())
+
+
+def mix_fwd_call(br0, ci, gb, chan, db, wop, m0):
     ng = lax.axis_size("dp") // TP
     rows, width = br0.shape
     n = rows // (2 * TP)
+    r = m0.shape[0]
+    _, big, small = cut(m0.shape[1], 0)
     S = jax.ShapeDtypeStruct
     return call(
         mix_fwd_kernel,
         (S((rows, width), BF), S((rows, width), BF), S((2, rows, width), F32), S((rows, width), F32),
-         S((2 * TP, 8, width), F32), S((2 * TP, width), F32), S((ng, 2, 2 * TP, width), F32)),
-        [VM] * 5,
-        (VM,) * 7,
+         S((2 * TP, 8, width), F32), S((2 * TP, width), F32), S((ng, 2, 2 * TP, width), F32), S((TP, ng, r, width), BF), S((TP, r, big), BF)),
+        [VM] * 5 + [HBM, HBM, VM],
+        (VM,) * 7 + (HBM, HBM),
         [pltpu.VMEM((width // 128, rows, 128), F32), pltpu.VMEM((width // 128, rows, 128), F32), pltpu.VMEM((2, n + 8, width), F32), pltpu.VMEM((2 * TP, 16, width), BF)],
-        5, 32,
-    )(br0, ci.reshape(2 * TP, n, width), gb, chan, db[None])
-
-
-def mix_bwd_kernel(gm, br0, ci, gb, chan, db, conv, gates, state, rim, carry, table, gbr, ggb, sums,
-                   a_ref, adj, gc, gpl, ext, heads, etab, rim_in, send, recv):
+        5, 128,
+    )(br0, ci.reshape(2 * TP, n, width), gb, chan, db[None], wop, m0, jnp.zeros((TP, r, big - small), BF))
+
+
+def mix_bwd_kernel(gm, br0, ci, gb, chan, db, conv, gates, state, rim, carry, table, gwo, r1, gbr, ggb, sums, rwo, o1,
+                   a_ref, adj, gc, gpl, ext, heads, etab, rim_in, su, ib, send, recv):
     c = Comm(send, recv)
-    greet(plane_partners(c))
+    greet(plane_partners(c) + line_partners(c))
     n, width = ci.shape[1], ci.shape[2]
+    z0 = spread_z(c, *units_back(lambda t: r1.at[t], o1))
+    next(z0)
+    fwd, rev = c.bits, c.bits[::-1]
+    red = [plane_reduce(c, lambda g, k=k: gwo.at[pl.ds(2 * k, 2), g], su.at[k], ib.at[k], rev if k else fwd) for k in range(2)]
+    for f in red:
+        next(f)
     for b in range(2 * TP):
         rows = pl.ds(b * n, n)
         act, slope = gelu_pair(br0[rows, :])
@@ -771,6 +931,9 @@
     e = jnp.concatenate(e, axis=1)
     etab[c.g] = e
     share(c, etab)
+    for f in red:
+        for _ in range(len(c.bits) - 1):
+            next(f)
     ein = entering(c, lambda g: table[g, 0], lambda g: etab[g], width, True)
 
     def step2(i, es):
@@ -830,39 +993,45 @@
         for k in range(1, 4):
             v = v + chan[k:k + 1] * gc[b, pl.ds(k, n), :]
         gbr[1, rows, :] = v.astype(BF)
-
-
-def mix_bwd_call(gm, br0, ci, gb, chan, db, saved):
+    held = []
+    for k, f in enumerate(red):
+        finish(f)
+        held.append(c.local(su.at[k, 0], rwo.at[pl.ds(2 * k, 2)], c.slot()))
+        held[-1].start()
+    run(z0)
+    for h in held:
+        h.wait()
+
+
+def mix_bwd_call(gm, br0, ci, gb, chan, db, saved, gwo, r1, units):
     ng = lax.axis_size("dp") // TP
     rows, width = br0.shape
     n = rows // (2 * TP)
+    r = r1.shape[1]
     S = jax.ShapeDtypeStruct
     V = pltpu.VMEM
     return call(
         mix_bwd_kernel,
-        (S((2, rows, width), BF), S((2, 2, 256, 256), F32), S((8, width), F32)),
-        [VM] * 12,
-        (VM,) * 3,
+        (S((2, rows, width), BF), S((2, 2, 256, 256), F32), S((8, width), F32), S((TP, r, width), BF), S((r, units), BF)),
+        [VM] * 12 + [HBM] * 2,
+        (VM,) * 3 + (HBM,) * 2,
         [V((width // 128, rows, 128), F32), V((width // 128, rows, 128), F32), V((2 * TP, n + 8, width), F32), V((2, rows, width), BF),
-         V((2, n + 8, width), F32), V((2 * TP, 8, width), F32), V((ng, 2 * TP, width), F32), V((2 * TP, 8, width), F32)],
-        6, 32,
-    )(gm, br0, ci.reshape(2 * TP, n, width), gb, chan, db[None], *saved)
+         V((2, n + 8, width), F32), V((2 * TP, 8, width), F32), V((ng, 2 * TP, width), F32), V((2 * TP, 8, width), F32),
+         V((2, ng // 2, 2, r, width), BF), V((2, ng - 1, 2, r, width), BF)],
+        6, 128,
+    )(gm, br0, ci.reshape(2 * TP, n, width), gb, chan, db[None], *saved, gwo, r1)
 
 
 def dot(a, b, ca, cb):
     return lax.dot_general(a, b, (((ca,), (cb,)), ((), ())), preferred_element_type=F32)
-
-
-def pack(parts):
-    return jnp.stack(parts)
 
 
 def body(block_input, lengths, norm_gains, w_branch, channel_params, gate_blocks, decay_param, w_out, w_mlp, w_down, out_grad):
     ndp, ng, t, g = plan()
     dp, mp = lax.axis_index("dp"), lax.axis_index("mp")
     rows, width = block_input.shape[1:]
-    r = w_branch.shape[1]
-    fs = w_mlp.shape[2] // TP
+    r, gr, units = w_branch.shape[1], gate_blocks.shape[2], w_mlp.shape[2]
+    fs = cut(units, 0)[1]
     chan = heads_of(channel_params, 1)
     dpar = heads_of(decay_param[None], 1)[0]
     decay_base = jax.nn.softplus(dpar)
@@ -870,45 +1039,40 @@
     valid = (pos[None] < lengths[:, None])[..., None]
     x = block_input
     grad_own = jnp.where(valid, out_grad, jnp.zeros_like(out_grad))
-    mlp = jnp.concatenate([w_mlp, w_down.T[None]], 0).reshape(3, r, TP, fs).transpose(2, 0, 1, 3)
-    na, go, wb, wo, gb, wm = start_call(x, grad_own, norm_gains[0], w_branch, w_out.T, gate_blocks, mlp)
-    na, go = na.reshape(-1, width), go.reshape(-1, width)
-    wb, wo, wm = wb.reshape(2, width, 512), wo.reshape(width, 512), wm.reshape(3, width, fs)
+    na, wb0, wb1, wop, gb = start_call(x, norm_gains[0], w_branch, w_out.T, gate_blocks)
+    na = na.reshape(-1, width)
+    wb0, wb1 = wb0.reshape(width, 512), wb1.reshape(width, 512)
     gb = gb.reshape(2, 2, 256, 256)
-    wd = wm[2]
-    branch0 = dot(na, wb[0], 1, 0)
-    conv_input = dot(na, wb[1], 1, 0).astype(BF)
-    mixed, *saved = mix_fwd_call(branch0, conv_input, gb, chan, decay_base)
-    residual, nb = mid_call(dot(mixed, wo, 1, 1).astype(BF), x, norm_gains[1])
-    nb = nb.reshape(-1, width)
-    first, second = dot(nb, wm[0], 1, 0), dot(nb, wm[1], 1, 0)
+    branch0 = dot(na, wb0, 1, 0)
+    conv_input = dot(na, wb1, 1, 0).astype(BF)
+    mixed, *saved, wo, p0 = mix_fwd_call(branch0, conv_input, gb, chan, decay_base, wop, w_mlp[0])
+    wo = wo.reshape(width, 512)
+    residual, nb, go, w0, w1, wd = mid_call(dot(mixed, wo, 1, 1).astype(BF), x, grad_own, norm_gains[1], p0, w_mlp[1], w_down.T)
+    nb, go = nb.reshape(-1, width), go.reshape(-1, width)
+    w0, w1, wd = w0.reshape(width, fs), w1.reshape(width, fs), wd.reshape(width, fs)
+    first, second = dot(nb, w0, 1, 0), dot(nb, w1, 1, 0)
     act, act_pull = jax.vjp(jax.nn.gelu, first)
     hidden = (act * second).astype(BF)
     mlp_part = dot(hidden, wd, 1, 1).astype(BF)
     gh = dot(go, wd, 1, 0)
-    gwd = dot(go, hidden, 0, 0).astype(BF)
+    block = (TP, ng, r, fs)
+    gwd = dot(go, hidden, 0, 0).astype(BF).reshape(block)
     ggu = [act_pull(gh * second)[0].astype(BF), (gh * act).astype(BF)]
-    gwm = [dot(nb, ggu[k], 0, 0).astype(BF) for k in range(2)]
-    gnb = (dot(ggu[0], wm[0], 1, 1) + dot(ggu[1], wm[1], 1, 1)).astype(BF)
-    gres, gain_b, mlp_own, gmo = back_call(gnb, mlp_part, residual, grad_own, norm_gains[1])
+    gw0, gw1 = [dot(nb, v, 0, 0).astype(BF).reshape(block) for v in ggu]
+    gnb = (dot(ggu[0], w0, 1, 1) + dot(ggu[1], w1, 1, 1)).astype(BF)
+    gres, gain_b, mlp_own, gmo, o0, r1, r2 = back_call(gnb, mlp_part, residual, grad_own, norm_gains[1], gw0, gw1, gwd, units)
     out = jnp.where(valid, residual + mlp_own, 0.0).astype(BF)
     gmo = gmo.reshape(-1, width)
-    gwo = dot(gmo, mixed, 0, 0).astype(BF)
-    gbr, ggb, chan_rows = mix_bwd_call(dot(gmo, wo, 1, 0), branch0, conv_input, gb, chan, decay_base, saved)
-    gwb = [dot(na, gbr[k], 0, 0).astype(BF) for k in range(2)]
-    gna = (dot(gbr[0], wb[0], 1, 1) + dot(gbr[1], wb[1], 1, 1)).astype(BF)
-    gr = gate_blocks.shape[2]
-    gin, gains, table, owb, owo, ogb, owm = end_call(
-        gna, x, gres, norm_gains[0],
-        jnp.stack(gwb).reshape(2, TP, ng, r, 512), gwo.reshape(TP, ng, r, 512),
-        ggb.astype(BF).reshape(2, 2, TP, ng, gr, 256), jnp.stack(gwm + [gwd]).reshape(3, TP, ng, r, fs), gain_b, chan_rows,
+    block = (TP, ng, r, 512)
+    gwo = dot(gmo, mixed, 0, 0).astype(BF).reshape(block)
+    gbr, ggb, chan_rows, rwo, o1 = mix_bwd_call(dot(gmo, wo, 1, 0), branch0, conv_input, gb, chan, decay_base, saved, gwo, r1, units)
+    gwb0, gwb1 = [dot(na, gbr[k], 0, 0).astype(BF).reshape(block) for k in range(2)]
+    gna = (dot(gbr[0], wb0, 1, 1) + dot(gbr[1], wb1, 1, 1)).astype(BF)
+    gin, gains, table, owb, owo, ogb, o2 = end_call(
+        gna, x, gres, norm_gains[0], gwb0, gwb1, ggb.astype(BF).reshape(2, 2, TP, ng, gr, 256), rwo, r2, gain_b, chan_rows, units,
     )
-    owb, owo = owb.astype(F32), owo.astype(F32)
-    g_wb = jnp.concatenate([owb[:, i, :, :256] for i in range(TP)] + [owb[:, 1, :, 256:]], -1)
-    g_wo = jnp.concatenate([owo[i, :, :256] for i in range(TP)] + [owo[1, :, 256:]], -1).T
-    g_gb = jnp.concatenate([ogb[:, 0], ogb[:, 1, 1:2]], 1).astype(F32)
-    g_wm = owm[:2].transpose(0, 2, 1, 3).reshape(2, r, TP * fs).astype(F32)
-    g_wd = owm[2].transpose(0, 2, 1).reshape(TP * fs, r).astype(F32)
+    g_wb, g_wo, g_gb = owb.astype(F32), owo.astype(F32).T, ogb.astype(F32)
+    g_wm, g_wd = jnp.stack([o0, o1]).astype(F32), o2.astype(F32).T
     crow = jnp.concatenate([table[i, :, :256] for i in range(TP)] + [table[1, :, 256:]], -1)
     return out, gin, gains[:2], g_wb, crow[:7], g_gb, crow[7] * jax.nn.sigmoid(decay_param), g_wo, g_wm, g_wd
 

time: 1150 us -> 887 us (0.77)
  Pallas kernels: 893 us -> 710 us
  local copies, waits for them, and re-layouts: 73.6 us -> 10.1 us
  other arithmetic: 31.6 us -> 17.1 us
    pallas_call x1, Pallas kernels: 303 us -> 138 us  [end_call(): call(end_kernel, (S((2, n, d), F32), S((8, d), F32), S((TP, 8, 512), F32)...]
    pallas_call x2, Pallas kernels: 407 us -> 306 us  [the longest x1 217 us: mid_call(): call(mid_kernel, (S((2, n, d), F32), S((2, TP, 2, n, d), BF), S((2, TP, 2...]
    pallas_call x1, Pallas kernels: 119 us -> 174 us  [back_call(): call(back_kernel, (S((2, n, d), F32), S((1, d), F32), S((2, n, d), F32),...]
    convert_element_type x7 -> x0, local copies, waits for them, and re-layouts: 42 us -> none  [the longest x2 15.9 us: body(): gwm = [dot(nb, ggu[k], 0, 0).astype(BF) for k in range(2)]]
    pallas_call x1, Pallas kernels: 28.6 us -> 45.8 us  [mix_fwd_call(): call(mix_fwd_kernel, (S((rows, width), BF), S((rows, width), BF), S((2, r...]
    another operation x2 -> x0, other arithmetic: 16.1 us -> none  [the longest x1 13.3 us: body(): jnp.stack(gwm + [gwd]).reshape(3, TP, ng, r, fs)]
    concatenate x6 -> x0, local copies, waits for them, and re-layouts: 12.3 us -> none  [the longest x4 12.3 us: body(): jnp.concatenate([w_mlp, w_down.T[None]], 0).reshape(3, r, TP, fs)]
where the time goes in v3:
time: 887 us; the launch traced here: 875 us
  Pallas kernels  710 us (80%)
  matrix products  136 us (15%)
  other arithmetic  17.1 us (2%)
  local copies, waits for them, and re-layouts  10.1 us (1%)
    pallas_call x1, Pallas kernels, mid_call(): call(mid_kernel, (S((2, n, d), F32), S((2, TP, 2, n, d), BF), S((2, TP, 2...  217 us
    pallas_call x1, Pallas kernels, back_call(): call(back_kernel, (S((2, n, d), F32), S((1, d), F32), S((2, n, d), F32),...  174 us
    pallas_call x1, Pallas kernels, end_call(): call(end_kernel, (S((2, n, d), F32), S((8, d), F32), S((TP, 8, 512), F32)...  138 us
    dot_general x18, matrix products, dot(): lax.dot_general(a, b, (((ca,), (cb,)), ((), ())), preferred_element_type=...  136 us
    pallas_call x1, Pallas kernels, start_call(): call(start_kernel, (S((2, TP, 2, n, d), BF), S((TP, ng, r, 512), BF), S((...  89 us
    pallas_call x1, Pallas kernels, mix_fwd_call(): call(mix_fwd_kernel, (S((rows, width), BF), S((rows, width), BF), S((2, r...  45.8 us
    pallas_call x1, Pallas kernels, mix_bwd_call(): call(mix_bwd_kernel, (S((2, rows, width), BF), S((2, 2, 256, 256), F32),...  45.7 us

profile of v3, /device:TPU:0, one launch (start us, length us, event | category | flops | bytes accessed | tf_op | source)
XLA Modules:
  0.0 874.8 jit_solution(7935220068774699000)
XLA Ops:
  0.6 1.4 fusion.16
  2.1 89.0 %shard_map.186 = (bf16[2,4,2,64,2560]{4,3,2,1,0:T(8,128)(2,1)}, bf16[4,4,160,512]{3,2,1,0:T(8,128)(2,1)}, bf16[4,4,160,512]{3,2,1,0:T(8,128)(2,1)}, bf16[4,160,5...) custom-call(bf16[2,64,2560]{2,1,0:T(8,128)(2,1)} %x.5, f32[1,2560]{1,0:T(1,128)} %get-tuple-element.96.gain, ...), custom_call_target="tpu_custom_call" | custom-call | tf_op jit(solution)/shard_map/pallas_call | solution.py:480
  91.1 7.6 fusion.17.br0
  98.7 3.8 convolution_convert_fusion.8
  102.5 0.7 constant_dynamic-slice_fusion
  103.3 0.6 pad_maximum_fusion.chan
  103.9 0.1 dynamic-slice.3
  104.0 0.6 compare_select_fusion.db
  104.6 1.6 slice_bitcast_fusion
  106.2 0.7 broadcast_11_zero.2.zero
  106.9 45.8 %shard_map.187 = (bf16[1024,512]{1,0:T(8,128)(2,1)}, bf16[1024,512]{1,0:T(8,128)(2,1)}, f32[2,1024,512]{2,1,0:T(8,128)}, f32[1024,512]{1,0:T(8,128)}, f32[8,8,51...) custom-call(f32[1024,512]{1,0:T(8,128)} %fusion.17.br0, ...), custom_call_target="tpu_custom_call" | custom-call | tf_op jit(solution)/shard_map/pallas_call | solution.py:896
  152.6 7.4 convolution_convert_fusion
  160.0 0.1 broadcast_compare_fusion
  160.1 1.0 broadcast_select_fusion.go
  161.0 217.2 %shard_map.188 = (f32[2,64,2560]{2,1,0:T(8,128)}, bf16[2,4,2,64,2560]{4,3,2,1,0:T(8,128)(2,1)}, bf16[2,4,2,64,2560]{4,3,2,1,0:T(8,128)(2,1)}, bf16[4,4,160,1024]...) custom-call(bf16[2,4,2,64,2560]{4,3,2,1,0:T(8,128)(2,1)} %bitcast.89, ...), custom_call_target="tpu_custom_call" | custom-call | tf_op jit(solution)/shard_map/pallas_call | solution.py:543
  378.3 9.8 %fusion.19 = f32[1024,1024]{1,0:T(8,128)S(1)} fusion(bf16[1024,2560]{1,0:T(8,128)(2,1)} %bitcast.118, bf16[2560,1024]{1,0:T(8,128)(2,1)} %bitcast.134), kind=kOutput, calls=%fused_computation.57 | convolution fusion | flops 5368709120 | bytes 14680064 | tf_op jit(solution)/shard_map/dot_general | solution.py:1026
  388.2 7.1 fusion.18
  395.4 11.4 %multiply_convert_fusion = (bf16[1024,1024]{1,0:T(8,128)(2,1)}, bf16[1024,1024]{1,0:T(8,128)(2,1)S(1)}, bf16[1024,1024]{1,0:T(8,128)(2,1)S(1)}) fusion(f32[1024,1024]{1,0:T(8,128)S(1)} %fusion.19, f32[1024,1024]{1,0:T(8,128)} %fusion.18, bf16[1024,2560]{1,0:T(8,128)(2,1)S(1)} %bitcast.121, bf16[2560,1024]{1,0:T(8,128)(2,1)S(1)} %bitcast.133), kind=kOutput, calls=%fused_computation.19 | convolution fusion | flops 5395972096 | bytes 25165824 | tf_op jit(solution)/shard_map/dot_general | solution.py:1026
  406.7 10.8 %fusion.20 = f32[1024,2560]{1,0:T(8,128)} fusion(bf16[1024,1024]{1,0:T(8,128)(2,1)S(1)} %get-tuple-element.89, bf16[2560,1024]{1,0:T(8,128)(2,1)} %bitcast.135), kind=kOutput, calls=%fused_computation.58 | convolution fusion | flops 5368709120 | bytes 17825792 | tf_op jit(solution)/shard_map/dot_general | solution.py:1026
  417.5 11.5 %add_convert_fusion.1 = bf16[1024,2560]{1,0:T(8,128)(2,1)} fusion(f32[1024,2560]{1,0:T(8,128)} %fusion.20, bf16[1024,1024]{1,0:T(8,128)(2,1)S(1)} %get-tuple-element.90, bf16[2560,1024]{1,0:T(8,128)(2,1)} %bitcast.130), kind=kOutput, calls=%fused_computation.1 | convolution fusion | flops 5373952000 | bytes 23068672 | tf_op jit(solution)/shard_map/dot_general | solution.py:1026
  429.0 10.4 %convolution_convert_fusion.4 = bf16[1024,2560]{1,0:T(8,128)(2,1)} fusion(bf16[1024,1024]{1,0:T(8,128)(2,1)} %get-tuple-element.88, bf16[2560,1024]{1,0:T(8,128)(2,1)} %bitcast.124), kind=kOutput, calls=%fused_computation.8 | convolution fusion | flops 5371330560 | bytes 12582912 | tf_op jit(solution)/shard_map/dot_general | solution.py:1026
  439.4 7.5 convolution_convert_fusion.3
  446.9 7.4 convolution_convert_fusion.2
  454.3 7.5 convolution_convert_fusion.1
  461.9 174.3 %shard_map.189 = (f32[2,64,2560]{2,1,0:T(8,128)}, f32[1,2560]{1,0:T(1,128)}, f32[2,64,2560]{2,1,0:T(8,128)}, bf16[2,4,2,64,2560]{4,3,2,1,0:T(8,128)(2,1)}, bf16[...) custom-call(bf16[2,4,2,64,2560]{4,3,2,1,0:T(8,128)(2,1)} %bitcast.91, ...), custom_call_target="tpu_custom_call" | custom-call | tf_op jit(solution)/shard_map/pallas_call | solution.py:620
  636.1 2.5 select_convert_fusion
  638.6 6.8 fusion.21.gm
  645.5 4.2 convolution_convert_fusion.7
  649.7 45.7 %shard_map.190 = (bf16[2,1024,512]{2,1,0:T(8,128)(2,1)}, f32[2,2,256,256]{3,2,1,0:T(8,128)}, f32[8,512]{1,0:T(8,128)}, bf16[4,160,512]{2,1,0:T(8,128)(2,1)}, bf16[160,3840]{1,0:T(8,128)(2,1)}) custom-call(f32[1024,512]{1,0:T(8,128)} %fusion.21.gm, f32[1024,512]{1,0:T(8,128)} %fusion.17.br0, bf16[8,128,512]{2,1,0:T(8,128)(2,1)} %bitcast.97, ...), custom_call_target="tpu_custom_call" | custom-call | tf_op jit(solution)/shard_map/pallas_call | solution.py:1013
  695.4 7.1 fusion.10
  702.5 7.4 add_convert_fusion
  710.0 4.2 convolution_convert_fusion.6
  714.2 4.2 convolution_convert_fusion.5
  718.4 0.8 convert_element_type.74
  719.3 138.2 %shard_map.191 = (f32[2,64,2560]{2,1,0:T(8,128)}, f32[8,2560]{1,0:T(8,128)}, f32[4,8,512]{2,1,0:T(8,128)}, bf16[2,160,1280]{2,1,0:T(8,128)(2,1)}, bf16[160,1280]...) custom-call(bf16[2,4,2,64,2560]{4,3,2,1,0:T(8,128)(2,1)} %bitcast.90, ...), custom_call_target="tpu_custom_call" | custom-call | tf_op jit(solution)/shard_map/pallas_call | solution.py:717
  857.5 1.6 slice.52
  859.2 2.4 convert_element_type.75
  861.6 0.7 constant_dynamic-update-slice_fusion.4
  862.3 0.7 constant_dynamic-update-slice_fusion.3
  863.0 0.7 constant_dynamic-update-slice_fusion.2
  863.7 0.7 constant_dynamic-update-slice_fusion.1
  864.4 0.7 constant_dynamic-update-slice_fusion
  865.1 1.6 convert_element_type.76
  866.7 0.6 divide_multiply_fusion
  867.3 2.0 convert_bitcast_fusion.1
  869.4 2.6 maximum_convert_fusion
  871.9 1.6 convert_bitcast_fusion
  873.5 1.1 copy.26
  (68 shorter events, 0.2 us)
Async XLA Ops:
  91.0 7.6 copy-start.11
  91.0 7.6 copy-start.14
  98.7 5.2 copy-start.8
  98.7 5.9 copy-start.1
  152.6 7.4 copy-start.20
  152.6 7.5 copy-start.7
  378.3 9.9 %copy-start.12 = (bf16[2,4,2,64,2560]{4,3,2,1,0:T(8,128)(2,1)S(1)}, bf16[2,4,2,64,2560]{4,3,2,1,0:T(8,128)(2,1)}, u32[]{:S(2)}) copy-start(bf16[2,4,2,64,2560]{4,3,2,1,0:T(8,128)(2,1)} %get-tuple-element.58) | copy-start | bytes 15728644
  378.3 9.9 %copy-start.13 = (bf16[4,4,160,1024]{3,2,1,0:T(8,128)(2,1)S(1)}, bf16[4,4,160,1024]{3,2,1,0:T(8,128)(2,1)}, u32[]{:S(2)}) copy-start(bf16[4,4,160,1024]{3,2,1,0:T(8,128)(2,1)} %get-tuple-element.59) | copy-start | bytes 15728644
  378.3 17.0 %slice-start.2 = ((s8[5242880]{0:T(1024)(128)(4,1)}), s8[4194304]{0:T(1024)(128)(4,1)S(1)}, s32[]{:S(2)}) async-start(s8[5242880]{0:T(1024)(128)(4,1)} %bitcast.119), calls=%async_computation.2 | async-start | bytes 8388608
  378.3 17.0 %slice-start.6 = ((s8[5242880]{0:T(1024)(128)(4,1)}), s8[4194304]{0:T(1024)(128)(4,1)S(1)}, s32[]{:S(2)}) async-start(s8[5242880]{0:T(1024)(128)(4,1)} %bitcast.131), calls=%async_computation.6 | async-start | bytes 8388608
  388.1 7.2 slice-start.3
  388.2 7.2 slice-start.7
  446.9 7.4 copy-start.21
  461.9 174.3 %copy-start = (f32[2,64,2560]{2,1,0:T(8,128)S(1)}, f32[2,64,2560]{2,1,0:T(8,128)}, u32[]{:S(2)}) copy-start(f32[2,64,2560]{2,1,0:T(8,128)} %get-tuple-element.57.res) | copy-start | bytes 3932164
  461.9 176.8 %copy-start.17 = (bf16[4,4,160,512]{3,2,1,0:T(8,128)(2,1)S(1)}, bf16[4,4,160,512]{3,2,1,0:T(8,128)(2,1)}, u32[]{:S(2)}) copy-start(bf16[4,4,160,512]{3,2,1,0:T(8,128)(2,1)} %get-tuple-element.55) | copy-start | bytes 7864324
  636.1 9.3 %slice-start.4 = ((s8[5242880]{0:T(1024)(128)(4,1)}), s8[4194304]{0:T(1024)(128)(4,1)S(1)}, s32[]{:S(2)}) async-start(s8[5242880]{0:T(1024)(128)(4,1)} %bitcast.127), calls=%async_computation.4 | async-start | bytes 8388608
  638.6 6.8 slice-start.5
  638.6 6.8 copy-start.19
  649.7 45.7 %copy-start.16 = (bf16[4,4,160,512]{3,2,1,0:T(8,128)(2,1)S(1)}, bf16[4,4,160,512]{3,2,1,0:T(8,128)(2,1)}, u32[]{:S(2)}) copy-start(bf16[4,4,160,512]{3,2,1,0:T(8,128)(2,1)} %get-tuple-element.50) | copy-start | bytes 7864324
  695.4 7.1 copy-start.15
  695.4 7.1 copy-start.18
  695.4 14.5 %slice-start = ((s8[5242880]{0:T(1024)(128)(4,1)}), s8[4194304]{0:T(1024)(128)(4,1)S(1)}, s32[]{:S(2)}) async-start(s8[5242880]{0:T(1024)(128)(4,1)} %bitcast.112), calls=%async_computation | async-start | bytes 8388608
  702.5 7.4 slice-start.1
  714.2 4.2 copy-start.6
  719.3 147.4 %copy-start.9 = (f32[1280]{0:T(1024)S(1)}, f32[1280]{0:T(1024)}, u32[]{:S(2)}) copy-start(f32[1280]{0:T(1024)} %param.17) | copy-start | bytes 15364
  857.5 11.9 %copy-start.3 = (bf16[160,3840]{1,0:T(8,128)(2,1)S(1)}, bf16[160,3840]{1,0:T(8,128)(2,1)}, u32[]{:S(2)}) copy-start(bf16[160,3840]{1,0:T(8,128)(2,1)} %get-tuple-element.85) | copy-start | bytes 3686404
  857.5 11.9 %copy-start.4 = (bf16[160,3840]{1,0:T(8,128)(2,1)S(1)}, bf16[160,3840]{1,0:T(8,128)(2,1)}, u32[]{:S(2)}) copy-start(bf16[160,3840]{1,0:T(8,128)(2,1)} %get-tuple-element.86) | copy-start | bytes 3686404
  865.1 6.9 copy-start.10
  867.3 4.6 copy-start.5
  869.4 4.2 copy-start.2

commit v4 on v3

--- a/solution.py
+++ b/solution.py
@@ -38,6 +38,9 @@
         g = self.g if g is None else g
         return (t * self.ng + g, self.m if m is None else m)
 
+    def fifth(self, t=None):
+        return (self.t if t is None else t) == 1 + self.m
+
     def flip(self, g, b):
         return g + b - 2 * b * ((g // b) % 2)
 
@@ -61,6 +64,17 @@
 
     def local(self, src, dst, slot):
         return pltpu.make_async_copy(src, dst, self.send.at[slot])
+
+
+def finish(*flows):
+    for f in flows:
+        for _ in f:
+            pass
+
+
+def step(*flows):
+    for f in flows:
+        next(f)
 
 
 def run(*flows):
@@ -73,67 +87,81 @@
                 flows.remove(f)
 
 
-def ag_flow(c, own, full):
+def ag_flow(c, own, full, late=False):
     t, m = c.t, c.m
     sib = c.at(m=1 - m)
-    up = [c.slot() for _ in range(TP - 1)]
-    down = [c.slot() for _ in range(TP - 1)]
-    d2u = [c.slot() for _ in range(TP - 1)]
-    d2d = [c.slot() for _ in range(TP - 1)]
-    d2o, loc = c.slot(), c.slot()
-
-    def up_copy(k):
+
+    def slots():
+        return [[c.slot() for _ in range(2)] for _ in range(TP - 1)]
+
+    up, down, d2u, d2d = slots(), slots(), slots(), slots()
+    d2o, loc = [c.slot() for _ in range(2)], [c.slot() for _ in range(2)]
+
+    def row(b, s, mm):
+        return full.at[s, b, mm]
+
+    def up_copy(k, s):
         b = t - k
-        return c.to(own if k == 0 else full.at[:, b, m], full.at[:, b, m], c.at(t=t + 1), up[k])
-
-    def down_copy(k):
+        return c.to(own.at[s] if k == 0 else row(b, s, m), row(b, s, m), c.at(t=t + 1), up[k][s])
+
+    def down_copy(k, s):
         b = t + k
-        return c.to(own if k == 0 else full.at[:, b, m], full.at[:, b, m], c.at(t=t - 1), down[k])
-
-    def side(b, slot, src=None):
-        return c.to(full.at[:, b, m] if src is None else src, full.at[:, b, m], sib, slot)
-
-    def got(b, slot, mm):
-        return c.to(full.at[:, b, mm], full.at[:, b, mm], sib, slot)
-
-    pl.when(t < TP - 1)(lambda: up_copy(0).start())
-    pl.when(t > 0)(lambda: down_copy(0).start())
-    side(t, d2o, own).start()
-    c.local(own, full.at[:, t, m], loc).start()
+        return c.to(own.at[s] if k == 0 else row(b, s, m), row(b, s, m), c.at(t=t - 1), down[k][s])
+
+    def side(b, slot, s, src=None):
+        return c.to(row(b, s, m) if src is None else src, row(b, s, m), sib, slot)
+
+    def got(b, slot, s, mm):
+        return c.to(row(b, s, mm), row(b, s, mm), sib, slot)
+
+    def both(f):
+        return lambda: [f(s) for s in range(2)] and None
+
+    pl.when((t < TP - 1) & (t > 0) if late else t < TP - 1)(both(lambda s: up_copy(0, s).start()))
+    pl.when((t > 0) & (t < TP - 1) if late else t > 0)(both(lambda s: down_copy(0, s).start()))
+    for s in range(2):
+        side(t, d2o[s], s, own.at[s]).start()
+        c.local(own.at[s], row(t, s, m), loc[s]).start()
     yield
+    if late:
+        pl.when(t == 0)(both(lambda s: up_copy(0, s).start()))
+        pl.when(t == TP - 1)(both(lambda s: down_copy(0, s).start()))
+        yield
     for k in range(TP - 1):
-        def from_below():
-            got(t - 1 - k, up[k], m).wait_recv()
-            side(t - 1 - k, d2u[k]).start()
+        def from_below(s):
+            got(t - 1 - k, up[k][s], s, m).wait_recv()
             if k < TP - 2:
-                pl.when(t < TP - 1)(lambda: up_copy(k + 1).start())
-
-        def from_above():
-            got(t + 1 + k, down[k], m).wait_recv()
-            side(t + 1 + k, d2d[k]).start()
+                pl.when(t < TP - 1)(lambda: up_copy(k + 1, s).start())
+            side(t - 1 - k, d2u[k][s], s).start()
+
+        def from_above(s):
+            got(t + 1 + k, down[k][s], s, m).wait_recv()
             if k < TP - 2:
-                pl.when(t > 0)(lambda: down_copy(k + 1).start())
-
-        pl.when(t - 1 - k >= 0)(from_below)
-        pl.when(t + 1 + k < TP)(from_above)
+                pl.when(t > 0)(lambda: down_copy(k + 1, s).start())
+            side(t + 1 + k, d2d[k][s], s).start()
+
+        for s in range(2):
+            pl.when(t - 1 - k >= 0)(lambda: from_below(s))
+            pl.when(t + 1 + k < TP)(lambda: from_above(s))
         yield
-    c.local(own, full.at[:, t, m], loc).wait()
-    side(t, d2o, own).wait_send()
-    got(t, d2o, 1 - m).wait_recv()
+    for s in range(2):
+        c.local(own.at[s], row(t, s, m), loc[s]).wait()
+        side(t, d2o[s], s, own.at[s]).wait_send()
+        got(t, d2o[s], s, 1 - m).wait_recv()
     for k in range(TP - 1):
-        pl.when((t < TP - 1) & (t - k >= 0))(lambda: up_copy(k).wait_send())
-        pl.when((t > 0) & (t + k < TP))(lambda: down_copy(k).wait_send())
-
-        def below():
-            side(t - 1 - k, d2u[k]).wait_send()
-            got(t - 1 - k, d2u[k], 1 - m).wait_recv()
-
-        def above():
-            side(t + 1 + k, d2d[k]).wait_send()
-            got(t + 1 + k, d2d[k], 1 - m).wait_recv()
-
-        pl.when(t - 1 - k >= 0)(below)
-        pl.when(t + 1 + k < TP)(above)
+        pl.when((t < TP - 1) & (t - k >= 0))(both(lambda s: up_copy(k, s).wait_send()))
+        pl.when((t > 0) & (t + k < TP))(both(lambda s: down_copy(k, s).wait_send()))
+
+        def below(s):
+            side(t - 1 - k, d2u[k][s], s).wait_send()
+            got(t - 1 - k, d2u[k][s], s, 1 - m).wait_recv()
+
+        def above(s):
+            side(t + 1 + k, d2d[k][s], s).wait_send()
+            got(t + 1 + k, d2d[k][s], s, 1 - m).wait_recv()
+
+        pl.when(t - 1 - k >= 0)(both(below))
+        pl.when(t + 1 + k < TP)(both(above))
 
 
 def rs_scratch(rows, width):
@@ -151,33 +179,32 @@
     lower = t < TP // 2
     u = jnp.where(lower, t, TP - 1 - t)
     da = jnp.where(lower, 0, 1)
-    step = 1 - 2 * da
-    near = [c.slot() for _ in range(TP)]
+    hop = 1 - 2 * da
+    near = [[c.slot() for _ in range(2)] for _ in range(TP)]
     base = c.n
-    for _ in range(2 * (TP - 1)):
+    for _ in range(4 * (TP - 1)):
         c.slot()
 
     def real(d):
         return jnp.where(lower, d, TP - 1 - d)
 
-    def cross(d):
-        return c.to(part.at[:, real(d), 1 - m], sib.at[:, real(d)], other, near[d])
-
-    def msg(flow, j):
+    def cross(d, s):
+        return c.to(part.at[s, real(d), 1 - m], sib.at[s, real(d)], other, near[d][s])
+
+    def msg(flow, j, s):
         way = da if flow == 0 else 1 - da
-        dev = c.at(t=t + step if flow == 0 else t - step)
-        return c.to(outbox.at[j if flow == 0 else 2], inbox.at[way, j], dev, base + way * (TP - 1) + j)
-
-    def add(d, into, terms):
+        dev = c.at(t=t + hop if flow == 0 else t - hop)
+        return c.to(outbox.at[j if flow == 0 else 2, s], inbox.at[way, j, s], dev, base + (way * (TP - 1) + j) * 2 + s)
+
+    def add(d, s, into, terms):
         b = real(d)
 
         def rows16(i, _):
             sl = pl.ds(pl.multiple_of(i * 16, 16), 16)
-            for s in range(2):
-                v = part[s, b, m, sl, :].astype(F32) + sib[s, b, sl, :].astype(F32)
-                for way, j in terms:
-                    v = v + inbox[way, j, s, sl, :].astype(F32)
-                into(s, sl, v)
+            v = part[s, b, m, sl, :].astype(F32) + sib[s, b, sl, :].astype(F32)
+            for way, j in terms:
+                v = v + inbox[way, j, s, sl, :].astype(F32)
+            into(s, sl, v)
             return 0
 
         lax.fori_loop(0, n // 16, rows16, 0)
@@ -191,52 +218,56 @@
         out[s, sl, :] = v
 
     for d in (3, 2, 0, 1):
-        cross(d).start()
+        for s in range(2):
+            cross(d, s).start()
     yield
     for d, j in ((3, 0), (2, 1)):
-        cross(d).wait_recv()
-        for lvl in range(2):
-            def go():
-                if lvl == 1:
-                    msg(0, j).wait_recv()
-                add(d, put(j), [(da, j)] if lvl else [])
-                msg(0, j).start()
-            pl.when(u == lvl)(go)
+        for s in range(2):
+            cross(d, s).wait_recv()
+            for lvl in range(2):
+                def go():
+                    if lvl == 1:
+                        msg(0, j, s).wait_recv()
+                    add(d, s, put(j), [(da, j)] if lvl else [])
+                    msg(0, j, s).start()
+                pl.when(u == lvl)(go)
         yield
-    cross(0).wait_recv()
-    cross(1).wait_recv()
-
-    def first():
-        add(1, put(2), [])
-        msg(0, 2).start()
-
-    pl.when(u == 0)(first)
-
-    def back():
-        msg(1, 0).wait_recv()
-        add(0, put(2), [(1 - da, 0)])
-        msg(1, 0).start()
-
-    pl.when(u == 1)(back)
+    for s in range(2):
+        cross(0, s).wait_recv()
+        cross(1, s).wait_recv()
+
+        def first():
+            add(1, s, put(2), [])
+            msg(0, 2, s).start()
+
+        pl.when(u == 0)(first)
+
+        def back():
+            msg(1, 0, s).wait_recv()
+            add(0, s, put(2), [(1 - da, 0)])
+            msg(1, 0, s).start()
+
+        pl.when(u == 1)(back)
     yield
-
-    def end0():
-        msg(1, 0).wait_recv()
-        add(0, final, [(1 - da, 0)])
-
-    def end1():
-        msg(0, 2).wait_recv()
-        msg(1, 1).wait_recv()
-        add(1, final, [(da, 2), (1 - da, 1)])
-
-    pl.when(u == 0)(end0)
-    pl.when(u == 1)(end1)
-    for d in range(TP):
-        cross(d).wait_send()
-    for j in range(2):
-        msg(0, j).wait_send()
-    pl.when(u == 0)(lambda: msg(0, 2).wait_send())
-    pl.when(u == 1)(lambda: msg(1, 0).wait_send())
+    for s in range(2):
+        def end0():
+            msg(1, 0, s).wait_recv()
+            add(0, s, final, [(1 - da, 0)])
+
+        def end1():
+            msg(0, 2, s).wait_recv()
+            msg(1, 1, s).wait_recv()
+            add(1, s, final, [(da, 2), (1 - da, 1)])
+
+        pl.when(u == 0)(end0)
+        pl.when(u == 1)(end1)
+    for s in range(2):
+        for d in range(TP):
+            cross(d, s).wait_send()
+        for j in range(2):
+            msg(0, j, s).wait_send()
+        pl.when(u == 0)(lambda: msg(0, 2, s).wait_send())
+        pl.when(u == 1)(lambda: msg(1, 0, s).wait_send())
 
 
 def inner(t):
@@ -245,10 +276,6 @@
 
 def outer(t):
     return (t == 0) | (t == TP - 1)
-
-
-def fifth(t):
-    return t == 1
 
 
 def cut(width, t):
@@ -289,13 +316,20 @@
         each_kind(c.t, (c.t + o) % TP, lambda k: copy(o, k).wait_send())
 
 
-def plane_gather(c, block, order, own=None):
+def only(cond, f):
+    if cond is None:
+        f()
+    else:
+        pl.when(cond)(f)
+
+
+def plane_gather(c, block, order, own=None, cond=None):
     have = [0]
     done = []
     held = None
     if own is not None:
         held = c.local(own, block(c.g), c.slot())
-        held.start()
+        only(cond, lambda: held.start())
     for b in order:
         dev = c.at(g=c.flip(c.g, b))
         sent = []
@@ -305,21 +339,18 @@
                 if x & bit:
                     gg = c.flip(gg, bit)
             src = own if own is not None and x == 0 else block(gg)
-            copy = c.to(src, block(gg), dev, c.slot())
-            copy.start()
-            sent.append(copy)
+            sent.append(c.to(src, block(gg), dev, c.slot()))
+        only(cond, lambda: [copy.start() for copy in sent] and None)
         yield
-        for copy in sent:
-            copy.wait_recv()
+        only(cond, lambda: [copy.wait_recv() for copy in sent] and None)
         done += sent
         have = have + [x ^ b for x in have]
-    for copy in done:
-        copy.wait_send()
+    only(cond, lambda: [copy.wait_send() for copy in done] and None)
     if held is not None:
-        held.wait()
-
-
-def plane_reduce(c, own, sums, inbox, order):
+        only(cond, lambda: held.wait())
+
+
+def plane_reduce(c, own, sums, inbox, order, cond=None):
     def place(x):
         gg = c.g
         for bit in c.bits:
@@ -335,33 +366,34 @@
         dev = c.at(g=c.flip(c.g, b))
         away = [x for x in left if x & b]
         left = [x for x in left if not x & b]
-        sent = []
-        for i, x in enumerate(away):
-            src = own(place(x)) if k == 0 else sums.at[spot[x]]
-            copy = c.to(src, inbox.at[base + i], dev, c.slot())
-            copy.start()
-            sent.append(copy)
-        held = []
         if k == 0:
             spot = {x: i for i, x in enumerate(left)}
-            for x in left:
-                held.append(c.local(own(place(x)), sums.at[spot[x]], c.slot()))
-                held[-1].start()
+        sent = [c.to(own(place(x)) if k == 0 else sums.at[spot[x]], inbox.at[base + i], dev, c.slot()) for i, x in enumerate(away)]
+        held = [c.local(own(place(x)), sums.at[spot[x]], c.slot()) for x in left] if k == 0 else []
+
+        def begin():
+            for copy in sent + held:
+                copy.start()
+
+        only(cond, begin)
         yield
-        for i, x in enumerate(left):
-            sent[i].wait_recv()
-            if k == 0:
-                held[i].wait()
-            add_blocks(sums.at[spot[x]], inbox.at[base + i])
+
+        def take():
+            for i, x in enumerate(left):
+                sent[i].wait_recv()
+                if k == 0:
+                    held[i].wait()
+                add_blocks(sums.at[spot[x]], inbox.at[base + i])
+
+        only(cond, take)
         base += len(away)
         done += sent
-    for copy in done:
-        copy.wait_send()
+    only(cond, lambda: [copy.wait_send() for copy in done] and None)
 
 
 def add_blocks(a, b):
     def one(i, _):
-        a[i] = (a[i].astype(F32) + b[i].astype(F32)).astype(BF)
+        a[i] = a[i] + b[i]
         return 0
 
     lax.fori_loop(0, a.shape[0], one, 0)
@@ -382,14 +414,14 @@
 VM = pl.BlockSpec(memory_space=pltpu.VMEM)
 
 
-def heads_to(ref, dst, extra):
+def heads_to(c, ref, dst, extra):
     def src(t, k):
         return ref.at[:, pl.ds(1024, 256)] if extra else ref.at[:, pl.ds(pl.multiple_of(t * 256, 256), 256)]
 
     def into(t, k):
         return dst(t).at[:, pl.ds(256 if extra else 0, 256)]
 
-    return src, into, (((fifth, 0),) if extra else ((None, 0),))
+    return src, into, (((c.fifth, 0),) if extra else ((None, 0),))
 
 
 def units_to(ref, dst):
@@ -418,14 +450,14 @@
     return src, into, ((inner, big), (outer, small)), "from"
 
 
-def heads_out(ref, dst, extra):
+def heads_out(c, ref, dst, extra):
     def src(t, k):
         return ref(t).at[:, pl.ds(256 if extra else 0, 256)]
 
     def into(t, k):
         return dst.at[:, pl.ds(1024, 256)] if extra else dst.at[:, pl.ds(pl.multiple_of(t * 256, 256), 256)]
 
-    return src, into, (((fifth, 0),) if extra else ((None, 0),)), "from"
+    return src, into, (((c.fifth, 0),) if extra else ((None, 0),)), "from"
 
 
 def start_kernel(x, gain, wbr, wot, gates, full_a, wb0, wb1, wop, gb, own, zero, send, recv):
@@ -435,41 +467,39 @@
     z = []
     for extra in (False, True):
         for k in range(2):
-            z.append(spread_z(c, *heads_to(wbr.at[k], lambda t, k=k: wb[k].at[t, c.g], extra)))
+            z.append(spread_z(c, *heads_to(c, wbr.at[k], lambda t, k=k: wb[k].at[t, c.g], extra)))
     z.append(spread_z(c, lambda t, k: gates.at[:, t], lambda t, k: gb.at[:, 0, t, c.g]))
-    z.append(spread_z(c, lambda t, k: gates.at[:, 4], lambda t, k: gb.at[:, 1, t, c.g], ((fifth, 0),)))
+    z.append(spread_z(c, lambda t, k: gates.at[:, 4], lambda t, k: gb.at[:, 1, t, c.g], ((c.fifth, 0),)))
     for f in z:
         next(f)
     for s in range(2):
         v = x[s].astype(F32)
         own[s] = (v * lax.rsqrt(jnp.mean(v * v, axis=-1, keepdims=True) + EPS) * gain[...]).astype(BF)
-    ag = ag_flow(c, own, full_a)
-    next(ag)
-    z2 = [spread_z(c, *heads_to(wot, lambda t: wop.at[t], extra)) for extra in (False, True)]
-    for f in z2:
-        next(f)
     zero[...] = jnp.zeros_like(zero)
-    fills = [(zero, wb[k].at[:, c.g, :, pl.ds(256, 256)], c.slot()) for k in range(2)]
-    fills.append((zero, wop.at[:, :, pl.ds(256, 256)], c.slot()))
-    for k in range(2):
-        fills.append((zero.at[:, pl.ds(0, gates.shape[2])], gb.at[k, 1, :, c.g], c.slot()))
-
-    def fill():
-        for f in fills:
-            c.local(*f).start()
-        for f in fills:
-            c.local(*f).wait()
-
-    pl.when(c.t != 1)(fill)
+    fills = [(zero, wb[k].at[:, g, :, pl.ds(256, 256)], c.slot()) for k in range(2) for g in range(c.ng)]
+    fills += [(zero.at[:, pl.ds(0, gates.shape[2])], gb.at[k, 1, :, g], c.slot()) for k in range(2) for g in range(c.ng)]
+    idle = jnp.logical_not(c.fifth())
+    pl.when(idle)(lambda: [c.local(*f).start() for f in fills] and None)
     for f in z:
         next(f)
     fwd, rev = c.bits, c.bits[::-1]
-    g1 = [plane_gather(c, lambda g: wb0.at[:, g], fwd), plane_gather(c, lambda g: wb1.at[:, g], rev),
-          plane_gather(c, lambda g: gb.at[0, :, :, g], fwd), plane_gather(c, lambda g: gb.at[1, :, :, g], rev)]
+    g1 = []
+    for h in range(2):
+        for k, order in ((0, fwd), (1, rev)):
+            g1.append(plane_gather(c, lambda g, k=k, h=h: wb[k].at[:, g, :, pl.ds(256 * h, 256)], order, None, c.fifth() if h else None))
+            g1.append(plane_gather(c, lambda g, k=k, h=h: gb.at[k, h, :, g], order, None, c.fifth() if h else None))
+    for f in g1:
+        next(f)
+    ag = ag_flow(c, own, full_a)
+    next(ag)
+    z2 = [spread_z(c, *heads_to(c, wot, lambda t: wop.at[t], extra)) for extra in (False, True)]
     for f in g1:
         next(f)
     next(ag)
-    run(*g1, ag, *z, *z2)
+    for f in z2:
+        next(f)
+    run(ag, *g1, *z, *z2)
+    pl.when(idle)(lambda: [c.local(*f).wait() for f in fills] and None)
 
 
 def start_call(x, gain, wbr, wot, gates):
@@ -483,53 +513,58 @@
         [VM, VM, HBM, HBM, HBM],
         (HBM,) * 5,
         [pltpu.VMEM((2, n, d), BF), pltpu.VMEM((TP, r, 256), BF)],
-        1,
+        1, 256,
     )(x, gain[None], wbr, wot, gates)
+
+
+MID_LATE = False
+MID_ORDER = "r0yar0ay1arNz1aAz2A2"
 
 
 def mid_kernel(part, x, go, gain, p0, m1, m2, zero, res, full, full_g, w0, w1, w2, tot, own, sib, inbox, outbox, send, recv):
     c = Comm(send, recv)
     c.barrier()
     fwd, rev = c.bits, c.bits[::-1]
-    rs = rs_flow(c, part, tot, sib, inbox, outbox)
-    next(rs)
     pad = zero.shape[2]
     fills = [(zero, w.at[:, c.g, :, pl.ds(w.shape[3] - pad, pad)], c.slot()) for w in (w1, w2)]
 
-    def fill():
-        for f in fills:
-            c.local(*f).start()
-        for f in fills:
-            c.local(*f).wait()
-
-    g0 = plane_gather(c, lambda g: w0.at[:, g], fwd, p0)
-    next(g0)
+    def gather(w, own=None):
+        for k, order in ((0, fwd), (1, rev)):
+            at = pl.ds(2 * k, 2)
+            yield plane_gather(c, lambda g, at=at: w.at[at, g], order, None if own is None else own.at[at])
+
+    last = len(c.bits) - 1
+    rs = rs_flow(c, part, tot, sib, inbox, outbox)
+    ag, ag2 = ag_flow(c, own, full), ag_flow(c, go, full_g, MID_LATE)
     z1 = spread_z(c, *units_to(m1, lambda t: w1.at[t, c.g]))
-    next(z1)
-    pl.when(outer(c.t))(fill)
     z2 = spread_z(c, *units_to(m2, lambda t: w2.at[t, c.g]))
-    next(rs)
-    next(z2)
-    next(rs)
-    next(z1)
-    g1 = plane_gather(c, lambda g: w1.at[:, g], rev)
-    next(g1)
-    next(rs)
-    next(g0)
-    next(z2)
-    half = [plane_gather(c, lambda g: w2.at[pl.ds(0, 2), g], fwd), plane_gather(c, lambda g: w2.at[pl.ds(2, 2), g], rev)]
-    for f in half:
-        next(f)
-    run(rs)
-    for s in range(2):
-        v = x[s].astype(F32) + tot[s]
-        res[s] = v
-        own[s] = (v * lax.rsqrt(jnp.mean(v * v, axis=-1, keepdims=True) + EPS) * gain[...]).astype(BF)
-    ag = ag_flow(c, own, full)
-    next(ag)
-    ag2 = ag_flow(c, go, full_g)
-    next(ag2)
-    run(g1, ag, *half, ag2, g0, z1, z2)
+    g = [list(gather(w0, p0)), list(gather(w1)), list(gather(w2))]
+
+    def norm():
+        finish(rs)
+        for s in range(2):
+            v = x[s].astype(F32) + tot[s]
+            res[s] = v
+            own[s] = (v * lax.rsqrt(jnp.mean(v * v, axis=-1, keepdims=True) + EPS) * gain[...]).astype(BF)
+        step(ag)
+
+    begun = [0, 0, 0]
+
+    def plane(k):
+        if not begun[k]:
+            step(*g[k])
+        else:
+            for _ in range(last):
+                step(*g[k])
+        begun[k] = 1
+
+    does = {"r": lambda: step(rs), "N": norm, "A": lambda: step(ag), "a": lambda: step(ag2), "y": lambda: step(z1), "z": lambda: step(z2),
+            "0": lambda: plane(0), "1": lambda: plane(1), "2": lambda: plane(2)}
+    for i, what in enumerate(MID_ORDER):
+        does[what]()
+        if i == 4:
+            pl.when(outer(c.t))(lambda: [c.local(*f).start() for f in fills] and [c.local(*f).wait() for f in fills] and None)
+    finish(ag, ag2, *g[0], *g[1], *g[2], z1, z2)
 
 
 def mid_call(part, x, go, gain, p0, m1, m2):
@@ -550,18 +585,30 @@
     )(part.reshape(2, TP, 2, n, d), x, go, gain[None], p0, m1, m2, zero)
 
 
-def back_kernel(part, part2, res, go, gain, h0, h1, h2, gres, gsum, mlp_own, full, o0, r1, r2,
+def back_kernel(part, part2, res, go, gain, h0, h1, h2, gres, gsum, mlp_own, full, o0, o1, r2,
                 tot, own, sib, inbox, outbox, sib2, inbox2, outbox2, su, ib, send, recv):
     c = Comm(send, recv)
     c.barrier()
     fwd, rev = c.bits, c.bits[::-1]
     rs = rs_flow(c, part, tot, sib, inbox, outbox)
     next(rs)
-    red = [plane_reduce(c, lambda g, h=h: h.at[:, g], su.at[k], ib.at[k], (fwd, rev, fwd)[k]) for k, h in enumerate((h0, h1, h2))]
-    for f in red[:2]:
-        next(f)
+    red = []
+    for k, h in enumerate((h0, h1, h2)):
+        red.append([plane_reduce(c, lambda g, h=h, q=q: h.at[pl.ds(2 * q, 2), g], su.at[2 * k + q], ib.at[2 * k + q], (fwd, rev)[q]) for q in range(2)])
+    last = len(c.bits) - 1
+
+    def onward(parts):
+        for _ in range(last):
+            step(*parts)
+
+    step(*red[0])
+    step(rs)
+    step(*red[1])
+    onward(red[0])
+    step(rs)
+    step(rs)
     rs2 = rs_flow(c, part2, mlp_own, sib2, inbox2, outbox2)
-    run(rs)
+    finish(rs)
     total = jnp.zeros_like(gsum)
     for s in range(2):
         v = res[s]
@@ -575,41 +622,32 @@
         own[s] = gr.astype(BF)
     gsum[...] = total
     ag = ag_flow(c, own, full)
-    next(ag)
-    next(rs2)
-    next(red[2])
-    next(red[0])
-    next(rs2)
-    next(ag)
-    next(red[1])
-    next(rs2)
-    next(ag)
-    for f in red[2:] + red[:1]:
-        for _ in range(len(c.bits) - 1 if f is red[2] else len(c.bits) - 2):
-            next(f)
-    for f in red[1:2]:
-        for _ in range(len(c.bits) - 2):
-            next(f)
-    next(rs2)
-    finish(red[0])
-    s0 = spread_z(c, *units_back(lambda t: su.at[0, 0, t], o0))
-    next(s0)
-    finish(ag)
-    finish(rs2)
-    finish(red[1])
-    l1 = c.local(su.at[1, 0], r1, c.slot())
-    l1.start()
-    finish(red[2])
-    l2 = c.local(su.at[2, 0], r2, c.slot())
-    l2.start()
-    run(s0)
-    l1.wait()
-    l2.wait()
-
-
-def finish(f):
-    for _ in f:
-        pass
+    step(ag, rs2)
+    finish(*red[0])
+    s0 = spread_z(c, *units_back(lambda t: su.at[t // 2, 0, t % 2], o0))
+    step(s0)
+    step(*red[2])
+    onward(red[1])
+    step(ag, rs2)
+    held = []
+
+    def keep(k, out):
+        finish(*red[k])
+        for q in range(2):
+            held.append(c.local(su.at[2 * k + q, 0], out.at[pl.ds(2 * q, 2)], c.slot()))
+            held[-1].start()
+
+    step(ag, rs2)
+    onward(red[2])
+    finish(*red[1])
+    s1 = spread_z(c, *units_back(lambda t: su.at[2 + t // 2, 0, t % 2], o1))
+    step(s1)
+    step(rs2)
+    finish(ag, rs2)
+    keep(2, r2)
+    finish(s0, s1)
+    for h in held:
+        h.wait()
 
 
 def back_call(part, part2, res, go, gain, h0, h1, h2, units):
@@ -619,11 +657,11 @@
     shape = (2, TP, 2, n, d)
     return call(
         back_kernel,
-        (S((2, n, d), F32), S((1, d), F32), S((2, n, d), F32), S(shape, BF), S((r, units), BF), S((TP, r, fs), BF), S((TP, r, fs), BF)),
+        (S((2, n, d), F32), S((1, d), F32), S((2, n, d), F32), S(shape, BF), S((r, units), BF), S((r, units), BF), S((TP, r, fs), BF)),
         [VM] * 5 + [HBM] * 3,
         (VM, VM, VM, HBM, HBM, HBM, HBM),
         [pltpu.VMEM((2, n, d), F32), pltpu.VMEM((2, n, d), BF)] + rs_scratch(n, d) + rs_scratch(n, d)
-        + [pltpu.VMEM((3, ng // 2, TP, r, fs), BF), pltpu.VMEM((3, ng - 1, TP, r, fs), BF)],
+        + [pltpu.VMEM((6, ng // 2, 2, r, fs), BF), pltpu.VMEM((6, ng - 1, 2, r, fs), BF)],
         3, 256,
     )(part.reshape(shape), part2.reshape(shape), res, go, gain[None], h0, h1, h2)
 
@@ -649,34 +687,30 @@
     gains[...] = sbox[0] + sbox[1]
 
 
-def end_kernel(part, x, gres, gain, gwb0, gwb1, ggb, rwo, r2, gain_b, chan_rows, gin, gains, table, owb, owo, ogb, o2,
+def end_kernel(part, x, gres, gain, gwb0, gwb1, ggb, rwo, gain_b, chan_rows, gin, gains, table, owb, owo, ogb,
                small, small_in, zbox, sbox, tot, sib, inbox, outbox, su_x, in_x, su_g, in_g, send, recv):
     c = Comm(send, recv)
     c.barrier()
     fwd, rev = c.bits, c.bits[::-1]
     red, spread = [], []
-    for k, gw in enumerate((gwb0, gwb1)):
-        red.append(plane_reduce(c, lambda g, gw=gw: gw.at[:, g], su_x.at[k], in_x.at[k], rev if k else fwd))
-        for extra in (False, True):
-            spread.append((k, spread_z(c, *heads_out(lambda t, k=k: su_x.at[k, 0, t], owb.at[k], extra))))
-    for k in range(2):
-        for h in range(2):
-            i = 2 * k + h
-            red.append(plane_reduce(c, lambda g, k=k, h=h: ggb.at[k, h, :, g], su_g.at[i], in_g.at[i], fwd if k else rev))
-            spread.append((2 + i, spread_z(
-                c, lambda t, q, i=i: su_g.at[i, 0, t], lambda t, q, k=k, h=h: ogb.at[k, 4 if h else t],
-                ((fifth, 0),) if h else ((None, 0),), "from")))
+    for h in range(2):
+        for k, gw in enumerate((gwb0, gwb1)):
+            i, order, cond = 2 * h + k, rev if k else fwd, c.fifth() if h else None
+            red.append(plane_reduce(c, lambda g, gw=gw, h=h: gw.at[:, g, :, pl.ds(256 * h, 256)], su_x.at[i], in_x.at[i], order, cond))
+            lane = (lambda t: pl.ds(1024, 256)) if h else (lambda t: pl.ds(pl.multiple_of(t * 256, 256), 256))
+            which = ((c.fifth, 0),) if h else ((None, 0),)
+            spread.append((len(red) - 1, spread_z(c, lambda t, q, i=i: su_x.at[i, 0, t], lambda t, q, k=k, lane=lane: owb.at[k, :, lane(t)], which, "from")))
+            red.append(plane_reduce(c, lambda g, k=k, h=h: ggb.at[k, h, :, g], su_g.at[i], in_g.at[i], order, cond))
+            spread.append((len(red) - 1, spread_z(c, lambda t, q, i=i: su_g.at[i, 0, t], lambda t, q, k=k, h=h: ogb.at[k, 4 if h else t], which, "from")))
     rs = rs_flow(c, part, tot, sib, inbox, outbox)
     next(rs)
     for f in red:
         next(f)
-    z0 = [spread_z(c, *units_back(lambda t: r2.at[t], o2))]
+    z0 = []
     for extra in (False, True):
-        z0.append(spread_z(c, *heads_out(lambda t: rwo.at[t], owo, extra)))
-    next(rs)
-    for f in z0:
-        next(f)
+        z0.append(spread_z(c, *heads_out(c, lambda t: rwo.at[t], owo, extra)))
     finish(rs)
+    step(*z0)
     total = jnp.zeros_like(gain)
     for s in range(2):
         v = x[s].astype(F32)
@@ -705,7 +739,7 @@
     run(sm, *z0, *[z for _, z in spread])
 
 
-def end_call(part, x, gres, gain, gwb0, gwb1, ggb, rwo, r2, gain_b, chan_rows, units):
+def end_call(part, x, gres, gain, gwb0, gwb1, ggb, rwo, gain_b, chan_rows):
     _, n, d = x.shape
     ng = lax.axis_size("dp") // TP
     r, gr, steps = gwb0.shape[2], ggb.shape[4], (lax.axis_size("dp") // TP).bit_length()
@@ -716,20 +750,20 @@
 
     return call(
         end_kernel,
-        (S((2, n, d), F32), S((8, d), F32), S((TP, 8, 512), F32), S((2, r, 1280), BF), S((r, 1280), BF), S((2, 5, gr, 256), BF), S((r, units), BF)),
-        [VM] * 4 + [HBM] * 5 + [VM] * 2,
-        (VM,) * 3 + (HBM,) * 4,
+        (S((2, n, d), F32), S((8, d), F32), S((TP, 8, 512), F32), S((2, r, 1280), BF), S((r, 1280), BF), S((2, 5, gr, 256), BF)),
+        [VM] * 4 + [HBM] * 4 + [VM] * 2,
+        (VM,) * 3 + (HBM,) * 3,
         [pltpu.VMEM((steps, 16, d), F32), pltpu.VMEM((steps - 1, 16, d), F32), pltpu.VMEM((TP, 16, d), F32), pltpu.VMEM((2, 8, d), F32),
-         pltpu.VMEM((2, n, d), F32)] + rs_scratch(n, d) + sets(2, r, 512) + sets(4, gr, 256),
+         pltpu.VMEM((2, n, d), F32)] + rs_scratch(n, d) + sets(4, r, 256) + sets(4, gr, 256),
         4, 256,
-    )(part.reshape(2, TP, 2, n, d), x, gres, gain[None], gwb0, gwb1, ggb, rwo, r2, gain_b, chan_rows)
+    )(part.reshape(2, TP, 2, n, d), x, gres, gain[None], gwb0, gwb1, ggb, rwo, gain_b, chan_rows)
 
 
 def heads_of(a, axis):
     _, _, t, _ = plan()
     p = lax.dynamic_slice_in_dim(a, t * 256, 256, axis)
     q = lax.dynamic_slice_in_dim(a, 1024, 256, axis)
-    q = jnp.where(t == 1, q, jnp.zeros_like(q))
+    q = jnp.where(t == 1 + lax.axis_index("mp"), q, jnp.zeros_like(q))
     return jnp.concatenate([p, q], axis)
 
 
@@ -784,15 +818,14 @@
 
 
 def share(c, table):
-    copies = []
-    for o in range(1, c.ng):
-        slot = c.slot()
-        copies.append((o, slot))
+    slots = [c.slot() for _ in range(1, c.ng)]
+    for o, slot in enumerate(slots, 1):
         c.to(table.at[c.g], table.at[c.g], c.at(g=(c.g + o) % c.ng), slot).start()
-    for o, slot in copies:
+    yield
+    for o, slot in enumerate(slots, 1):
         frm = (c.g + c.ng - o) % c.ng
         c.to(table.at[frm], table.at[frm], c.at(g=frm), slot).wait_recv()
-    for o, slot in copies:
+    for o, slot in enumerate(slots, 1):
         c.to(table.at[c.g], table.at[c.g], c.at(g=(c.g + o) % c.ng), slot).wait_send()
 
 
@@ -809,22 +842,43 @@
     return jnp.concatenate(rows, axis=0)
 
 
-def mix_fwd_kernel(br0, ci, gb, chan, db, wop, m0, zero, mixed, conv, gates, state, rim, carry, table, wo, p0, a_ref, d_ref, ext, rim_in, send, recv):
+def mix_fwd_kernel(na, wb0, wb1, gb, chan, db, wop, m0, zero, blank, mixed, conv, gates, state, rim, carry, table, br0, ci, wo, p0, a_ref, d_ref, ext, rim_in, send, recv):
     c = Comm(send, recv)
     greet(plane_partners(c) + line_partners(c))
     n, width = ci.shape[1], ci.shape[2]
-    rslot = c.slot()
-    out = c.to(ci.at[:, pl.ds(n - 16, 16)], rim_in, c.at(g=(c.g + 1) % c.ng), rslot)
-    out.start()
     z0 = spread_z(c, *units_to(m0, lambda t: p0.at[t]))
     next(z0)
     fwd, rev = c.bits, c.bits[::-1]
-    g0 = [plane_gather(c, lambda g: wo.at[pl.ds(0, 2), g], fwd, wop.at[pl.ds(0, 2)]), plane_gather(c, lambda g: wo.at[pl.ds(2, 2), g], rev, wop.at[pl.ds(2, 2)])]
-    for f in g0:
-        next(f)
+    g0 = []
+    for h in range(2):
+        for q, order in ((0, fwd), (1, rev)):
+            at, lane = pl.ds(2 * q, 2), pl.ds(256 * h, 256)
+            g0.append(plane_gather(c, lambda g, at=at, lane=lane: wo.at[at, g, :, lane], order, wop.at[at, :, lane], c.fifth() if h else None))
+    step(*g0)
+    fills = [c.local(blank, wo.at[:, g, :, pl.ds(256, 256)], c.slot()) for g in range(c.ng)]
+    idle = jnp.logical_not(c.fifth())
+    pl.when(idle)(lambda: [f.start() for f in fills] and None)
     pad = zero.shape[2]
     fill = c.local(zero, p0.at[:, :, pl.ds(p0.shape[2] - pad, pad)], c.slot())
     pl.when(outer(c.t))(lambda: fill.start())
+
+    def branch(i, _):
+        rows = pl.ds(pl.multiple_of(i * 2 * n, 2 * n), 2 * n)
+        v = jnp.dot(na[rows, :], wb1[...], preferred_element_type=F32).astype(BF)
+        ci[2 * i] = v[:n]
+        ci[2 * i + 1] = v[n:]
+        return 0
+
+    lax.fori_loop(0, TP, branch, 0)
+    out = c.to(ci.at[:, pl.ds(n - 16, 16)], rim_in, c.at(g=(c.g + 1) % c.ng), c.slot())
+    out.start()
+
+    def gate(i, _):
+        rows = pl.ds(pl.multiple_of(i * 2 * n, 2 * n), 2 * n)
+        br0[rows, :] = jnp.dot(na[rows, :], wb0[...], preferred_element_type=F32)
+        return 0
+
+    lax.fori_loop(0, TP, gate, 0)
     out.wait()
     row = lax.broadcasted_iota(jnp.int32, (n, 1), 0)
     for b in range(2 * TP):
@@ -863,9 +917,11 @@
     h = jnp.concatenate([v[1] for v in ph], axis=1)
     table[c.g, 0] = p
     table[c.g, 1] = h
+    sh = share(c, table)
+    next(sh)
     for f in g0:
         next(f)
-    share(c, table)
+    finish(sh)
     cin = entering(c, lambda g: table[g, 0], lambda g: table[g, 1], width, False)
     carry[...] = cin
 
@@ -884,11 +940,12 @@
         mixed[rows, :] = (v * gelu_pair(br0[rows, :])[0]).astype(BF)
     run(*g0, z0)
     pl.when(outer(c.t))(lambda: fill.wait())
-
-
-def mix_fwd_call(br0, ci, gb, chan, db, wop, m0):
+    pl.when(idle)(lambda: [f.wait() for f in fills] and None)
+
+
+def mix_fwd_call(na, wb0, wb1, gb, chan, db, wop, m0):
     ng = lax.axis_size("dp") // TP
-    rows, width = br0.shape
+    rows, width = na.shape[0], wb0.shape[1]
     n = rows // (2 * TP)
     r = m0.shape[0]
     _, big, small = cut(m0.shape[1], 0)
@@ -896,25 +953,36 @@
     return call(
         mix_fwd_kernel,
         (S((rows, width), BF), S((rows, width), BF), S((2, rows, width), F32), S((rows, width), F32),
-         S((2 * TP, 8, width), F32), S((2 * TP, width), F32), S((ng, 2, 2 * TP, width), F32), S((TP, ng, r, width), BF), S((TP, r, big), BF)),
-        [VM] * 5 + [HBM, HBM, VM],
-        (VM,) * 7 + (HBM, HBM),
+         S((2 * TP, 8, width), F32), S((2 * TP, width), F32), S((ng, 2, 2 * TP, width), F32), S((rows, width), F32), S((2 * TP, n, width), BF), S((TP, ng, r, width), BF), S((TP, r, big), BF)),
+        [VM] * 6 + [HBM, HBM, VM, VM],
+        (VM,) * 9 + (HBM, HBM),
         [pltpu.VMEM((width // 128, rows, 128), F32), pltpu.VMEM((width // 128, rows, 128), F32), pltpu.VMEM((2, n + 8, width), F32), pltpu.VMEM((2 * TP, 16, width), BF)],
         5, 128,
-    )(br0, ci.reshape(2 * TP, n, width), gb, chan, db[None], wop, m0, jnp.zeros((TP, r, big - small), BF))
-
-
-def mix_bwd_kernel(gm, br0, ci, gb, chan, db, conv, gates, state, rim, carry, table, gwo, r1, gbr, ggb, sums, rwo, o1,
-                   a_ref, adj, gc, gpl, ext, heads, etab, rim_in, su, ib, send, recv):
+    )(na, wb0, wb1, gb, chan, db[None], wop, m0, jnp.zeros((TP, r, big - small), BF), jnp.zeros((TP, r, 256), BF))
+
+
+def mix_bwd_kernel(gmo, wo, wb0, wb1, br0, ci, gb, chan, db, conv, gates, state, rim, carry, table, gwo, r1, gbr, ggb, sums, gna, rwo, o1,
+                   gm, a_ref, adj, gc, gpl, ext, heads, etab, rim_in, su, ib, send, recv):
     c = Comm(send, recv)
     greet(plane_partners(c) + line_partners(c))
     n, width = ci.shape[1], ci.shape[2]
     z0 = spread_z(c, *units_back(lambda t: r1.at[t], o1))
     next(z0)
     fwd, rev = c.bits, c.bits[::-1]
-    red = [plane_reduce(c, lambda g, k=k: gwo.at[pl.ds(2 * k, 2), g], su.at[k], ib.at[k], rev if k else fwd) for k in range(2)]
+    red = []
+    for h in range(2):
+        for q, order in ((0, fwd), (1, rev)):
+            i = 2 * h + q
+            red.append(plane_reduce(c, lambda g, h=h, q=q: gwo.at[pl.ds(2 * q, 2), g, :, pl.ds(256 * h, 256)], su.at[i], ib.at[i], order, c.fifth() if h else None))
     for f in red:
         next(f)
+
+    def product(i, _):
+        rows = pl.ds(pl.multiple_of(i * 2 * n, 2 * n), 2 * n)
+        gm[rows, :] = jnp.dot(gmo[rows, :], wo[...], preferred_element_type=F32)
+        return 0
+
+    lax.fori_loop(0, TP, product, 0)
     for b in range(2 * TP):
         rows = pl.ds(b * n, n)
         act, slope = gelu_pair(br0[rows, :])
@@ -930,10 +998,12 @@
     e = lax.fori_loop(0, n, step1, [jnp.zeros((2 * TP, 128), F32)] * (width // 128), unroll=8)
     e = jnp.concatenate(e, axis=1)
     etab[c.g] = e
-    share(c, etab)
+    sh = share(c, etab)
+    next(sh)
     for f in red:
         for _ in range(len(c.bits) - 1):
             next(f)
+    finish(sh)
     ein = entering(c, lambda g: table[g, 0], lambda g: etab[g], width, True)
 
     def step2(i, es):
@@ -993,17 +1063,25 @@
         for k in range(1, 4):
             v = v + chan[k:k + 1] * gc[b, pl.ds(k, n), :]
         gbr[1, rows, :] = v.astype(BF)
+
+    def onto(i, _):
+        rows = pl.ds(pl.multiple_of(i * 2 * n, 2 * n), 2 * n)
+        v = [lax.dot_general(gbr[k, rows, :], w[...], (((1,), (1,)), ((), ())), preferred_element_type=F32) for k, w in enumerate((wb0, wb1))]
+        gna[rows, :] = (v[0] + v[1]).astype(BF)
+        return 0
+
+    lax.fori_loop(0, TP, onto, 0)
     held = []
-    for k, f in enumerate(red):
+    for i, f in enumerate(red):
         finish(f)
-        held.append(c.local(su.at[k, 0], rwo.at[pl.ds(2 * k, 2)], c.slot()))
-        held[-1].start()
+        held.append(c.local(su.at[i, 0], rwo.at[pl.ds(2 * (i % 2), 2), :, pl.ds(256 * (i // 2), 256)], c.slot()))
+        only(c.fifth() if i >= 2 else None, lambda: held[-1].start())
     run(z0)
-    for h in held:
-        h.wait()
-
-
-def mix_bwd_call(gm, br0, ci, gb, chan, db, saved, gwo, r1, units):
+    for i, h in enumerate(held):
+        only(c.fifth() if i >= 2 else None, lambda: h.wait())
+
+
+def mix_bwd_call(gmo, wo, wb0, wb1, br0, ci, gb, chan, db, saved, gwo, r1, units):
     ng = lax.axis_size("dp") // TP
     rows, width = br0.shape
     n = rows // (2 * TP)
@@ -1012,14 +1090,63 @@
     V = pltpu.VMEM
     return call(
         mix_bwd_kernel,
-        (S((2, rows, width), BF), S((2, 2, 256, 256), F32), S((8, width), F32), S((TP, r, width), BF), S((r, units), BF)),
-        [VM] * 12 + [HBM] * 2,
-        (VM,) * 3 + (HBM,) * 2,
-        [V((width // 128, rows, 128), F32), V((width // 128, rows, 128), F32), V((2 * TP, n + 8, width), F32), V((2, rows, width), BF),
+        (S((2, rows, width), BF), S((2, 2, 256, 256), F32), S((8, width), F32), S(gmo.shape, BF), S((TP, r, width), BF), S((r, units), BF)),
+        [VM] * 15 + [HBM] * 2,
+        (VM,) * 4 + (HBM,) * 2,
+        [V((rows, width), F32), V((width // 128, rows, 128), F32), V((width // 128, rows, 128), F32), V((2 * TP, n + 8, width), F32), V((2, rows, width), BF),
          V((2, n + 8, width), F32), V((2 * TP, 8, width), F32), V((ng, 2 * TP, width), F32), V((2 * TP, 8, width), F32),
-         V((2, ng // 2, 2, r, width), BF), V((2, ng - 1, 2, r, width), BF)],
+         V((4, ng // 2, 2, r, 256), BF), V((4, ng - 1, 2, r, 256), BF)],
         6, 128,
-    )(gm, br0, ci.reshape(2 * TP, n, width), gb, chan, db[None], *saved, gwo, r1)
+    )(gmo, wo, wb0, wb1, br0, ci, gb, chan, db[None], *saved, gwo, r1)
+
+
+def mlp_kernel(nb, go, w0, w1, w2, hidden, gg0, gg1, part, gnb, v0, v1, v2, sems):
+    copies = [pltpu.make_async_copy(a, b, sems.at[k]) for k, (a, b) in enumerate(((w0, v0), (w1, v1), (w2, v2)))]
+    begin = pl.program_id(0) == 0
+
+    @pl.when(begin)
+    def _():
+        for copy in copies:
+            copy.start()
+
+    def ready(k):
+        pl.when(begin)(lambda: copies[k].wait())
+
+    def back(a, w):
+        return lax.dot_general(a, w, (((1,), (1,)), ((), ())), preferred_element_type=F32)
+
+    ready(0)
+    first = jnp.dot(nb[...], v0[...], preferred_element_type=F32)
+    ready(1)
+    second = jnp.dot(nb[...], v1[...], preferred_element_type=F32)
+    act, slope = gelu_pair(first)
+    low = (act * second).astype(BF)
+    hidden[...] = low
+    ready(2)
+    gh = jnp.dot(go[...], v2[...], preferred_element_type=F32)
+    a, b = (gh * second * slope).astype(BF), (gh * act).astype(BF)
+    gg0[...] = a
+    gg1[...] = b
+    gnb[...] = (back(a, v0[...]) + back(b, v1[...])).astype(BF)
+    part[...] = back(low, v2[...]).astype(BF)
+
+
+def mlp_call(nb, go, w0, w1, w2):
+    rows, d = nb.shape
+    fs = w0.shape[1]
+    n = 256
+    S = jax.ShapeDtypeStruct
+    wide = pl.BlockSpec((n, d), lambda i: (i, 0))
+    slim = pl.BlockSpec((n, fs), lambda i: (i, 0))
+    return pl.pallas_call(
+        mlp_kernel,
+        grid=(rows // n,),
+        out_shape=(S((rows, fs), BF),) * 3 + (S((rows, d), BF),) * 2,
+        in_specs=[wide, wide, HBM, HBM, HBM],
+        out_specs=(slim,) * 3 + (wide,) * 2,
+        scratch_shapes=[pltpu.VMEM((d, fs), BF)] * 3 + [pltpu.SemaphoreType.DMA((3,))],
+        compiler_params=pltpu.CompilerParams(vmem_limit_bytes=VMEM_LIMIT),
+    )(nb, go, w0, w1, w2)
 
 
 def dot(a, b, ca, cb):
@@ -1043,37 +1170,27 @@
     na = na.reshape(-1, width)
     wb0, wb1 = wb0.reshape(width, 512), wb1.reshape(width, 512)
     gb = gb.reshape(2, 2, 256, 256)
-    branch0 = dot(na, wb0, 1, 0)
-    conv_input = dot(na, wb1, 1, 0).astype(BF)
-    mixed, *saved, wo, p0 = mix_fwd_call(branch0, conv_input, gb, chan, decay_base, wop, w_mlp[0])
+    mixed, *saved, branch0, conv_input, wo, p0 = mix_fwd_call(na, wb0, wb1, gb, chan, decay_base, wop, w_mlp[0])
     wo = wo.reshape(width, 512)
     residual, nb, go, w0, w1, wd = mid_call(dot(mixed, wo, 1, 1).astype(BF), x, grad_own, norm_gains[1], p0, w_mlp[1], w_down.T)
     nb, go = nb.reshape(-1, width), go.reshape(-1, width)
     w0, w1, wd = w0.reshape(width, fs), w1.reshape(width, fs), wd.reshape(width, fs)
-    first, second = dot(nb, w0, 1, 0), dot(nb, w1, 1, 0)
-    act, act_pull = jax.vjp(jax.nn.gelu, first)
-    hidden = (act * second).astype(BF)
-    mlp_part = dot(hidden, wd, 1, 1).astype(BF)
-    gh = dot(go, wd, 1, 0)
+    hidden, gg0, gg1, mlp_part, gnb = mlp_call(nb, go, w0, w1, wd)
     block = (TP, ng, r, fs)
-    gwd = dot(go, hidden, 0, 0).astype(BF).reshape(block)
-    ggu = [act_pull(gh * second)[0].astype(BF), (gh * act).astype(BF)]
-    gw0, gw1 = [dot(nb, v, 0, 0).astype(BF).reshape(block) for v in ggu]
-    gnb = (dot(ggu[0], w0, 1, 1) + dot(ggu[1], w1, 1, 1)).astype(BF)
-    gres, gain_b, mlp_own, gmo, o0, r1, r2 = back_call(gnb, mlp_part, residual, grad_own, norm_gains[1], gw0, gw1, gwd, units)
+    gwd, gw0, gw1 = [dot(p, q, 0, 0).astype(BF).reshape(block) for p, q in ((go, hidden), (nb, gg0), (nb, gg1))]
+    gres, gain_b, mlp_own, gmo, o0, o1, r2 = back_call(gnb, mlp_part, residual, grad_own, norm_gains[1], gw0, gw1, gwd, units)
     out = jnp.where(valid, residual + mlp_own, 0.0).astype(BF)
     gmo = gmo.reshape(-1, width)
     block = (TP, ng, r, 512)
     gwo = dot(gmo, mixed, 0, 0).astype(BF).reshape(block)
-    gbr, ggb, chan_rows, rwo, o1 = mix_bwd_call(dot(gmo, wo, 1, 0), branch0, conv_input, gb, chan, decay_base, saved, gwo, r1, units)
+    gbr, ggb, chan_rows, gna, rwo, o2 = mix_bwd_call(gmo, wo, wb0, wb1, branch0, conv_input, gb, chan, decay_base, saved, gwo, r2, units)
     gwb0, gwb1 = [dot(na, gbr[k], 0, 0).astype(BF).reshape(block) for k in range(2)]
-    gna = (dot(gbr[0], wb0, 1, 1) + dot(gbr[1], wb1, 1, 1)).astype(BF)
-    gin, gains, table, owb, owo, ogb, o2 = end_call(
-        gna, x, gres, norm_gains[0], gwb0, gwb1, ggb.astype(BF).reshape(2, 2, TP, ng, gr, 256), rwo, r2, gain_b, chan_rows, units,
+    gin, gains, table, owb, owo, ogb = end_call(
+        gna, x, gres, norm_gains[0], gwb0, gwb1, ggb.astype(BF).reshape(2, 2, TP, ng, gr, 256), rwo, gain_b, chan_rows,
     )
     g_wb, g_wo, g_gb = owb.astype(F32), owo.astype(F32).T, ogb.astype(F32)
     g_wm, g_wd = jnp.stack([o0, o1]).astype(F32), o2.astype(F32).T
-    crow = jnp.concatenate([table[i, :, :256] for i in range(TP)] + [table[1, :, 256:]], -1)
+    crow = jnp.concatenate([table[i, :, :256] for i in range(TP)] + [jnp.where(mp == 0, table[1, :, 256:], table[2, :, 256:])], -1)
     return out, gin, gains[:2], g_wb, crow[:7], g_gb, crow[7] * jax.nn.sigmoid(decay_param), g_wo, g_wm, g_wd
 
 

time: 887 us -> 781 us (0.88)
  matrix products: 136 us -> 50.9 us
  Pallas kernels: 710 us -> 690 us
    dot_general x18 -> x7, matrix products: 136 us -> 50.9 us  [dot(): lax.dot_general(a, b, (((ca,), (cb,)), ((), ())), preferred_element_type=...]
    pallas_call x0 -> x1, Pallas kernels: none -> 42.7 us  [mlp_call(): pl.pallas_call(mlp_kernel, grid=(rows // n,), out_shape=(S((rows, fs), BF...]
    pallas_call x1, Pallas kernels: 138 us -> 101 us  [end_call(): call(end_kernel, (S((2, n, d), F32), S((8, d), F32), S((TP, 8, 512), F32)...]
    pallas_call x1, Pallas kernels: 217 us -> 184 us  [mid_call(): call(mid_kernel, (S((2, n, d), F32), S((2, TP, 2, n, d), BF), S((2, TP, 2...]
    pallas_call x1, Pallas kernels: 45.7 us -> 60.8 us  [mix_bwd_call(): call(mix_bwd_kernel, (S((2, rows, width), BF), S((2, 2, 256, 256), F32),...]
where the time goes in v4:
time: 781 us; the launch traced here: 778 us
  Pallas kernels  690 us (88%)
  matrix products  50.9 us (7%)
  other arithmetic  22.2 us (3%)
  local copies, waits for them, and re-layouts  13.1 us (2%)
    pallas_call x1, Pallas kernels, mid_call(): call(mid_kernel, (S((2, n, d), F32), S((2, TP, 2, n, d), BF), S((2, TP, 2...  184 us
    pallas_call x1, Pallas kernels, back_call(): call(back_kernel, (S((2, n, d), F32), S((1, d), F32), S((2, n, d), F32),...  181 us
    pallas_call x1, Pallas kernels, end_call(): call(end_kernel, (S((2, n, d), F32), S((8, d), F32), S((TP, 8, 512), F32)...  101 us
    pallas_call x1, Pallas kernels, start_call(): call(start_kernel, (S((2, TP, 2, n, d), BF), S((TP, ng, r, 512), BF), S((...  80.5 us
    pallas_call x1, Pallas kernels, mix_bwd_call(): call(mix_bwd_kernel, (S((2, rows, width), BF), S((2, 2, 256, 256), F32),...  60.8 us
    dot_general x7, matrix products, dot(): lax.dot_general(a, b, (((ca,), (cb,)), ((), ())), preferred_element_type=...  50.9 us
    pallas_call x1, Pallas kernels, mlp_call(): pl.pallas_call(mlp_kernel, grid=(rows // n,), out_shape=(S((rows, fs), BF...  42.7 us
    pallas_call x1, Pallas kernels, mix_fwd_call(): call(mix_fwd_kernel, (S((rows, width), BF), S((rows, width), BF), S((2, r...  40.3 us

profile of v4, /device:TPU:0, one launch (start us, length us, event | category | flops | bytes accessed | tf_op | source)
XLA Modules:
  0.0 777.6 jit_solution(8918539423552522652)
XLA Ops:
  0.7 0.7 broadcast_compare_fusion
  1.4 0.8 dynamic-slice.3
  2.2 0.7 broadcast_in_dim.40
  2.9 0.6 compare_select_fusion.db
  3.5 0.7 constant_dynamic-slice_fusion
  4.2 0.6 pad_maximum_fusion.chan
  4.8 1.4 fusion.4
  6.2 2.0 broadcast_select_fusion.go
  8.3 3.2 slice_bitcast_fusion
  11.5 80.5 %shard_map.186 = (bf16[2,4,2,64,2560]{4,3,2,1,0:T(8,128)(2,1)}, bf16[4,4,160,512]{3,2,1,0:T(8,128)(2,1)}, bf16[4,4,160,512]{3,2,1,0:T(8,128)(2,1)}, bf16[4,160,5...) custom-call(bf16[2,64,2560]{2,1,0:T(8,128)(2,1)} %x.5, f32[1,2560]{1,0:T(1,128)} %get-tuple-element.107.gain, ...), custom_call_target="tpu_custom_call" | custom-call | tf_op jit(solution)/shard_map/pallas_call | solution.py:510
  92.0 0.7 broadcast_3_zero.2.zero
  92.7 0.7 broadcast_in_dim.42.blank
  93.5 40.3 %shard_map.187 = (bf16[1024,512]{1,0:T(8,128)(2,1)}, bf16[1024,512]{1,0:T(8,128)(2,1)}, f32[2,1024,512]{2,1,0:T(8,128)}, f32[1024,512]{1,0:T(8,128)}, f32[8,8,51...) custom-call(bf16[1024,2560]{1,0:T(8,128)(2,1)} %bitcast.69, ...), custom_call_target="tpu_custom_call" | custom-call | tf_op jit(solution)/shard_map/pallas_call | solution.py:953
  133.8 7.3 convolution_convert_fusion
  141.1 184.3 %shard_map.188 = (f32[2,64,2560]{2,1,0:T(8,128)}, bf16[2,4,2,64,2560]{4,3,2,1,0:T(8,128)(2,1)}, bf16[2,4,2,64,2560]{4,3,2,1,0:T(8,128)(2,1)}, bf16[4,4,160,1024]...) custom-call(bf16[2,4,2,64,2560]{4,3,2,1,0:T(8,128)(2,1)} %bitcast.74, ...), custom_call_target="tpu_custom_call" | custom-call | tf_op jit(solution)/shard_map/pallas_call | solution.py:578
  325.4 0.0 slice-start.2
  325.4 42.7 %shard_map.189 = (bf16[1024,1024]{1,0:T(8,128)(2,1)}, bf16[1024,1024]{1,0:T(8,128)(2,1)}, bf16[1024,1024]{1,0:T(8,128)(2,1)}, bf16[1024,2560]{1,0:T(8,128)(2,1)}, bf16[1024,2560]{1,0:T(8,128)(2,1)}) custom-call(bf16[1024,2560]{1,0:T(8,128)(2,1)} %bitcast.79, bf16[1024,2560]{1,0:T(8,128)(2,1)} %bitcast.85, bf16[2560,1024]{1,0:T(8,128)(2,1)} %bitcast.88, ...), custom_call_target="tpu_custom_call" | custom-call | tf_op jit(solution)/shard_map/pallas_call | solution.py:1141
  368.1 0.0 slice-start.3
  368.1 0.0 copy-start.8
  368.1 10.4 %convolution_convert_fusion.1 = bf16[2560,1024]{1,0:T(8,128)(2,1)} fusion(bf16[1024,2560]{1,0:T(8,128)(2,1)} %bitcast.86, bf16[1024,1024]{1,0:T(8,128)(2,1)} %get-tuple-element.74), kind=kOutput, calls=%fused_computation.1 | convolution fusion | flops 5371330560 | bytes 12582912 | tf_op jit(solution)/shard_map/dot_general | solution.py:1153
  378.5 0.0 slice-done.2
  378.6 7.7 convolution_convert_fusion.3
  386.2 7.5 convolution_convert_fusion.2
  393.7 181.0 %shard_map.190 = (f32[2,64,2560]{2,1,0:T(8,128)}, f32[1,2560]{1,0:T(1,128)}, f32[2,64,2560]{2,1,0:T(8,128)}, bf16[2,4,2,64,2560]{4,3,2,1,0:T(8,128)(2,1)}, bf16[...) custom-call(bf16[2,4,2,64,2560]{4,3,2,1,0:T(8,128)(2,1)} %bitcast.78, ...), custom_call_target="tpu_custom_call" | custom-call | tf_op jit(solution)/shard_map/pallas_call | solution.py:658
  574.7 2.4 select_convert_fusion
  577.1 0.0 copy-done.9
  577.1 6.7 convolution_convert_fusion.6
  583.8 60.8 %shard_map.191 = (bf16[2,1024,512]{2,1,0:T(8,128)(2,1)}, f32[2,2,256,256]{3,2,1,0:T(8,128)}, f32[8,512]{1,0:T(8,128)}, bf16[1024,2560]{1,0:T(8,128)(2,1)}, bf16[...) custom-call(bf16[1024,2560]{1,0:T(8,128)(2,1)} %bitcast.76, bf16[2560,512]{1,0:T(8,128)(2,1)} %bitcast.95, ...), custom_call_target="tpu_custom_call" | custom-call | tf_op jit(solution)/shard_map/pallas_call | solution.py:1091
  644.7 2.2 convert_element_type.46
  646.9 3.0 convert_bitcast_fusion
  649.9 7.1 convolution_convert_fusion.4
  657.0 0.0 slice-done
  657.0 4.2 convolution_convert_fusion.5
  661.3 100.5 %shard_map.192 = (f32[2,64,2560]{2,1,0:T(8,128)}, f32[8,2560]{1,0:T(8,128)}, f32[4,8,512]{2,1,0:T(8,128)}, bf16[2,160,1280]{2,1,0:T(8,128)(2,1)}, bf16[160,1280]...) custom-call(bf16[2,4,2,64,2560]{4,3,2,1,0:T(8,128)(2,1)} %bitcast.68, bf16[2,64,2560]{2,1,0:T(8,128)(2,1)} %x.5, ...), custom_call_target="tpu_custom_call" | custom-call | tf_op jit(solution)/shard_map/pallas_call | solution.py:751
  761.8 1.6 slice.53
  763.5 0.7 constant_dynamic-update-slice_fusion.4
  764.2 0.7 constant_dynamic-update-slice_fusion.3
  764.9 0.7 constant_dynamic-update-slice_fusion.2
  765.6 0.7 constant_dynamic-update-slice_fusion.1
  766.3 0.7 constant_dynamic-update-slice_fusion
  767.0 0.6 divide_multiply_fusion
  767.6 1.6 convert_element_type.48
  769.2 1.9 convert_bitcast_fusion.1
  771.2 2.4 convert_element_type.47
  773.6 0.0 copy-done.2
  773.6 2.6 maximum_convert_fusion
  776.1 0.0 copy-done.1
  776.1 1.1 copy.26
  (25 shorter events, 0.1 us)
Async XLA Ops:
  325.4 53.1 %slice-start.2 = ((s8[5242880]{0:T(1024)(128)(4,1)}), s8[1048576]{0:T(1024)(128)(4,1)S(1)}, s32[]{:S(2)}) async-start(s8[5242880]{0:T(1024)(128)(4,1)} %bitcast.80), calls=%async_computation.2 | async-start | bytes 2097152
  368.1 10.4 %slice-start.3 = ((s8[5242880]{0:T(1024)(128)(4,1)}), s8[4194304]{0:T(1024)(128)(4,1)S(1)}, s32[]{:S(2)}) async-start(s8[5242880]{0:T(1024)(128)(4,1)} %bitcast.80), calls=%async_computation.3 | async-start | bytes 8388608
  368.1 10.4 %copy-start.8 = (bf16[1024,1024]{1,0:T(8,128)(2,1)S(1)}, bf16[1024,1024]{1,0:T(8,128)(2,1)}, u32[]{:S(2)}) copy-start(bf16[1024,1024]{1,0:T(8,128)(2,1)} %get-tuple-element.72) | copy-start | bytes 6291460
  378.6 7.7 copy-start.7
  393.7 181.0 %copy-start = (f32[2,64,2560]{2,1,0:T(8,128)S(1)}, f32[2,64,2560]{2,1,0:T(8,128)}, u32[]{:S(2)}) copy-start(f32[2,64,2560]{2,1,0:T(8,128)} %get-tuple-element.64.res) | copy-start | bytes 3932164
  574.7 2.4 copy-start.9
  644.7 5.3 copy-start.6
  646.9 10.1 %slice-start = ((s8[5242880]{0:T(1024)(128)(4,1)}), s8[4194304]{0:T(1024)(128)(4,1)S(1)}, s32[]{:S(2)}) async-start(s8[5242880]{0:T(1024)(128)(4,1)} %bitcast.71), calls=%async_computation | async-start | bytes 8388608
  649.9 7.1 slice-start.1
  661.3 105.8 %copy-start.4 = (f32[1280]{0:T(1024)S(1)}, f32[1280]{0:T(1024)}, u32[]{:S(2)}) copy-start(f32[1280]{0:T(1024)} %param.17) | copy-start | bytes 15364
  761.8 11.8 %copy-start.2 = (bf16[160,3840]{1,0:T(8,128)(2,1)S(1)}, bf16[160,3840]{1,0:T(8,128)(2,1)}, u32[]{:S(2)}) copy-start(bf16[160,3840]{1,0:T(8,128)(2,1)} %get-tuple-element.99) | copy-start | bytes 3686404
  761.8 11.8 %copy-start.3 = (bf16[160,3840]{1,0:T(8,128)(2,1)S(1)}, bf16[160,3840]{1,0:T(8,128)(2,1)}, u32[]{:S(2)}) copy-start(bf16[160,3840]{1,0:T(8,128)(2,1)} %get-tuple-element.100) | copy-start | bytes 3686404
  767.0 9.2 %copy-start.5 = (f32[8,1280]{1,0:T(8,128)}, f32[8,1280]{1,0:T(8,128)S(1)}, u32[]{:S(2)}) copy-start(f32[8,1280]{1,0:T(8,128)S(1)} %constant_dynamic-update-slice_fusion) | copy-start | bytes 122884
  773.6 2.6 copy-start.1

commit v5 on v4

--- a/solution.py
+++ b/solution.py
@@ -164,15 +164,15 @@
         pl.when(t + 1 + k < TP)(both(above))
 
 
-def rs_scratch(rows, width):
+def rs_scratch(rows, width, made=False):
     return [
-        pltpu.VMEM((2, TP, rows, width), BF),
+        pltpu.VMEM((1 if made else 2, 2, TP, rows, width), BF),
         pltpu.VMEM((2, TP - 1, 2, rows, width), BF),
         pltpu.VMEM((TP - 1, 2, rows, width), BF),
     ]
 
 
-def rs_flow(c, part, out, sib, inbox, outbox):
+def rs_flow(c, part, out, pair, inbox, outbox, make=None):
     t, m = c.t, c.m
     n = part.shape[3]
     other = c.at(m=1 - m)
@@ -181,6 +181,9 @@
     da = jnp.where(lower, 0, 1)
     hop = 1 - 2 * da
     near = [[c.slot() for _ in range(2)] for _ in range(TP)]
+    here = [[c.slot() for _ in range(2)] for _ in range(TP)]
+    sib = pair.at[pair.shape[0] - 1]
+    own = (lambda s, b: part.at[s, b, m]) if make else (lambda s, b: pair.at[0, s, b])
     base = c.n
     for _ in range(4 * (TP - 1)):
         c.slot()
@@ -190,6 +193,14 @@
 
     def cross(d, s):
         return c.to(part.at[s, real(d), 1 - m], sib.at[s, real(d)], other, near[d][s])
+
+    def load(d, s):
+        return c.local(part.at[s, real(d), m], own(s, real(d)), here[d][s])
+
+    def near_in(d, s):
+        cross(d, s).wait_recv()
+        if make is None:
+            load(d, s).wait()
 
     def msg(flow, j, s):
         way = da if flow == 0 else 1 - da
@@ -201,7 +212,7 @@
 
         def rows16(i, _):
             sl = pl.ds(pl.multiple_of(i * 16, 16), 16)
-            v = part[s, b, m, sl, :].astype(F32) + sib[s, b, sl, :].astype(F32)
+            v = own(s, b)[sl, :].astype(F32) + sib[s, b, sl, :].astype(F32)
             for way, j in terms:
                 v = v + inbox[way, j, s, sl, :].astype(F32)
             into(s, sl, v)
@@ -217,44 +228,61 @@
     def final(s, sl, v):
         out[s, sl, :] = v
 
-    for d in (3, 2, 0, 1):
+    def issue(d):
+        if make is not None:
+            b = real(d)
+            rows = [pl.ds(pl.multiple_of((s * TP + b) * 2 * n, 2 * n), 2 * n) for s in range(2)]
+            v = make(rows).astype(BF).reshape(2, 2, n, part.shape[4])
+            for s in range(2):
+                part[s, b] = v[s]
         for s in range(2):
+            if make is None:
+                load(d, s).start()
             cross(d, s).start()
+
+    def send_out(d, j):
+        for s in range(2):
+            near_in(d, s)
+            add(d, s, put(j), [])
+            msg(0, j, s).start()
+
+    issue(3)
+    issue(2)
+    yield
+    pl.when(u == 0)(lambda: send_out(3, 0))
+    issue(1)
+    pl.when(u == 0)(lambda: send_out(2, 1))
+    issue(0)
+    pl.when(u == 0)(lambda: send_out(1, 2))
     yield
     for d, j in ((3, 0), (2, 1)):
+        def pass_on():
+            for s in range(2):
+                near_in(d, s)
+                msg(0, j, s).wait_recv()
+                add(d, s, put(j), [(da, j)])
+                msg(0, j, s).start()
+
+        pl.when(u == 1)(pass_on)
+        yield
+
+    def back():
         for s in range(2):
-            cross(d, s).wait_recv()
-            for lvl in range(2):
-                def go():
-                    if lvl == 1:
-                        msg(0, j, s).wait_recv()
-                    add(d, s, put(j), [(da, j)] if lvl else [])
-                    msg(0, j, s).start()
-                pl.when(u == lvl)(go)
-        yield
-    for s in range(2):
-        cross(0, s).wait_recv()
-        cross(1, s).wait_recv()
-
-        def first():
-            add(1, s, put(2), [])
-            msg(0, 2, s).start()
-
-        pl.when(u == 0)(first)
-
-        def back():
+            near_in(0, s)
             msg(1, 0, s).wait_recv()
             add(0, s, put(2), [(1 - da, 0)])
             msg(1, 0, s).start()
 
-        pl.when(u == 1)(back)
+    pl.when(u == 1)(back)
     yield
     for s in range(2):
         def end0():
+            near_in(0, s)
             msg(1, 0, s).wait_recv()
             add(0, s, final, [(1 - da, 0)])
 
         def end1():
+            near_in(1, s)
             msg(0, 2, s).wait_recv()
             msg(1, 1, s).wait_recv()
             add(1, s, final, [(da, 2), (1 - da, 1)])
@@ -397,6 +425,30 @@
         return 0
 
     lax.fori_loop(0, a.shape[0], one, 0)
+
+
+def grad_flow(c, lhs, rhs, out, rbuf, lbuf, stage, halves):
+    wide = lbuf.shape[2]
+    _, ng, r, cols = stage.shape
+    load = c.local(rhs, rbuf, c.slot())
+    load.start()
+    pieces = [c.local(lhs.at[:, pl.ds(k * wide, wide)], lbuf.at[k % 2], c.slot()) for k in range(TP)]
+    puts = [c.local(stage.at[k % 2], out.at[k], c.slot()) for k in range(TP)]
+    pieces[0].start()
+    pieces[1].start()
+    load.wait()
+    for k in range(TP):
+        pieces[k].wait()
+        v = lax.dot_general(lbuf[k % 2], rbuf[...], (((0,), (0,)), ((), ())), preferred_element_type=F32)
+        if k + 2 < TP:
+            pieces[k + 2].start()
+        stage[k % 2] = v.astype(BF).reshape(ng, r, cols)
+        puts[k].start()
+        if k % 2:
+            puts[k - 1].wait()
+            puts[k].wait()
+            step(*halves[k // 2])
+            yield
 
 
 def call(kernel, out_shape, in_specs, out_specs, scratch, cid, slots=160):
@@ -518,10 +570,10 @@
 
 
 MID_LATE = False
-MID_ORDER = "r0yar0ay1arNz1aAz2A2"
-
-
-def mid_kernel(part, x, go, gain, p0, m1, m2, zero, res, full, full_g, w0, w1, w2, tot, own, sib, inbox, outbox, send, recv):
+MID_ORDER = "r0yarr0ary1arNz1aAz2A2"
+
+
+def mid_kernel(mixed, wo, x, go, gain, p0, m1, m2, zero, res, full, full_g, w0, w1, w2, tot, own, part, pair, inbox, outbox, send, recv):
     c = Comm(send, recv)
     c.barrier()
     fwd, rev = c.bits, c.bits[::-1]
@@ -534,7 +586,12 @@
             yield plane_gather(c, lambda g, at=at: w.at[at, g], order, None if own is None else own.at[at])
 
     last = len(c.bits) - 1
-    rs = rs_flow(c, part, tot, sib, inbox, outbox)
+
+    def make(rows):
+        v = jnp.concatenate([mixed[at, :] for at in rows], axis=0)
+        return lax.dot_general(v, wo[...], (((1,), (1,)), ((), ())), preferred_element_type=F32)
+
+    rs = rs_flow(c, part, tot, pair, inbox, outbox, make)
     ag, ag2 = ag_flow(c, own, full), ag_flow(c, go, full_g, MID_LATE)
     z1 = spread_z(c, *units_to(m1, lambda t: w1.at[t, c.g]))
     z2 = spread_z(c, *units_to(m2, lambda t: w2.at[t, c.g]))
@@ -567,7 +624,7 @@
     finish(ag, ag2, *g[0], *g[1], *g[2], z1, z2)
 
 
-def mid_call(part, x, go, gain, p0, m1, m2):
+def mid_call(mixed, wo, x, go, gain, p0, m1, m2):
     _, n, d = x.shape
     ng = lax.axis_size("dp") // TP
     _, r, fs = p0.shape
@@ -578,36 +635,40 @@
     return call(
         mid_kernel,
         (S((2, n, d), F32), S((2, TP, 2, n, d), BF), S((2, TP, 2, n, d), BF), w, w, w),
-        [VM, VM, VM, VM, HBM, HBM, HBM, VM],
+        [VM, VM, VM, VM, VM, HBM, HBM, HBM, VM],
         (VM,) + (HBM,) * 5,
-        [pltpu.VMEM((2, n, d), F32), pltpu.VMEM((2, n, d), BF)] + rs_scratch(n, d),
+        [pltpu.VMEM((2, n, d), F32), pltpu.VMEM((2, n, d), BF), pltpu.VMEM((2, TP, 2, n, d), BF)] + rs_scratch(n, d, True),
         2,
-    )(part.reshape(2, TP, 2, n, d), x, go, gain[None], p0, m1, m2, zero)
-
-
-def back_kernel(part, part2, res, go, gain, h0, h1, h2, gres, gsum, mlp_own, full, o0, o1, r2,
-                tot, own, sib, inbox, outbox, sib2, inbox2, outbox2, su, ib, send, recv):
+    )(mixed, wo, x, go, gain[None], p0, m1, m2, zero)
+
+
+def back_kernel(part, part2, res, go, gain, nb, gall, gg0, gg1, hidden, gres, gsum, mlp_own, full, o0, r1, r2, h0, h1, h2,
+                tot, own, pair, inbox, outbox, pair2, inbox2, outbox2, su, ib, rbuf, lbuf, stage, send, recv):
     c = Comm(send, recv)
     c.barrier()
     fwd, rev = c.bits, c.bits[::-1]
-    rs = rs_flow(c, part, tot, sib, inbox, outbox)
+    rs = rs_flow(c, part, tot, pair, inbox, outbox)
     next(rs)
-    red = []
+    red, grad = [], []
     for k, h in enumerate((h0, h1, h2)):
         red.append([plane_reduce(c, lambda g, h=h, q=q: h.at[pl.ds(2 * q, 2), g], su.at[2 * k + q], ib.at[2 * k + q], (fwd, rev)[q]) for q in range(2)])
+        grad.append(grad_flow(c, gall if k == 2 else nb, (gg0, gg1, hidden)[k], h, rbuf, lbuf, stage, [[f] for f in red[k]]))
     last = len(c.bits) - 1
 
     def onward(parts):
         for _ in range(last):
             step(*parts)
 
-    step(*red[0])
     step(rs)
-    step(*red[1])
+    step(grad[0])
+    step(grad[0])
+    step(rs)
+    step(grad[1])
+    step(rs)
+    step(grad[1])
     onward(red[0])
     step(rs)
-    step(rs)
-    rs2 = rs_flow(c, part2, mlp_own, sib2, inbox2, outbox2)
+    rs2 = rs_flow(c, part2, mlp_own, pair2, inbox2, outbox2)
     finish(rs)
     total = jnp.zeros_like(gsum)
     for s in range(2):
@@ -623,10 +684,12 @@
     gsum[...] = total
     ag = ag_flow(c, own, full)
     step(ag, rs2)
+    step(rs2)
     finish(*red[0])
     s0 = spread_z(c, *units_back(lambda t: su.at[t // 2, 0, t % 2], o0))
     step(s0)
-    step(*red[2])
+    step(grad[2])
+    step(grad[2])
     onward(red[1])
     step(ag, rs2)
     held = []
@@ -639,34 +702,35 @@
 
     step(ag, rs2)
     onward(red[2])
-    finish(*red[1])
-    s1 = spread_z(c, *units_back(lambda t: su.at[2 + t // 2, 0, t % 2], o1))
-    step(s1)
+    keep(1, r1)
     step(rs2)
     finish(ag, rs2)
     keep(2, r2)
-    finish(s0, s1)
+    finish(s0, *grad)
     for h in held:
         h.wait()
 
 
-def back_call(part, part2, res, go, gain, h0, h1, h2, units):
+def back_call(part, part2, res, go, gain, nb, gall, gg0, gg1, hidden, ng, r, units):
     _, n, d = go.shape
-    _, ng, r, fs = h0.shape
+    rows, fs = hidden.shape
     S = jax.ShapeDtypeStruct
     shape = (2, TP, 2, n, d)
-    return call(
+    h = S((TP, ng, r, fs), BF)
+    *outs, _, _, _ = call(
         back_kernel,
-        (S((2, n, d), F32), S((1, d), F32), S((2, n, d), F32), S(shape, BF), S((r, units), BF), S((r, units), BF), S((TP, r, fs), BF)),
-        [VM] * 5 + [HBM] * 3,
-        (VM, VM, VM, HBM, HBM, HBM, HBM),
+        (S((2, n, d), F32), S((1, d), F32), S((2, n, d), F32), S(shape, BF), S((r, units), BF), S((TP, r, fs), BF), S((TP, r, fs), BF), h, h, h),
+        [HBM] * 2 + [VM] * 3 + [HBM] * 5,
+        (VM, VM, VM) + (HBM,) * 7,
         [pltpu.VMEM((2, n, d), F32), pltpu.VMEM((2, n, d), BF)] + rs_scratch(n, d) + rs_scratch(n, d)
-        + [pltpu.VMEM((6, ng // 2, 2, r, fs), BF), pltpu.VMEM((6, ng - 1, 2, r, fs), BF)],
+        + [pltpu.VMEM((6, ng // 2, 2, r, fs), BF), pltpu.VMEM((6, ng - 1, 2, r, fs), BF)]
+        + [pltpu.VMEM((rows, fs), BF), pltpu.VMEM((2, rows, ng * r), BF), pltpu.VMEM((2, ng, r, fs), BF)],
         3, 256,
-    )(part.reshape(shape), part2.reshape(shape), res, go, gain[None], h0, h1, h2)
-
-
-def small_flow(c, small, inbox, zbox, sbox, gains, table):
+    )(part.reshape(shape), part2.reshape(shape), res, go, gain[None], nb, gall, gg0, gg1, hidden)
+    return outs
+
+
+def small_flow(c, small, inbox, zbox):
     for k, b in enumerate(c.bits):
         copy = c.to(small.at[k], inbox.at[k], c.at(g=c.flip(c.g, b)), c.slot())
         copy.start()
@@ -678,17 +742,10 @@
     next(z)
     yield
     run(z)
-    sbox[0] = zbox[0, 0:8] + zbox[1, 0:8] + zbox[2, 0:8] + zbox[3, 0:8]
-    table[...] = zbox[:, 8:16, 0:512]
-    copy = c.to(sbox.at[0], sbox.at[1], c.at(m=1 - c.m), c.slot())
-    copy.start()
-    yield
-    copy.wait()
-    gains[...] = sbox[0] + sbox[1]
-
-
-def end_kernel(part, x, gres, gain, gwb0, gwb1, ggb, rwo, gain_b, chan_rows, gin, gains, table, owb, owo, ogb,
-               small, small_in, zbox, sbox, tot, sib, inbox, outbox, su_x, in_x, su_g, in_g, send, recv):
+
+
+def end_kernel(wb0, wb1, gbr, x, gres, gain, na, gsrc, ggb, rwo, gain_b, chan_rows, gin, gains, table, owb, owo, ogb, gwb0, gwb1,
+               sm_a, in_a, z_a, sm_b, in_b, sbox, z_b, tot, part, pair, inbox, outbox, su_x, in_x, su_g, in_g, rbuf, lbuf, stage, send, recv):
     c = Comm(send, recv)
     c.barrier()
     fwd, rev = c.bits, c.bits[::-1]
@@ -702,15 +759,40 @@
             spread.append((len(red) - 1, spread_z(c, lambda t, q, i=i: su_x.at[i, 0, t], lambda t, q, k=k, lane=lane: owb.at[k, :, lane(t)], which, "from")))
             red.append(plane_reduce(c, lambda g, k=k, h=h: ggb.at[k, h, :, g], su_g.at[i], in_g.at[i], order, cond))
             spread.append((len(red) - 1, spread_z(c, lambda t, q, i=i: su_g.at[i, 0, t], lambda t, q, k=k, h=h: ogb.at[k, 4 if h else t], which, "from")))
-    rs = rs_flow(c, part, tot, sib, inbox, outbox)
+
+    def make(rows):
+        v = [jnp.concatenate([gbr[k, at, :] for at in rows], axis=0) for k in range(2)]
+        v = [lax.dot_general(v[k], w[...], (((1,), (1,)), ((), ())), preferred_element_type=F32) for k, w in enumerate((wb0, wb1))]
+        return v[0] + v[1]
+
+    rs = rs_flow(c, part, tot, pair, inbox, outbox, make)
     next(rs)
-    for f in red:
-        next(f)
-    z0 = []
-    for extra in (False, True):
-        z0.append(spread_z(c, *heads_out(c, lambda t: rwo.at[t], owo, extra)))
+    grad = [grad_flow(c, na, gsrc.at[k], gw, rbuf, lbuf, stage, ([], [red[2 * k], red[4 + 2 * k]])) for k, gw in enumerate((gwb0, gwb1))]
+    for k in range(4):
+        step(red[2 * k + 1])
+    sm_a[0] = chan_rows[...]
+    chan = small_flow(c, sm_a, in_a, z_a)
+    step(chan)
+    z0 = [spread_z(c, *heads_out(c, lambda t: rwo.at[t], owo, extra)) for extra in (False, True)]
+    step(rs)
+    step(grad[0])
+    step(grad[0])
+    step(rs)
+    step(grad[1])
+    step(grad[1])
+    for _ in c.bits:
+        step(chan)
+    step(*z0)
+    step(rs)
+    for _ in range(len(c.bits) - 1):
+        step(*red)
+    step(rs)
+    for i, f in enumerate(red):
+        finish(f)
+        for k, z in spread:
+            if k == i:
+                next(z)
     finish(rs)
-    step(*z0)
     total = jnp.zeros_like(gain)
     for s in range(2):
         v = x[s].astype(F32)
@@ -720,43 +802,44 @@
         total = total + jnp.sum(gn * normal, axis=0, keepdims=True)
         q = gn * gain[...]
         gin[s] = scale * (q - normal * jnp.mean(q * normal, axis=-1, keepdims=True)) + gres[s]
-    small[0] = jnp.zeros_like(small[0])
-    small[0, 0:1, :] = total
-    small[0, 1:2, :] = gain_b[...]
-    small[0, 8:16, 0:512] = chan_rows[...]
-    sm = small_flow(c, small, small_in, zbox, sbox, gains, table)
-    next(sm)
-    for _ in range(len(c.bits) - 1):
-        for f in red:
-            next(f)
-        next(sm)
-    for i, f in enumerate(red):
-        finish(f)
-        for k, z in spread:
-            if k == i:
-                next(z)
-    next(sm)
-    run(sm, *z0, *[z for _, z in spread])
-
-
-def end_call(part, x, gres, gain, gwb0, gwb1, ggb, rwo, gain_b, chan_rows):
+    quarter = sm_b.shape[2]
+    for k in range(4):
+        sm_b[0, k:k + 1, :] = total[:, k * quarter:(k + 1) * quarter]
+        sm_b[0, 4 + k:5 + k, :] = gain_b[:, k * quarter:(k + 1) * quarter]
+    finish(small_flow(c, sm_b, in_b, z_b))
+    sbox[0] = z_b[0] + z_b[1] + z_b[2] + z_b[3]
+    copy = c.to(sbox.at[0], sbox.at[1], c.at(m=1 - c.m), c.slot())
+    copy.start()
+    finish(chan)
+    table[...] = z_a[...]
+    copy.wait()
+    gains[...] = sbox[0] + sbox[1]
+    run(*grad, *z0, *[z for _, z in spread])
+
+
+def end_call(wb0, wb1, x, gres, gain, na, gsrc, ggb, rwo, gain_b, chan_rows, r):
     _, n, d = x.shape
     ng = lax.axis_size("dp") // TP
-    r, gr, steps = gwb0.shape[2], ggb.shape[4], (lax.axis_size("dp") // TP).bit_length()
+    gr, steps = ggb.shape[4], (lax.axis_size("dp") // TP).bit_length()
+    V = pltpu.VMEM
     S = jax.ShapeDtypeStruct
 
     def sets(k, rows, width):
         return [pltpu.VMEM((k, ng // 2, TP, rows, width), BF), pltpu.VMEM((k, ng - 1, TP, rows, width), BF)]
 
-    return call(
+    *outs, _, _ = call(
         end_kernel,
-        (S((2, n, d), F32), S((8, d), F32), S((TP, 8, 512), F32), S((2, r, 1280), BF), S((r, 1280), BF), S((2, 5, gr, 256), BF)),
-        [VM] * 4 + [HBM] * 4 + [VM] * 2,
-        (VM,) * 3 + (HBM,) * 3,
-        [pltpu.VMEM((steps, 16, d), F32), pltpu.VMEM((steps - 1, 16, d), F32), pltpu.VMEM((TP, 16, d), F32), pltpu.VMEM((2, 8, d), F32),
-         pltpu.VMEM((2, n, d), F32)] + rs_scratch(n, d) + sets(4, r, 256) + sets(4, gr, 256),
+        (S((2, n, d), F32), S((8, d // 4), F32), S((TP, 8, 512), F32), S((2, r, 1280), BF), S((r, 1280), BF), S((2, 5, gr, 256), BF))
+        + (S((TP, ng, r, 512), BF),) * 2,
+        [VM] * 6 + [HBM] * 4 + [VM] * 2,
+        (VM,) * 3 + (HBM,) * 5,
+        [V((steps, 8, 512), F32), V((steps - 1, 8, 512), F32), V((TP, 8, 512), F32),
+         V((steps, 8, d // 4), F32), V((steps - 1, 8, d // 4), F32), V((2, 8, d // 4), F32), V((TP, 8, d // 4), F32),
+         pltpu.VMEM((2, n, d), F32), pltpu.VMEM((2, TP, 2, n, d), BF)] + rs_scratch(n, d, True) + sets(4, r, 256) + sets(4, gr, 256)
+        + [pltpu.VMEM((na.shape[0], 512), BF), pltpu.VMEM((2, na.shape[0], ng * r), BF), pltpu.VMEM((2, ng, r, 512), BF)],
         4, 256,
-    )(part.reshape(2, TP, 2, n, d), x, gres, gain[None], gwb0, gwb1, ggb, rwo, gain_b, chan_rows)
+    )(wb0, wb1, gsrc, x, gres, gain[None], na, gsrc, ggb, rwo, gain_b, chan_rows)
+    return outs
 
 
 def heads_of(a, axis):
@@ -961,13 +1044,13 @@
     )(na, wb0, wb1, gb, chan, db[None], wop, m0, jnp.zeros((TP, r, big - small), BF), jnp.zeros((TP, r, 256), BF))
 
 
-def mix_bwd_kernel(gmo, wo, wb0, wb1, br0, ci, gb, chan, db, conv, gates, state, rim, carry, table, gwo, r1, gbr, ggb, sums, gna, rwo, o1,
+def mix_bwd_kernel(gmo, wo, br0, ci, gb, chan, db, conv, gates, state, rim, carry, table, gwo, r1, r2, gbr, ggb, sums, rwo, o1, o2,
                    gm, a_ref, adj, gc, gpl, ext, heads, etab, rim_in, su, ib, send, recv):
     c = Comm(send, recv)
     greet(plane_partners(c) + line_partners(c))
     n, width = ci.shape[1], ci.shape[2]
-    z0 = spread_z(c, *units_back(lambda t: r1.at[t], o1))
-    next(z0)
+    zs = [spread_z(c, *units_back(lambda t, rr=rr: rr.at[t], oo)) for rr, oo in ((r1, o1), (r2, o2))]
+    step(*zs)
     fwd, rev = c.bits, c.bits[::-1]
     red = []
     for h in range(2):
@@ -1063,25 +1146,17 @@
         for k in range(1, 4):
             v = v + chan[k:k + 1] * gc[b, pl.ds(k, n), :]
         gbr[1, rows, :] = v.astype(BF)
-
-    def onto(i, _):
-        rows = pl.ds(pl.multiple_of(i * 2 * n, 2 * n), 2 * n)
-        v = [lax.dot_general(gbr[k, rows, :], w[...], (((1,), (1,)), ((), ())), preferred_element_type=F32) for k, w in enumerate((wb0, wb1))]
-        gna[rows, :] = (v[0] + v[1]).astype(BF)
-        return 0
-
-    lax.fori_loop(0, TP, onto, 0)
     held = []
     for i, f in enumerate(red):
         finish(f)
         held.append(c.local(su.at[i, 0], rwo.at[pl.ds(2 * (i % 2), 2), :, pl.ds(256 * (i // 2), 256)], c.slot()))
         only(c.fifth() if i >= 2 else None, lambda: held[-1].start())
-    run(z0)
+    run(*zs)
     for i, h in enumerate(held):
         only(c.fifth() if i >= 2 else None, lambda: h.wait())
 
 
-def mix_bwd_call(gmo, wo, wb0, wb1, br0, ci, gb, chan, db, saved, gwo, r1, units):
+def mix_bwd_call(gmo, wo, br0, ci, gb, chan, db, saved, gwo, r1, r2, units):
     ng = lax.axis_size("dp") // TP
     rows, width = br0.shape
     n = rows // (2 * TP)
@@ -1090,14 +1165,14 @@
     V = pltpu.VMEM
     return call(
         mix_bwd_kernel,
-        (S((2, rows, width), BF), S((2, 2, 256, 256), F32), S((8, width), F32), S(gmo.shape, BF), S((TP, r, width), BF), S((r, units), BF)),
-        [VM] * 15 + [HBM] * 2,
-        (VM,) * 4 + (HBM,) * 2,
+        (S((2, rows, width), BF), S((2, 2, 256, 256), F32), S((8, width), F32), S((TP, r, width), BF), S((r, units), BF), S((r, units), BF)),
+        [VM] * 13 + [HBM] * 3,
+        (VM,) * 3 + (HBM,) * 3,
         [V((rows, width), F32), V((width // 128, rows, 128), F32), V((width // 128, rows, 128), F32), V((2 * TP, n + 8, width), F32), V((2, rows, width), BF),
          V((2, n + 8, width), F32), V((2 * TP, 8, width), F32), V((ng, 2 * TP, width), F32), V((2 * TP, 8, width), F32),
          V((4, ng // 2, 2, r, 256), BF), V((4, ng - 1, 2, r, 256), BF)],
         6, 128,
-    )(gmo, wo, wb0, wb1, br0, ci, gb, chan, db[None], *saved, gwo, r1)
+    )(gmo, wo, br0, ci, gb, chan, db[None], *saved, gwo, r1, r2)
 
 
 def mlp_kernel(nb, go, w0, w1, w2, hidden, gg0, gg1, part, gnb, v0, v1, v2, sems):
@@ -1172,26 +1247,23 @@
     gb = gb.reshape(2, 2, 256, 256)
     mixed, *saved, branch0, conv_input, wo, p0 = mix_fwd_call(na, wb0, wb1, gb, chan, decay_base, wop, w_mlp[0])
     wo = wo.reshape(width, 512)
-    residual, nb, go, w0, w1, wd = mid_call(dot(mixed, wo, 1, 1).astype(BF), x, grad_own, norm_gains[1], p0, w_mlp[1], w_down.T)
+    residual, nb, go, w0, w1, wd = mid_call(mixed, wo, x, grad_own, norm_gains[1], p0, w_mlp[1], w_down.T)
     nb, go = nb.reshape(-1, width), go.reshape(-1, width)
     w0, w1, wd = w0.reshape(width, fs), w1.reshape(width, fs), wd.reshape(width, fs)
     hidden, gg0, gg1, mlp_part, gnb = mlp_call(nb, go, w0, w1, wd)
-    block = (TP, ng, r, fs)
-    gwd, gw0, gw1 = [dot(p, q, 0, 0).astype(BF).reshape(block) for p, q in ((go, hidden), (nb, gg0), (nb, gg1))]
-    gres, gain_b, mlp_own, gmo, o0, o1, r2 = back_call(gnb, mlp_part, residual, grad_own, norm_gains[1], gw0, gw1, gwd, units)
+    gres, gain_b, mlp_own, gmo, o0, r1, r2 = back_call(gnb, mlp_part, residual, grad_own, norm_gains[1], nb, go, gg0, gg1, hidden, ng, r, units)
     out = jnp.where(valid, residual + mlp_own, 0.0).astype(BF)
     gmo = gmo.reshape(-1, width)
     block = (TP, ng, r, 512)
     gwo = dot(gmo, mixed, 0, 0).astype(BF).reshape(block)
-    gbr, ggb, chan_rows, gna, rwo, o2 = mix_bwd_call(gmo, wo, wb0, wb1, branch0, conv_input, gb, chan, decay_base, saved, gwo, r2, units)
-    gwb0, gwb1 = [dot(na, gbr[k], 0, 0).astype(BF).reshape(block) for k in range(2)]
+    gbr, ggb, chan_rows, rwo, o1, o2 = mix_bwd_call(gmo, wo, branch0, conv_input, gb, chan, decay_base, saved, gwo, r1, r2, units)
     gin, gains, table, owb, owo, ogb = end_call(
-        gna, x, gres, norm_gains[0], gwb0, gwb1, ggb.astype(BF).reshape(2, 2, TP, ng, gr, 256), rwo, gain_b, chan_rows,
+        wb0, wb1, x, gres, norm_gains[0], na, gbr, ggb.astype(BF).reshape(2, 2, TP, ng, gr, 256), rwo, gain_b, chan_rows, r,
     )
     g_wb, g_wo, g_gb = owb.astype(F32), owo.astype(F32).T, ogb.astype(F32)
     g_wm, g_wd = jnp.stack([o0, o1]).astype(F32), o2.astype(F32).T
     crow = jnp.concatenate([table[i, :, :256] for i in range(TP)] + [jnp.where(mp == 0, table[1, :, 256:], table[2, :, 256:])], -1)
-    return out, gin, gains[:2], g_wb, crow[:7], g_gb, crow[7] * jax.nn.sigmoid(decay_param), g_wo, g_wm, g_wd
+    return out, gin, gains.reshape(2, width), g_wb, crow[:7], g_gb, crow[7] * jax.nn.sigmoid(decay_param), g_wo, g_wm, g_wd
 
 
 def solution(mesh):

time: 781 us -> 737 us (0.944)
  matrix products: 50.9 us -> 6.71 us
    dot_general x7 -> x1, matrix products: 50.9 us -> 6.71 us  [dot(): lax.dot_general(a, b, (((ca,), (cb,)), ((), ())), preferred_element_type=...]
    pallas_call x1, Pallas kernels: 101 us -> 109 us  [end_call(): call(end_kernel, (S((2, n, d), F32), S((8, d // 4), F32), S((TP, 8, 512),...]
where the time goes in v5:
time: 737 us; the launch traced here: 733 us
  Pallas kernels  691 us (94%)
  other arithmetic  20.6 us (3%)
  local copies, waits for them, and re-layouts  13.8 us (2%)
    pallas_call x1, Pallas kernels, mid_call(): call(mid_kernel, (S((2, n, d), F32), S((2, TP, 2, n, d), BF), S((2, TP, 2...  185 us
    pallas_call x1, Pallas kernels, back_call(): call(back_kernel, (S((2, n, d), F32), S((1, d), F32), S((2, n, d), F32),...  174 us
    pallas_call x1, Pallas kernels, end_call(): call(end_kernel, (S((2, n, d), F32), S((8, d // 4), F32), S((TP, 8, 512),...  109 us
    pallas_call x1, Pallas kernels, start_call(): call(start_kernel, (S((2, TP, 2, n, d), BF), S((TP, ng, r, 512), BF), S((...  80.5 us
    pallas_call x1, Pallas kernels, mix_bwd_call(): call(mix_bwd_kernel, (S((2, rows, width), BF), S((2, 2, 256, 256), F32),...  60 us
    pallas_call x1, Pallas kernels, mlp_call(): pl.pallas_call(mlp_kernel, grid=(rows // n,), out_shape=(S((rows, fs), BF...  42.6 us
    pallas_call x1, Pallas kernels, mix_fwd_call(): call(mix_fwd_kernel, (S((rows, width), BF), S((rows, width), BF), S((2, r...  40.5 us

profile of v5, /device:TPU:0, one launch (start us, length us, event | category | flops | bytes accessed | tf_op | source)
XLA Modules:
  0.0 733.2 jit_solution(2976523448609536807)
XLA Ops:
  0.7 0.7 broadcast_compare_fusion
  1.4 0.8 dynamic-slice.3
  2.2 0.7 broadcast_in_dim.40
  2.9 0.6 compare_select_fusion.db
  3.5 0.7 constant_dynamic-slice_fusion
  4.2 0.6 pad_maximum_fusion.chan
  4.8 1.4 fusion
  6.2 2.0 broadcast_select_fusion.go
  8.3 3.2 slice_bitcast_fusion
  11.5 80.5 %shard_map.186 = (bf16[2,4,2,64,2560]{4,3,2,1,0:T(8,128)(2,1)}, bf16[4,4,160,512]{3,2,1,0:T(8,128)(2,1)}, bf16[4,4,160,512]{3,2,1,0:T(8,128)(2,1)}, bf16[4,160,5...) custom-call(bf16[2,64,2560]{2,1,0:T(8,128)(2,1)} %x.5, f32[1,2560]{1,0:T(1,128)} %get-tuple-element.107.gain, ...), custom_call_target="tpu_custom_call" | custom-call | tf_op jit(solution)/shard_map/pallas_call | solution.py:562
  92.0 0.7 broadcast_3_zero.2.zero
  92.7 0.7 broadcast_in_dim.42.blank
  93.5 40.5 %shard_map.187 = (bf16[1024,512]{1,0:T(8,128)(2,1)}, bf16[1024,512]{1,0:T(8,128)(2,1)}, f32[2,1024,512]{2,1,0:T(8,128)}, f32[1024,512]{1,0:T(8,128)}, f32[8,8,51...) custom-call(bf16[1024,2560]{1,0:T(8,128)(2,1)} %bitcast.41, ...), custom_call_target="tpu_custom_call" | custom-call | tf_op jit(solution)/shard_map/pallas_call | solution.py:1036
  134.0 185.0 %shard_map.188 = (f32[2,64,2560]{2,1,0:T(8,128)}, bf16[2,4,2,64,2560]{4,3,2,1,0:T(8,128)(2,1)}, bf16[2,4,2,64,2560]{4,3,2,1,0:T(8,128)(2,1)}, bf16[4,4,160,1024]...) custom-call(bf16[1024,512]{1,0:T(8,128)(2,1)} %get-tuple-element.61.mixed, ...), custom_call_target="tpu_custom_call" | custom-call | tf_op jit(solution)/shard_map/pallas_call | solution.py:635
  318.9 42.6 %shard_map.189 = (bf16[1024,1024]{1,0:T(8,128)(2,1)}, bf16[1024,1024]{1,0:T(8,128)(2,1)}, bf16[1024,1024]{1,0:T(8,128)(2,1)}, bf16[1024,2560]{1,0:T(8,128)(2,1)}, bf16[1024,2560]{1,0:T(8,128)(2,1)}) custom-call(bf16[1024,2560]{1,0:T(8,128)(2,1)} %bitcast.43, bf16[1024,2560]{1,0:T(8,128)(2,1)} %bitcast.45, bf16[2560,1024]{1,0:T(8,128)(2,1)} %bitcast.57, ...), custom_call_target="tpu_custom_call" | custom-call | tf_op jit(solution)/shard_map/pallas_call | solution.py:1216
  361.6 0.0 copy-start
  361.6 173.6 %shard_map.190 = (f32[2,64,2560]{2,1,0:T(8,128)}, f32[1,2560]{1,0:T(1,128)}, f32[2,64,2560]{2,1,0:T(8,128)}, bf16[2,4,2,64,2560]{4,3,2,1,0:T(8,128)(2,1)}, bf16[...) custom-call(bf16[2,4,2,64,2560]{4,3,2,1,0:T(8,128)(2,1)} %bitcast.56, ...), custom_call_target="tpu_custom_call" | custom-call | tf_op jit(solution)/shard_map/pallas_call | solution.py:720
  535.1 0.0 copy-start.5
  535.1 0.0 copy-done
  535.2 2.4 select_convert_fusion
  537.5 0.0 copy-done.5
  537.6 6.7 convolution_convert_fusion
  544.3 60.0 %shard_map.191 = (bf16[2,1024,512]{2,1,0:T(8,128)(2,1)}, f32[2,2,256,256]{3,2,1,0:T(8,128)}, f32[8,512]{1,0:T(8,128)}, bf16[4,160,512]{2,1,0:T(8,128)(2,1)}, bf1...) custom-call(bf16[1024,2560]{1,0:T(8,128)(2,1)} %bitcast.54, bf16[2560,512]{1,0:T(8,128)(2,1)} %bitcast.52, ...), custom_call_target="tpu_custom_call" | custom-call | tf_op jit(solution)/shard_map/pallas_call | solution.py:1166
  604.3 2.1 convert_element_type.22
  606.4 0.0 copy-start.6
  606.4 108.6 %shard_map.192 = (f32[2,64,2560]{2,1,0:T(8,128)}, f32[8,640]{1,0:T(8,128)}, f32[4,8,512]{2,1,0:T(8,128)}, bf16[2,160,1280]{2,1,0:T(8,128)(2,1)}, bf16[160,1280]{...) custom-call(bf16[2560,512]{1,0:T(8,128)(2,1)} %bitcast.48, ...), custom_call_target="tpu_custom_call" | custom-call | tf_op jit(solution)/shard_map/pallas_call | solution.py:830
  715.0 0.0 copy-start.4
  715.0 1.4 reshape.226
  716.4 0.7 constant_dynamic-update-slice_fusion.4
  717.1 0.7 constant_dynamic-update-slice_fusion.3
  717.8 0.7 constant_dynamic-update-slice_fusion.2
  718.5 0.7 constant_dynamic-update-slice_fusion.1
  719.2 0.7 constant_dynamic-update-slice_fusion
  720.0 0.0 copy-start.7
  720.0 0.0 copy-done.6
  720.0 0.6 divide_multiply_fusion
  720.6 1.6 convert_element_type.24
  722.2 1.9 convert_bitcast_fusion.1
  724.1 2.4 convert_element_type.23
  726.5 0.0 copy-done.4
  726.5 0.0 copy-start.2
  726.5 1.6 convert_bitcast_fusion
  728.1 0.0 copy-done.7
  728.1 0.2 copy-done.2
  728.3 0.8 copy-done.3
  729.1 2.6 maximum_convert_fusion
  731.7 0.0 copy-done.1
  731.7 1.1 copy.26
  (5 shorter events, 0.0 us)
Async XLA Ops:
  361.6 173.6 %copy-start = (f32[2,64,2560]{2,1,0:T(8,128)S(1)}, f32[2,64,2560]{2,1,0:T(8,128)}, u32[]{:S(2)}) copy-start(f32[2,64,2560]{2,1,0:T(8,128)} %get-tuple-element.64.res) | copy-start | bytes 3932164
  535.1 2.4 copy-start.5
  606.4 113.6 %copy-start.6 = (f32[1280]{0:T(1024)S(1)}, f32[1280]{0:T(1024)}, u32[]{:S(2)}) copy-start(f32[1280]{0:T(1024)} %param.17) | copy-start | bytes 15364
  715.0 11.5 %copy-start.4 = (bf16[160,3840]{1,0:T(8,128)(2,1)S(1)}, bf16[160,3840]{1,0:T(8,128)(2,1)}, u32[]{:S(2)}) copy-start(bf16[160,3840]{1,0:T(8,128)(2,1)} %get-tuple-element.101) | copy-start | bytes 3686404
  720.0 8.2 %copy-start.7 = (f32[8,1280]{1,0:T(8,128)}, f32[8,1280]{1,0:T(8,128)S(1)}, u32[]{:S(2)}) copy-start(f32[8,1280]{1,0:T(8,128)S(1)} %constant_dynamic-update-slice_fusion) | copy-start | bytes 122884
  726.5 1.8 copy-start.2
  726.5 2.5 copy-start.3
  729.1 2.6 copy-start.1

commit v6 on v5

--- a/solution.py
+++ b/solution.py
@@ -512,6 +512,9 @@
     return src, into, (((c.fifth, 0),) if extra else ((None, 0),)), "from"
 
 
+START_ORDER = "azgagaw"
+
+
 def start_kernel(x, gain, wbr, wot, gates, full_a, wb0, wb1, wop, gb, own, zero, send, recv):
     c = Comm(send, recv)
     c.barrier()
@@ -532,24 +535,17 @@
     fills += [(zero.at[:, pl.ds(0, gates.shape[2])], gb.at[k, 1, :, g], c.slot()) for k in range(2) for g in range(c.ng)]
     idle = jnp.logical_not(c.fifth())
     pl.when(idle)(lambda: [c.local(*f).start() for f in fills] and None)
-    for f in z:
-        next(f)
     fwd, rev = c.bits, c.bits[::-1]
     g1 = []
     for h in range(2):
         for k, order in ((0, fwd), (1, rev)):
             g1.append(plane_gather(c, lambda g, k=k, h=h: wb[k].at[:, g, :, pl.ds(256 * h, 256)], order, None, c.fifth() if h else None))
             g1.append(plane_gather(c, lambda g, k=k, h=h: gb.at[k, h, :, g], order, None, c.fifth() if h else None))
-    for f in g1:
-        next(f)
     ag = ag_flow(c, own, full_a)
-    next(ag)
     z2 = [spread_z(c, *heads_to(c, wot, lambda t: wop.at[t], extra)) for extra in (False, True)]
-    for f in g1:
-        next(f)
-    next(ag)
-    for f in z2:
-        next(f)
+    does = {"z": lambda: step(*z), "g": lambda: step(*g1), "a": lambda: step(ag), "w": lambda: step(*z2)}
+    for what in START_ORDER:
+        does[what]()
     run(ag, *g1, *z, *z2)
     pl.when(idle)(lambda: [c.local(*f).wait() for f in fills] and None)
 
@@ -570,7 +566,7 @@
 
 
 MID_LATE = False
-MID_ORDER = "r0yarr0ary1arNz1aAz2A2"
+MID_ORDER = "ra0yrr0ary1raNza1z2A2A"
 
 
 def mid_kernel(mixed, wo, x, go, gain, p0, m1, m2, zero, res, full, full_g, w0, w1, w2, tot, own, part, pair, inbox, outbox, send, recv):
@@ -685,11 +681,11 @@
     ag = ag_flow(c, own, full)
     step(ag, rs2)
     step(rs2)
+    step(grad[2])
+    step(grad[2])
     finish(*red[0])
     s0 = spread_z(c, *units_back(lambda t: su.at[t // 2, 0, t % 2], o0))
     step(s0)
-    step(grad[2])
-    step(grad[2])
     onward(red[1])
     step(ag, rs2)
     held = []
@@ -744,21 +740,32 @@
     run(z)
 
 
-def end_kernel(wb0, wb1, gbr, x, gres, gain, na, gsrc, ggb, rwo, gain_b, chan_rows, gin, gains, table, owb, owo, ogb, gwb0, gwb1,
+def end_kernel(wb0, wb1, gbr, x, gres, gain, na, gsrc, gmo, mixed, ggb, gain_b, chan_rows, gin, gains, gchan, gdec, owb, owo, ogb, gwb0, gwb1, gwo,
                sm_a, in_a, z_a, sm_b, in_b, sbox, z_b, tot, part, pair, inbox, outbox, su_x, in_x, su_g, in_g, rbuf, lbuf, stage, send, recv):
     c = Comm(send, recv)
     c.barrier()
     fwd, rev = c.bits, c.bits[::-1]
-    red, spread = [], []
-    for h in range(2):
-        for k, gw in enumerate((gwb0, gwb1)):
-            i, order, cond = 2 * h + k, rev if k else fwd, c.fifth() if h else None
-            red.append(plane_reduce(c, lambda g, gw=gw, h=h: gw.at[:, g, :, pl.ds(256 * h, 256)], su_x.at[i], in_x.at[i], order, cond))
+    red, gate, every = [], [], []
+    for k, gw in enumerate((gwb0, gwb1, gwo)):
+        red.append(([], []))
+        for h in range(2):
+            i, cond = 2 * k + h, c.fifth() if h else None
             lane = (lambda t: pl.ds(1024, 256)) if h else (lambda t: pl.ds(pl.multiple_of(t * 256, 256), 256))
             which = ((c.fifth, 0),) if h else ((None, 0),)
-            spread.append((len(red) - 1, spread_z(c, lambda t, q, i=i: su_x.at[i, 0, t], lambda t, q, k=k, lane=lane: owb.at[k, :, lane(t)], which, "from")))
-            red.append(plane_reduce(c, lambda g, k=k, h=h: ggb.at[k, h, :, g], su_g.at[i], in_g.at[i], order, cond))
-            spread.append((len(red) - 1, spread_z(c, lambda t, q, i=i: su_g.at[i, 0, t], lambda t, q, k=k, h=h: ogb.at[k, 4 if h else t], which, "from")))
+            dst = (lambda t, q, k=k, lane=lane: owb.at[k, :, lane(t)]) if k < 2 else (lambda t, q, lane=lane: owo.at[:, lane(t)])
+            flows = []
+            for q, order in ((0, fwd), (1, rev)):
+                at = pl.ds(2 * q, 2)
+                flows.append(plane_reduce(c, lambda g, gw=gw, h=h, at=at: gw.at[at, g, :, pl.ds(256 * h, 256)], su_x.at[i, :, at], in_x.at[i, :, at], order, cond))
+                red[k][q].append(flows[q])
+            every.append((flows, spread_z(c, lambda t, q, i=i: su_x.at[i, 0, t], dst, which, "from")))
+            if k < 2:
+                gate.append(plane_reduce(c, lambda g, k=k, h=h: ggb.at[k, h, :, g], su_g.at[i], in_g.at[i], rev if k else fwd, cond))
+                every.append((gate[-1:], spread_z(c, lambda t, q, i=i: su_g.at[i, 0, t], lambda t, q, k=k, h=h: ogb.at[k, 4 if h else t], which, "from")))
+
+    def onward(*flows):
+        for _ in range(len(c.bits) - 1):
+            step(*flows)
 
     def make(rows):
         v = [jnp.concatenate([gbr[k, at, :] for at in rows], axis=0) for k in range(2)]
@@ -767,31 +774,29 @@
 
     rs = rs_flow(c, part, tot, pair, inbox, outbox, make)
     next(rs)
-    grad = [grad_flow(c, na, gsrc.at[k], gw, rbuf, lbuf, stage, ([], [red[2 * k], red[4 + 2 * k]])) for k, gw in enumerate((gwb0, gwb1))]
-    for k in range(4):
-        step(red[2 * k + 1])
+    grad = [grad_flow(c, lhs, rhs, gw, rbuf, lbuf, stage, red[k]) for k, (lhs, rhs, gw) in enumerate(((na, gsrc.at[0], gwb0), (na, gsrc.at[1], gwb1), (gmo, mixed, gwo)))]
+    step(*gate)
     sm_a[0] = chan_rows[...]
     chan = small_flow(c, sm_a, in_a, z_a)
     step(chan)
-    z0 = [spread_z(c, *heads_out(c, lambda t: rwo.at[t], owo, extra)) for extra in (False, True)]
+    step(rs)
+    step(grad[2])
+    step(grad[2])
     step(rs)
     step(grad[0])
     step(grad[0])
+    step(chan)
     step(rs)
     step(grad[1])
     step(grad[1])
-    for _ in c.bits:
+    onward(*red[2][0], *red[2][1], *red[0][0], *red[0][1])
+    for _ in c.bits[1:]:
         step(chan)
-    step(*z0)
     step(rs)
-    for _ in range(len(c.bits) - 1):
-        step(*red)
-    step(rs)
-    for i, f in enumerate(red):
-        finish(f)
-        for k, z in spread:
-            if k == i:
-                next(z)
+    onward(*red[1][0], *red[1][1], *gate)
+    for flows, z in every:
+        finish(*flows)
+        step(z)
     finish(rs)
     total = jnp.zeros_like(gain)
     for s in range(2):
@@ -811,13 +816,17 @@
     copy = c.to(sbox.at[0], sbox.at[1], c.at(m=1 - c.m), c.slot())
     copy.start()
     finish(chan)
-    table[...] = z_a[...]
+    fifth = z_a[1 + c.m]
+    for out, rows in ((gchan, slice(0, 7)), (gdec, slice(7, 8))):
+        for t in range(TP):
+            out[:, t * 256:(t + 1) * 256] = z_a[t, rows, :256]
+        out[:, 1024:] = fifth[rows, 256:]
     copy.wait()
     gains[...] = sbox[0] + sbox[1]
-    run(*grad, *z0, *[z for _, z in spread])
-
-
-def end_call(wb0, wb1, x, gres, gain, na, gsrc, ggb, rwo, gain_b, chan_rows, r):
+    run(*grad, *[z for _, z in every])
+
+
+def end_call(wb0, wb1, x, gres, gain, na, gsrc, gmo, mixed, ggb, gain_b, chan_rows, r):
     _, n, d = x.shape
     ng = lax.axis_size("dp") // TP
     gr, steps = ggb.shape[4], (lax.axis_size("dp") // TP).bit_length()
@@ -827,18 +836,18 @@
     def sets(k, rows, width):
         return [pltpu.VMEM((k, ng // 2, TP, rows, width), BF), pltpu.VMEM((k, ng - 1, TP, rows, width), BF)]
 
-    *outs, _, _ = call(
+    *outs, _, _, _ = call(
         end_kernel,
-        (S((2, n, d), F32), S((8, d // 4), F32), S((TP, 8, 512), F32), S((2, r, 1280), BF), S((r, 1280), BF), S((2, 5, gr, 256), BF))
-        + (S((TP, ng, r, 512), BF),) * 2,
-        [VM] * 6 + [HBM] * 4 + [VM] * 2,
-        (VM,) * 3 + (HBM,) * 5,
+        (S((2, n, d), F32), S((8, d // 4), F32), S((7, 1280), F32), S((1, 1280), F32), S((2, r, 1280), BF), S((r, 1280), BF), S((2, 5, gr, 256), BF))
+        + (S((TP, ng, r, 512), BF),) * 3,
+        [VM] * 6 + [HBM] * 4 + [HBM] + [VM] * 2,
+        (VM,) * 4 + (HBM,) * 6,
         [V((steps, 8, 512), F32), V((steps - 1, 8, 512), F32), V((TP, 8, 512), F32),
          V((steps, 8, d // 4), F32), V((steps - 1, 8, d // 4), F32), V((2, 8, d // 4), F32), V((TP, 8, d // 4), F32),
-         pltpu.VMEM((2, n, d), F32), pltpu.VMEM((2, TP, 2, n, d), BF)] + rs_scratch(n, d, True) + sets(4, r, 256) + sets(4, gr, 256)
+         pltpu.VMEM((2, n, d), F32), pltpu.VMEM((2, TP, 2, n, d), BF)] + rs_scratch(n, d, True) + sets(6, r, 256) + sets(4, gr, 256)
         + [pltpu.VMEM((na.shape[0], 512), BF), pltpu.VMEM((2, na.shape[0], ng * r), BF), pltpu.VMEM((2, ng, r, 512), BF)],
         4, 256,
-    )(wb0, wb1, gsrc, x, gres, gain[None], na, gsrc, ggb, rwo, gain_b, chan_rows)
+    )(wb0, wb1, gsrc, x, gres, gain[None], na, gsrc, gmo, mixed, ggb, gain_b, chan_rows)
     return outs
 
 
@@ -1044,22 +1053,13 @@
     )(na, wb0, wb1, gb, chan, db[None], wop, m0, jnp.zeros((TP, r, big - small), BF), jnp.zeros((TP, r, 256), BF))
 
 
-def mix_bwd_kernel(gmo, wo, br0, ci, gb, chan, db, conv, gates, state, rim, carry, table, gwo, r1, r2, gbr, ggb, sums, rwo, o1, o2,
-                   gm, a_ref, adj, gc, gpl, ext, heads, etab, rim_in, su, ib, send, recv):
+def mix_bwd_kernel(gmo, wo, br0, ci, gb, chan, db, conv, gates, state, rim, carry, table, r1, r2, gbr, ggb, sums, o1, o2,
+                   gm, a_ref, adj, gc, gpl, ext, heads, etab, rim_in, send, recv):
     c = Comm(send, recv)
     greet(plane_partners(c) + line_partners(c))
     n, width = ci.shape[1], ci.shape[2]
     zs = [spread_z(c, *units_back(lambda t, rr=rr: rr.at[t], oo)) for rr, oo in ((r1, o1), (r2, o2))]
     step(*zs)
-    fwd, rev = c.bits, c.bits[::-1]
-    red = []
-    for h in range(2):
-        for q, order in ((0, fwd), (1, rev)):
-            i = 2 * h + q
-            red.append(plane_reduce(c, lambda g, h=h, q=q: gwo.at[pl.ds(2 * q, 2), g, :, pl.ds(256 * h, 256)], su.at[i], ib.at[i], order, c.fifth() if h else None))
-    for f in red:
-        next(f)
-
     def product(i, _):
         rows = pl.ds(pl.multiple_of(i * 2 * n, 2 * n), 2 * n)
         gm[rows, :] = jnp.dot(gmo[rows, :], wo[...], preferred_element_type=F32)
@@ -1083,9 +1083,6 @@
     etab[c.g] = e
     sh = share(c, etab)
     next(sh)
-    for f in red:
-        for _ in range(len(c.bits) - 1):
-            next(f)
     finish(sh)
     ein = entering(c, lambda g: table[g, 0], lambda g: etab[g], width, True)
 
@@ -1146,17 +1143,10 @@
         for k in range(1, 4):
             v = v + chan[k:k + 1] * gc[b, pl.ds(k, n), :]
         gbr[1, rows, :] = v.astype(BF)
-    held = []
-    for i, f in enumerate(red):
-        finish(f)
-        held.append(c.local(su.at[i, 0], rwo.at[pl.ds(2 * (i % 2), 2), :, pl.ds(256 * (i // 2), 256)], c.slot()))
-        only(c.fifth() if i >= 2 else None, lambda: held[-1].start())
     run(*zs)
-    for i, h in enumerate(held):
-        only(c.fifth() if i >= 2 else None, lambda: h.wait())
-
-
-def mix_bwd_call(gmo, wo, br0, ci, gb, chan, db, saved, gwo, r1, r2, units):
+
+
+def mix_bwd_call(gmo, wo, br0, ci, gb, chan, db, saved, r1, r2, units):
     ng = lax.axis_size("dp") // TP
     rows, width = br0.shape
     n = rows // (2 * TP)
@@ -1165,14 +1155,13 @@
     V = pltpu.VMEM
     return call(
         mix_bwd_kernel,
-        (S((2, rows, width), BF), S((2, 2, 256, 256), F32), S((8, width), F32), S((TP, r, width), BF), S((r, units), BF), S((r, units), BF)),
-        [VM] * 13 + [HBM] * 3,
-        (VM,) * 3 + (HBM,) * 3,
+        (S((2, rows, width), BF), S((2, 2, 256, 256), F32), S((8, width), F32), S((r, units), BF), S((r, units), BF)),
+        [VM] * 13 + [HBM] * 2,
+        (VM,) * 3 + (HBM,) * 2,
         [V((rows, width), F32), V((width // 128, rows, 128), F32), V((width // 128, rows, 128), F32), V((2 * TP, n + 8, width), F32), V((2, rows, width), BF),
-         V((2, n + 8, width), F32), V((2 * TP, 8, width), F32), V((ng, 2 * TP, width), F32), V((2 * TP, 8, width), F32),
-         V((4, ng // 2, 2, r, 256), BF), V((4, ng - 1, 2, r, 256), BF)],
+         V((2, n + 8, width), F32), V((2 * TP, 8, width), F32), V((ng, 2 * TP, width), F32), V((2 * TP, 8, width), F32)],
         6, 128,
-    )(gmo, wo, br0, ci, gb, chan, db[None], *saved, gwo, r1, r2)
+    )(gmo, wo, br0, ci, gb, chan, db[None], *saved, r1, r2)
 
 
 def mlp_kernel(nb, go, w0, w1, w2, hidden, gg0, gg1, part, gnb, v0, v1, v2, sems):
@@ -1254,16 +1243,13 @@
     gres, gain_b, mlp_own, gmo, o0, r1, r2 = back_call(gnb, mlp_part, residual, grad_own, norm_gains[1], nb, go, gg0, gg1, hidden, ng, r, units)
     out = jnp.where(valid, residual + mlp_own, 0.0).astype(BF)
     gmo = gmo.reshape(-1, width)
-    block = (TP, ng, r, 512)
-    gwo = dot(gmo, mixed, 0, 0).astype(BF).reshape(block)
-    gbr, ggb, chan_rows, rwo, o1, o2 = mix_bwd_call(gmo, wo, branch0, conv_input, gb, chan, decay_base, saved, gwo, r1, r2, units)
-    gin, gains, table, owb, owo, ogb = end_call(
-        wb0, wb1, x, gres, norm_gains[0], na, gbr, ggb.astype(BF).reshape(2, 2, TP, ng, gr, 256), rwo, gain_b, chan_rows, r,
+    gbr, ggb, chan_rows, o1, o2 = mix_bwd_call(gmo, wo, branch0, conv_input, gb, chan, decay_base, saved, r1, r2, units)
+    gin, gains, gchan, gdec, owb, owo, ogb = end_call(
+        wb0, wb1, x, gres, norm_gains[0], na, gbr, gmo, mixed, ggb.astype(BF).reshape(2, 2, TP, ng, gr, 256), gain_b, chan_rows, r,
     )
     g_wb, g_wo, g_gb = owb.astype(F32), owo.astype(F32).T, ogb.astype(F32)
     g_wm, g_wd = jnp.stack([o0, o1]).astype(F32), o2.astype(F32).T
-    crow = jnp.concatenate([table[i, :, :256] for i in range(TP)] + [jnp.where(mp == 0, table[1, :, 256:], table[2, :, 256:])], -1)
-    return out, gin, gains.reshape(2, width), g_wb, crow[:7], g_gb, crow[7] * jax.nn.sigmoid(decay_param), g_wo, g_wm, g_wd
+    return out, gin, gains.reshape(2, width), g_wb, gchan, g_gb, gdec[0] * jax.nn.sigmoid(decay_param), g_wo, g_wm, g_wd
 
 
 def solution(mesh):

time: 737 us -> 708 us (0.961)
  Pallas kernels: 691 us -> 671 us
    pallas_call x1, Pallas kernels: 174 us -> 160 us  [back_call(): call(back_kernel, (S((2, n, d), F32), S((1, d), F32), S((2, n, d), F32),...]
    pallas_call x1, Pallas kernels: 109 us -> 100 us  [end_call(): call(end_kernel, (S((2, n, d), F32), S((8, d // 4), F32), S((7, 1280), F3...]
where the time goes in v6:
time: 708 us; the launch traced here: 705 us
  Pallas kernels  671 us (95%)
  other arithmetic  20.6 us (3%)
  local copies, waits for them, and re-layouts  11.5 us (2%)
    pallas_call x1, Pallas kernels, mid_call(): call(mid_kernel, (S((2, n, d), F32), S((2, TP, 2, n, d), BF), S((2, TP, 2...  186 us
    pallas_call x1, Pallas kernels, back_call(): call(back_kernel, (S((2, n, d), F32), S((1, d), F32), S((2, n, d), F32),...  160 us
    pallas_call x1, Pallas kernels, end_call(): call(end_kernel, (S((2, n, d), F32), S((8, d // 4), F32), S((7, 1280), F3...  100 us
    pallas_call x1, Pallas kernels, start_call(): call(start_kernel, (S((2, TP, 2, n, d), BF), S((TP, ng, r, 512), BF), S((...  74.3 us
    pallas_call x1, Pallas kernels, mix_bwd_call(): call(mix_bwd_kernel, (S((2, rows, width), BF), S((2, 2, 256, 256), F32),...  67 us
    pallas_call x1, Pallas kernels, mlp_call(): pl.pallas_call(mlp_kernel, grid=(rows // n,), out_shape=(S((rows, fs), BF...  42.6 us
    pallas_call x1, Pallas kernels, mix_fwd_call(): call(mix_fwd_kernel, (S((rows, width), BF), S((rows, width), BF), S((2, r...  40.3 us

profile of v6, /device:TPU:0, one launch (start us, length us, event | category | flops | bytes accessed | tf_op | source)
XLA Modules:
  0.0 704.5 jit_solution(11017164826595275947)
XLA Ops:
  0.7 0.7 broadcast_compare_fusion
  1.4 0.8 dynamic-slice.3
  2.2 0.7 broadcast_in_dim.40
  2.9 0.6 compare_select_fusion.db
  3.5 0.7 constant_dynamic-slice_fusion
  4.2 0.6 pad_maximum_fusion.chan
  4.8 1.4 fusion
  6.2 2.0 broadcast_select_fusion.go
  8.3 3.2 slice_bitcast_fusion
  11.5 74.3 %shard_map.186 = (bf16[2,4,2,64,2560]{4,3,2,1,0:T(8,128)(2,1)}, bf16[4,4,160,512]{3,2,1,0:T(8,128)(2,1)}, bf16[4,4,160,512]{3,2,1,0:T(8,128)(2,1)}, bf16[4,160,5...) custom-call(bf16[2,64,2560]{2,1,0:T(8,128)(2,1)} %x.5, f32[1,2560]{1,0:T(1,128)} %get-tuple-element.107.gain, ...), custom_call_target="tpu_custom_call" | custom-call | tf_op jit(solution)/shard_map/pallas_call | solution.py:558
  85.9 0.7 broadcast_3_zero.2.zero
  86.6 0.7 broadcast_in_dim.42.blank
  87.3 40.3 %shard_map.187 = (bf16[1024,512]{1,0:T(8,128)(2,1)}, bf16[1024,512]{1,0:T(8,128)(2,1)}, f32[2,1024,512]{2,1,0:T(8,128)}, f32[1024,512]{1,0:T(8,128)}, f32[8,8,51...) custom-call(bf16[1024,2560]{1,0:T(8,128)(2,1)} %bitcast.27, ...), custom_call_target="tpu_custom_call" | custom-call | tf_op jit(solution)/shard_map/pallas_call | solution.py:1045
  127.7 186.3 %shard_map.188 = (f32[2,64,2560]{2,1,0:T(8,128)}, bf16[2,4,2,64,2560]{4,3,2,1,0:T(8,128)(2,1)}, bf16[2,4,2,64,2560]{4,3,2,1,0:T(8,128)(2,1)}, bf16[4,4,160,1024]...) custom-call(bf16[1024,512]{1,0:T(8,128)(2,1)} %get-tuple-element.61.mixed, ...), custom_call_target="tpu_custom_call" | custom-call | tf_op jit(solution)/shard_map/pallas_call | solution.py:631
  314.0 42.6 %shard_map.189 = (bf16[1024,1024]{1,0:T(8,128)(2,1)}, bf16[1024,1024]{1,0:T(8,128)(2,1)}, bf16[1024,1024]{1,0:T(8,128)(2,1)}, bf16[1024,2560]{1,0:T(8,128)(2,1)}, bf16[1024,2560]{1,0:T(8,128)(2,1)}) custom-call(bf16[1024,2560]{1,0:T(8,128)(2,1)} %bitcast.31, bf16[1024,2560]{1,0:T(8,128)(2,1)} %bitcast.33, bf16[2560,1024]{1,0:T(8,128)(2,1)} %bitcast.43, ...), custom_call_target="tpu_custom_call" | custom-call | tf_op jit(solution)/shard_map/pallas_call | solution.py:1205
  356.6 0.0 copy-start
  356.6 160.2 %shard_map.190 = (f32[2,64,2560]{2,1,0:T(8,128)}, f32[1,2560]{1,0:T(1,128)}, f32[2,64,2560]{2,1,0:T(8,128)}, bf16[2,4,2,64,2560]{4,3,2,1,0:T(8,128)(2,1)}, bf16[...) custom-call(bf16[2,4,2,64,2560]{4,3,2,1,0:T(8,128)(2,1)} %bitcast.42, ...), custom_call_target="tpu_custom_call" | custom-call | tf_op jit(solution)/shard_map/pallas_call | solution.py:716
  516.9 0.0 copy-done
  516.9 2.3 select_convert_fusion
  519.2 67.0 %shard_map.191 = (bf16[2,1024,512]{2,1,0:T(8,128)(2,1)}, f32[2,2,256,256]{3,2,1,0:T(8,128)}, f32[8,512]{1,0:T(8,128)}, bf16[160,3840]{1,0:T(8,128)(2,1)}, bf16[160,3840]{1,0:T(8,128)(2,1)}) custom-call(bf16[1024,2560]{1,0:T(8,128)(2,1)} %bitcast.29, bf16[2560,512]{1,0:T(8,128)(2,1)} %bitcast.40, f32[1024,512]{1,0:T(8,128)} %get-tuple-element.77.br0, ...), custom_call_target="tpu_custom_call" | custom-call | tf_op jit(solution)/shard_map/pallas_call | solution.py:1156
  586.2 2.1 convert_element_type.18
  588.3 0.0 copy-start.6
  588.3 100.2 %shard_map.192 = (f32[2,64,2560]{2,1,0:T(8,128)}, f32[8,640]{1,0:T(8,128)}, f32[7,1280]{1,0:T(8,128)}, f32[1,1280]{1,0:T(1,128)}, bf16[2,160,1280]{2,1,0:T(8,128...) custom-call(bf16[2560,512]{1,0:T(8,128)(2,1)} %bitcast.36, ...), custom_call_target="tpu_custom_call" | custom-call | tf_op jit(solution)/shard_map/pallas_call | solution.py:839
  688.6 0.0 copy-start.4
  688.6 0.8 reduce
  689.4 0.0 copy-done.6
  689.4 0.6 divide_multiply_fusion
  690.0 1.3 reshape.220
  691.3 1.6 convert_element_type.20
  692.9 1.9 convert_bitcast_fusion.1
  694.9 2.4 convert_element_type.19
  697.3 0.0 copy-done.4
  697.3 0.0 copy-start.2
  697.3 0.0 copy-start.3
  697.3 1.6 convert_bitcast_fusion
  698.9 0.2 copy-done.2
  699.0 0.8 copy-done.3
  699.8 0.0 copy-start.1
  699.8 2.6 maximum_convert_fusion
  702.4 0.0 copy-done.1
  702.4 0.0 copy-start.5
  702.4 1.1 copy.23
  703.5 0.0 copy-done.5
  703.5 0.6 copy.24
  (2 shorter events, 0.0 us)
Async XLA Ops:
  356.6 160.3 %copy-start = (f32[2,64,2560]{2,1,0:T(8,128)S(1)}, f32[2,64,2560]{2,1,0:T(8,128)}, u32[]{:S(2)}) copy-start(f32[2,64,2560]{2,1,0:T(8,128)} %get-tuple-element.64.res) | copy-start | bytes 3932164
  588.3 101.1 %copy-start.6 = (f32[1280]{0:T(1024)S(1)}, f32[1280]{0:T(1024)}, u32[]{:S(2)}) copy-start(f32[1280]{0:T(1024)} %param.17) | copy-start | bytes 15364
  688.6 8.7 %copy-start.4 = (bf16[160,3840]{1,0:T(8,128)(2,1)S(1)}, bf16[160,3840]{1,0:T(8,128)(2,1)}, u32[]{:S(2)}) copy-start(bf16[160,3840]{1,0:T(8,128)(2,1)} %get-tuple-element.101) | copy-start | bytes 3686404
  697.3 1.8 copy-start.2
  697.3 2.5 copy-start.3
  699.8 2.6 copy-start.1
  702.4 1.1 copy-start.5

commit v7 on v6

--- a/solution.py
+++ b/solution.py
@@ -851,14 +851,6 @@
     return outs
 
 
-def heads_of(a, axis):
-    _, _, t, _ = plan()
-    p = lax.dynamic_slice_in_dim(a, t * 256, 256, axis)
-    q = lax.dynamic_slice_in_dim(a, 1024, 256, axis)
-    q = jnp.where(t == 1 + lax.axis_index("mp"), q, jnp.zeros_like(q))
-    return jnp.concatenate([p, q], axis)
-
-
 def gelu_pair(v):
     k = 0.7978845608028654
     v2 = v * v
@@ -934,7 +926,7 @@
     return jnp.concatenate(rows, axis=0)
 
 
-def mix_fwd_kernel(na, wb0, wb1, gb, chan, db, wop, m0, zero, blank, mixed, conv, gates, state, rim, carry, table, br0, ci, wo, p0, a_ref, d_ref, ext, rim_in, send, recv):
+def mix_fwd_kernel(na, wb0, wb1, gb, chan_all, db_all, wop, m0, zero, blank, mixed, conv, gates, state, rim, carry, table, br0, ci, chan, db, wo, p0, a_ref, d_ref, ext, rim_in, send, recv):
     c = Comm(send, recv)
     greet(plane_partners(c) + line_partners(c))
     n, width = ci.shape[1], ci.shape[2]
@@ -953,6 +945,11 @@
     pad = zero.shape[2]
     fill = c.local(zero, p0.at[:, :, pl.ds(p0.shape[2] - pad, pad)], c.slot())
     pl.when(outer(c.t))(lambda: fill.start())
+
+    for own, whole, empty in ((chan, chan_all, 0.0), (db, db_all, 1.0)):
+        last = whole[:, 1024:]
+        own[:, :256] = whole[:, pl.ds(pl.multiple_of(c.t * 256, 256), 256)]
+        own[:, 256:] = jnp.where(c.fifth(), last, jnp.full_like(last, empty))
 
     def branch(i, _):
         rows = pl.ds(pl.multiple_of(i * 2 * n, 2 * n), 2 * n)
@@ -1045,9 +1042,9 @@
     return call(
         mix_fwd_kernel,
         (S((rows, width), BF), S((rows, width), BF), S((2, rows, width), F32), S((rows, width), F32),
-         S((2 * TP, 8, width), F32), S((2 * TP, width), F32), S((ng, 2, 2 * TP, width), F32), S((rows, width), F32), S((2 * TP, n, width), BF), S((TP, ng, r, width), BF), S((TP, r, big), BF)),
+         S((2 * TP, 8, width), F32), S((2 * TP, width), F32), S((ng, 2, 2 * TP, width), F32), S((rows, width), F32), S((2 * TP, n, width), BF), S((7, width), F32), S((1, width), F32), S((TP, ng, r, width), BF), S((TP, r, big), BF)),
         [VM] * 6 + [HBM, HBM, VM, VM],
-        (VM,) * 9 + (HBM, HBM),
+        (VM,) * 11 + (HBM, HBM),
         [pltpu.VMEM((width // 128, rows, 128), F32), pltpu.VMEM((width // 128, rows, 128), F32), pltpu.VMEM((2, n + 8, width), F32), pltpu.VMEM((2 * TP, 16, width), BF)],
         5, 128,
     )(na, wb0, wb1, gb, chan, db[None], wop, m0, jnp.zeros((TP, r, big - small), BF), jnp.zeros((TP, r, 256), BF))
@@ -1132,7 +1129,7 @@
     sums[...] = jnp.concatenate(total, axis=0)
     for k in range(2):
         for h in range(2):
-            ggb[k, h] = lax.dot_general(conv[:, h * 256:(h + 1) * 256], gpl[k, :, h * 256:(h + 1) * 256], (((0,), (0,)), ((), ())), preferred_element_type=F32)
+            ggb[k, h] = lax.dot_general(conv[:, h * 256:(h + 1) * 256], gpl[k, :, h * 256:(h + 1) * 256], (((0,), (0,)), ((), ())), preferred_element_type=F32).astype(BF)
     out.wait()
     for b in range(2 * TP):
         rows = pl.ds(b * n, n)
@@ -1155,13 +1152,13 @@
     V = pltpu.VMEM
     return call(
         mix_bwd_kernel,
-        (S((2, rows, width), BF), S((2, 2, 256, 256), F32), S((8, width), F32), S((r, units), BF), S((r, units), BF)),
+        (S((2, rows, width), BF), S((2, 2, 256, 256), BF), S((8, width), F32), S((r, units), BF), S((r, units), BF)),
         [VM] * 13 + [HBM] * 2,
         (VM,) * 3 + (HBM,) * 2,
         [V((rows, width), F32), V((width // 128, rows, 128), F32), V((width // 128, rows, 128), F32), V((2 * TP, n + 8, width), F32), V((2, rows, width), BF),
          V((2, n + 8, width), F32), V((2 * TP, 8, width), F32), V((ng, 2 * TP, width), F32), V((2 * TP, 8, width), F32)],
         6, 128,
-    )(gmo, wo, br0, ci, gb, chan, db[None], *saved, r1, r2)
+    )(gmo, wo, br0, ci, gb, chan, db, *saved, r1, r2)
 
 
 def mlp_kernel(nb, go, w0, w1, w2, hidden, gg0, gg1, part, gnb, v0, v1, v2, sems):
@@ -1223,9 +1220,7 @@
     rows, width = block_input.shape[1:]
     r, gr, units = w_branch.shape[1], gate_blocks.shape[2], w_mlp.shape[2]
     fs = cut(units, 0)[1]
-    chan = heads_of(channel_params, 1)
-    dpar = heads_of(decay_param[None], 1)[0]
-    decay_base = jax.nn.softplus(dpar)
+    decay_base = jax.nn.softplus(decay_param)
     pos = dp * 2 * rows + mp * rows + jnp.arange(rows, dtype=jnp.int32)
     valid = (pos[None] < lengths[:, None])[..., None]
     x = block_input
@@ -1234,7 +1229,7 @@
     na = na.reshape(-1, width)
     wb0, wb1 = wb0.reshape(width, 512), wb1.reshape(width, 512)
     gb = gb.reshape(2, 2, 256, 256)
-    mixed, *saved, branch0, conv_input, wo, p0 = mix_fwd_call(na, wb0, wb1, gb, chan, decay_base, wop, w_mlp[0])
+    mixed, *saved, branch0, conv_input, chan, db, wo, p0 = mix_fwd_call(na, wb0, wb1, gb, channel_params, decay_base, wop, w_mlp[0])
     wo = wo.reshape(width, 512)
     residual, nb, go, w0, w1, wd = mid_call(mixed, wo, x, grad_own, norm_gains[1], p0, w_mlp[1], w_down.T)
     nb, go = nb.reshape(-1, width), go.reshape(-1, width)
@@ -1243,9 +1238,9 @@
     gres, gain_b, mlp_own, gmo, o0, r1, r2 = back_call(gnb, mlp_part, residual, grad_own, norm_gains[1], nb, go, gg0, gg1, hidden, ng, r, units)
     out = jnp.where(valid, residual + mlp_own, 0.0).astype(BF)
     gmo = gmo.reshape(-1, width)
-    gbr, ggb, chan_rows, o1, o2 = mix_bwd_call(gmo, wo, branch0, conv_input, gb, chan, decay_base, saved, r1, r2, units)
+    gbr, ggb, chan_rows, o1, o2 = mix_bwd_call(gmo, wo, branch0, conv_input, gb, chan, db, saved, r1, r2, units)
     gin, gains, gchan, gdec, owb, owo, ogb = end_call(
-        wb0, wb1, x, gres, norm_gains[0], na, gbr, gmo, mixed, ggb.astype(BF).reshape(2, 2, TP, ng, gr, 256), gain_b, chan_rows, r,
+        wb0, wb1, x, gres, norm_gains[0], na, gbr, gmo, mixed, ggb.reshape(2, 2, TP, ng, gr, 256), gain_b, chan_rows, r,
     )
     g_wb, g_wo, g_gb = owb.astype(F32), owo.astype(F32).T, ogb.astype(F32)
     g_wm, g_wd = jnp.stack([o0, o1]).astype(F32), o2.astype(F32).T

time: 708 us -> 704 us (level)
  no operation moved by 1% of the time
where the time goes in v7:
time: 704 us; the launch traced here: 700 us
  Pallas kernels  671 us (95%)
  other arithmetic  17.3 us (2%)
  local copies, waits for them, and re-layouts  10.7 us (2%)
    pallas_call x1, Pallas kernels, mid_call(): call(mid_kernel, (S((2, n, d), F32), S((2, TP, 2, n, d), BF), S((2, TP, 2...  186 us
    pallas_call x1, Pallas kernels, back_call(): call(back_kernel, (S((2, n, d), F32), S((1, d), F32), S((2, n, d), F32),...  160 us
    pallas_call x1, Pallas kernels, end_call(): call(end_kernel, (S((2, n, d), F32), S((8, d // 4), F32), S((7, 1280), F3...  100 us
    pallas_call x1, Pallas kernels, start_call(): call(start_kernel, (S((2, TP, 2, n, d), BF), S((TP, ng, r, 512), BF), S((...  74.3 us
    pallas_call x1, Pallas kernels, mix_bwd_call(): call(mix_bwd_kernel, (S((2, rows, width), BF), S((2, 2, 256, 256), BF), S...  66.9 us
    pallas_call x1, Pallas kernels, mlp_call(): pl.pallas_call(mlp_kernel, grid=(rows // n,), out_shape=(S((rows, fs), BF...  42.6 us
    pallas_call x1, Pallas kernels, mix_fwd_call(): call(mix_fwd_kernel, (S((rows, width), BF), S((rows, width), BF), S((2, r...  40.4 us

profile of v7, /device:TPU:0, one launch (start us, length us, event | category | flops | bytes accessed | tf_op | source)
XLA Modules:
  0.0 700.2 jit_solution(15523469364335824456)
XLA Ops:
  0.7 0.7 broadcast_compare_fusion
  1.4 0.7 compare_select_fusion
  2.1 0.6 broadcast_in_dim.31.db_all
  2.7 1.4 fusion
  4.1 2.0 broadcast_select_fusion.go
  6.2 3.2 slice_bitcast_fusion
  9.4 74.3 %shard_map.186 = (bf16[2,4,2,64,2560]{4,3,2,1,0:T(8,128)(2,1)}, bf16[4,4,160,512]{3,2,1,0:T(8,128)(2,1)}, bf16[4,4,160,512]{3,2,1,0:T(8,128)(2,1)}, bf16[4,160,5...) custom-call(bf16[2,64,2560]{2,1,0:T(8,128)(2,1)} %x.5, f32[1,2560]{1,0:T(1,128)} %get-tuple-element.109.gain, ...), custom_call_target="tpu_custom_call" | custom-call | tf_op jit(solution)/shard_map/pallas_call | solution.py:558
  83.8 0.7 broadcast_3_zero.2.zero
  84.5 0.7 broadcast_in_dim.32.blank
  85.2 40.4 %shard_map.187 = (bf16[1024,512]{1,0:T(8,128)(2,1)}, bf16[1024,512]{1,0:T(8,128)(2,1)}, f32[2,1024,512]{2,1,0:T(8,128)}, f32[1024,512]{1,0:T(8,128)}, f32[8,8,51...) custom-call(bf16[1024,2560]{1,0:T(8,128)(2,1)} %bitcast.26, ...), custom_call_target="tpu_custom_call" | custom-call | tf_op jit(solution)/shard_map/pallas_call | solution.py:1042
  125.6 186.3 %shard_map.188 = (f32[2,64,2560]{2,1,0:T(8,128)}, bf16[2,4,2,64,2560]{4,3,2,1,0:T(8,128)(2,1)}, bf16[2,4,2,64,2560]{4,3,2,1,0:T(8,128)(2,1)}, bf16[4,4,160,1024]...) custom-call(bf16[1024,512]{1,0:T(8,128)(2,1)} %get-tuple-element.63.mixed, ...), custom_call_target="tpu_custom_call" | custom-call | tf_op jit(solution)/shard_map/pallas_call | solution.py:631
  311.9 42.6 %shard_map.189 = (bf16[1024,1024]{1,0:T(8,128)(2,1)}, bf16[1024,1024]{1,0:T(8,128)(2,1)}, bf16[1024,1024]{1,0:T(8,128)(2,1)}, bf16[1024,2560]{1,0:T(8,128)(2,1)}, bf16[1024,2560]{1,0:T(8,128)(2,1)}) custom-call(bf16[1024,2560]{1,0:T(8,128)(2,1)} %bitcast.30, bf16[1024,2560]{1,0:T(8,128)(2,1)} %bitcast.32, bf16[2560,1024]{1,0:T(8,128)(2,1)} %bitcast.42, ...), custom_call_target="tpu_custom_call" | custom-call | tf_op jit(solution)/shard_map/pallas_call | solution.py:1202
  354.5 0.0 copy-start
  354.5 160.3 %shard_map.190 = (f32[2,64,2560]{2,1,0:T(8,128)}, f32[1,2560]{1,0:T(1,128)}, f32[2,64,2560]{2,1,0:T(8,128)}, bf16[2,4,2,64,2560]{4,3,2,1,0:T(8,128)(2,1)}, bf16[...) custom-call(bf16[2,4,2,64,2560]{4,3,2,1,0:T(8,128)(2,1)} %bitcast.41, ...), custom_call_target="tpu_custom_call" | custom-call | tf_op jit(solution)/shard_map/pallas_call | solution.py:716
  514.8 0.0 copy-done
  514.8 2.3 select_convert_fusion
  517.1 66.9 %shard_map.191 = (bf16[2,1024,512]{2,1,0:T(8,128)(2,1)}, bf16[2,2,256,256]{3,2,1,0:T(8,128)(2,1)}, f32[8,512]{1,0:T(8,128)}, bf16[160,3840]{1,0:T(8,128)(2,1)}, bf16[160,3840]{1,0:T(8,128)(2,1)}) custom-call(bf16[1024,2560]{1,0:T(8,128)(2,1)} %bitcast.28, bf16[2560,512]{1,0:T(8,128)(2,1)} %bitcast.39, f32[1024,512]{1,0:T(8,128)} %get-tuple-element.79.br0, ...), custom_call_target="tpu_custom_call" | custom-call | tf_op jit(solution)/shard_map/pallas_call | solution.py:1153
  584.0 0.0 copy-start.6
  584.0 100.2 %shard_map.192 = (f32[2,64,2560]{2,1,0:T(8,128)}, f32[8,640]{1,0:T(8,128)}, f32[7,1280]{1,0:T(8,128)}, f32[1,1280]{1,0:T(1,128)}, bf16[2,160,1280]{2,1,0:T(8,128...) custom-call(bf16[2560,512]{1,0:T(8,128)(2,1)} %bitcast.35, ...), custom_call_target="tpu_custom_call" | custom-call | tf_op jit(solution)/shard_map/pallas_call | solution.py:839
  684.3 0.0 copy-start.4
  684.3 0.8 reduce
  685.1 0.0 copy-done.6
  685.1 0.6 divide_multiply_fusion
  685.7 1.3 reshape.111
  687.1 1.6 convert_element_type.16
  688.6 1.9 convert_bitcast_fusion.1
  690.6 2.4 convert_element_type.15
  693.0 0.0 copy-done.4
  693.0 0.0 copy-start.2
  693.0 0.0 copy-start.3
  693.0 1.6 convert_bitcast_fusion
  694.6 0.2 copy-done.2
  694.8 0.8 copy-done.3
  695.6 0.0 copy-start.1
  695.6 2.6 maximum_convert_fusion
  698.1 0.0 copy-done.1
  698.1 0.0 copy-start.5
  698.1 1.1 copy.23
  699.2 0.0 copy-done.5
  699.2 0.6 copy.24
  (1 shorter events, 0.0 us)
Async XLA Ops:
  354.5 160.3 %copy-start = (f32[2,64,2560]{2,1,0:T(8,128)S(1)}, f32[2,64,2560]{2,1,0:T(8,128)}, u32[]{:S(2)}) copy-start(f32[2,64,2560]{2,1,0:T(8,128)} %get-tuple-element.66.res) | copy-start | bytes 3932164
  584.0 101.1 %copy-start.6 = (f32[1280]{0:T(1024)S(1)}, f32[1280]{0:T(1024)}, u32[]{:S(2)}) copy-start(f32[1280]{0:T(1024)} %param.17) | copy-start | bytes 15364
  684.3 8.7 %copy-start.4 = (bf16[160,3840]{1,0:T(8,128)(2,1)S(1)}, bf16[160,3840]{1,0:T(8,128)(2,1)}, u32[]{:S(2)}) copy-start(bf16[160,3840]{1,0:T(8,128)(2,1)} %get-tuple-element.105) | copy-start | bytes 3686404
  693.0 1.8 copy-start.2
  693.0 2.5 copy-start.3
  695.6 2.6 copy-start.1
  698.1 1.1 copy-start.5
